TPU v7x, 32 devices: a whole 2x2x4 slice. The times are simulated.
32 devices in a mesh: node: 8 (over y, x, core), local: 4 (over z).
Axes of the slice: x: 2, y: 2, z: 4, core: 2. Of those that a mesh axis runs over, the one named last changes fastest.
Arguments:
- tokens: bfloat16 [512, 4096], P('local', 'node'), may hold values from -6 to 6
- cotangent: bfloat16 [512, 4096], P('local', 'node'), may hold values from -0.25 to 0.25
- gain: bfloat16 [1, 4096], P(None, 'node'), may hold values from 0.099609375 to 1.8984375
- up_q: bfloat16 [4096, 14336], P('local', 'node'), may hold values from -4 to 4
- up_scale: bfloat16 [32, 14336], P('local', 'node'), may hold values from 0.0078125 to 0.0390625
- down_q: bfloat16 [14336, 4096], P('node', 'local'), may hold values from -4 to 4
- down_scale: bfloat16 [14336, 32], P('node', 'local'), may hold values from 0.005004883 to 0.025024414
Outputs:
- states: bfloat16 [512, 4096], P('local', 'node')
- grad_down: bfloat16 [14336, 4096], P('node', 'local')
All inputs are finite; a program needn't handle non-finite values.
Results may differ from a plain program's by a relative error of at most 0.035.
Values may be sent and summed in bfloat16 or wider, within the bound.
No kernel may reach another device: no remote copies, remote signals or barrier semaphores. Data moves between devices by JAX's collectives and lax.ppermute only.
A program may use at most 128 MiB of HBM per device.

v0:
```python
import jax
import jax.numpy as jnp
from jax import lax
from jax.experimental import pallas as pl
from jax.sharding import PartitionSpec as P

LANES = 128
PAD = 16
ROW_TILE = 256
CHUNKS = 2
epsilon = 1e-05
F32 = jnp.float32
BF16 = jnp.bfloat16


def dequant_rows(quanta, scales):
    blocks = scales.shape[0]
    widened = quanta.astype(F32).reshape(blocks, quanta.shape[0] // blocks, quanta.shape[1])
    return (widened * scales.astype(F32)[:, None, :]).reshape(quanta.shape).astype(BF16)


def scale_columns(quanta_ref, scales_ref, out_ref):
    blocks = scales_ref.shape[1]
    width = quanta_ref.shape[1] // blocks
    for block in range(blocks):
        columns = slice(block * width, (block + 1) * width)
        scale = scales_ref[:, block : block + 1].astype(F32)
        out_ref[:, columns] = (quanta_ref[:, columns].astype(F32) * scale).astype(BF16)


def dequant_cols(quanta, scales):
    rows, columns = quanta.shape
    tile = ROW_TILE if rows % ROW_TILE == 0 else rows
    return pl.pallas_call(
        scale_columns,
        grid=(rows // tile,),
        in_specs=[
            pl.BlockSpec((tile, columns), lambda i: (i, 0)),
            pl.BlockSpec((tile, scales.shape[1]), lambda i: (i, 0)),
        ],
        out_specs=pl.BlockSpec((tile, columns), lambda i: (i, 0)),
        out_shape=jax.ShapeDtypeStruct((rows, columns), BF16),
        cost_estimate=pl.CostEstimate(
            flops=rows * columns, bytes_accessed=4 * rows * columns, transcendentals=0
        ),
    )(quanta, scales)


def dot(left, right, dims):
    return lax.dot_general(left, right, (dims, ((), ())), preferred_element_type=F32)


def split_pair(column):
    high = column.astype(BF16)
    low = (column - high.astype(F32)).astype(BF16)
    shape = (column.shape[0], LANES // 2)
    return [jnp.broadcast_to(high, shape), jnp.broadcast_to(low, shape)]


def join_pair(lanes):
    lanes = lanes.astype(F32)
    return lanes[:, :1] + lanes[:, -1:]


def body(n_node, n_local, tokens, cotangent, gain, up_q, up_scale, down_q, down_scale):
    rows, cols = tokens.shape
    part = rows // CHUNKS
    hidden_units = up_q.shape[1]
    halves = n_node // n_local
    chips = n_local
    features = cols * n_node
    z = lax.axis_index("local")
    node = lax.axis_index("node")
    chip, core = node // halves, node % halves
    last = n_local - 1

    swap = [
        ((halves * c + j) * n_local + l, (halves * l + j) * n_local + c)
        for c in range(n_local)
        for j in range(halves)
        for l in range(n_local)
    ]

    def exchange(block):
        return lax.ppermute(block, ("node", "local"), swap)

    def core_swap(block):
        return lax.ppermute(block, "node", [(n, n ^ 1) for n in range(n_node)])

    def chip_swap(block, shift):
        return lax.ppermute(block, "node", [(n, n ^ (2 * shift)) for n in range(n_node)])

    even = z % 2 == 0

    def pair_swap(block, low, used=None):
        pairs = [(s, s + 1) for s in range(low, last, 2) if used is None or used(s)]
        if not pairs:
            return jnp.zeros_like(block)
        return lax.ppermute(block, "local", pairs + [(t, s) for s, t in pairs])

    def after(value, *others):
        return lax.optimization_barrier((value,) + others)[0]

    def take(array, index):
        width = array.shape[1]
        array = array.reshape(-1, n_local, part, width)
        return lax.dynamic_slice_in_dim(array, index, 1, 1).reshape(-1, width)

    def put(array, block, index):
        width = array.shape[1]
        stacked = array.reshape(-1, n_local, part, width)
        block = block.reshape(-1, 1, part, width)
        return lax.dynamic_update_slice_in_dim(stacked, block, index, 1).reshape(array.shape)

    def order(own, other):
        return jnp.where(
            core == 0,
            jnp.concatenate([own, other], axis=1),
            jnp.concatenate([other, own], axis=1),
        )

    def gather_chips(block):
        mine = jnp.zeros((block.shape[0] * chips, block.shape[1]), block.dtype)
        mine = put(mine, block, chip)
        for shift in range(1, chips):
            mine = put(mine, chip_swap(block, shift), chip ^ shift)
        return mine

    def gather_core(mine):
        return order(mine, core_swap(mine))

    def gather_node(block):
        return gather_core(gather_chips(block))

    def scatter_core(partial, tail=()):
        first, second = partial[:, :cols], partial[:, cols:]
        keep = jnp.where(core == 0, first, second)
        send = jnp.where(core == 0, second, first)
        if tail:
            keep = jnp.concatenate([keep, *tail], axis=1)
            send = jnp.concatenate([send, *tail], axis=1)
        return (keep.astype(F32) + core_swap(send).astype(F32)).astype(BF16)

    def swap_chips(both):
        return [chip_swap(take(both, chip ^ shift), shift) for shift in range(1, chips)]

    def scatter_chips(both):
        return sum_chips(both, swap_chips(both))

    def sum_chips(both, others):
        total = take(both, chip).astype(F32)
        for other in others:
            total = total + other.astype(F32)
        return total

    def scatter_node(partial):
        return scatter_chips(scatter_core(partial))

    def line(block, partial):
        first = second = None
        firsts, seconds = [], []
        if block is not None:
            first, second = pair_swap(block, 0), pair_swap(block, 1)
            firsts.append(first)
            seconds.append(second)
        for step in range(1, n_local if partial is not None else last):
            to_first, to_second = second, first
            if partial is not None:
                right = jnp.minimum(z + n_local - step, last)
                left = jnp.maximum(z - n_local + step, 0)
                to_first = take(partial, jnp.where(even, right, left))
                to_second = take(partial, jnp.where(even, left, right))
                if first is not None:
                    zero = jnp.zeros((), F32)
                    adds_right, adds_left = z < step, last - z < step
                    adds = jnp.where(even, adds_right, adds_left)
                    to_first = jnp.where(adds, to_first.astype(F32), zero)
                    to_first = (second.astype(F32) + to_first).astype(BF16)
                    adds = jnp.where(even, adds_left, adds_right)
                    to_second = jnp.where(adds, to_second.astype(F32), zero)
                    to_second = (first.astype(F32) + to_second).astype(BF16)
            used = None
            if block is None:
                used = lambda s, step=step: s < step or s + 1 > last - step
            elif partial is None:
                used = lambda s, step=step: s >= step or s + 1 <= last - step
            first, second = pair_swap(to_first, 0, used), pair_swap(to_second, 1, used)
            firsts.append(first)
            seconds.append(second)
        total = None
        if partial is not None:
            total = take(partial, z).astype(F32) + first.astype(F32) + second.astype(F32)
        out = None
        if block is not None:
            out = jnp.zeros((part * n_local, block.shape[1]), block.dtype)
            out = put(out, block, z)
            for ahead in range(1, n_local):
                behind = n_local - ahead
                right = jnp.where(even, seconds[behind - 1], firsts[behind - 1])
                left = jnp.where(even, firsts[ahead - 1], seconds[ahead - 1])
                piece = jnp.where(z >= behind, right, left)
                out = put(out, piece, (z + ahead) % n_local)
        return out, total

    def widen(block):
        return jnp.pad(block, ((0, 0), (0, LANES)))

    def chunk_of(array, h):
        size = part * n_local
        return array[h * size : (h + 1) * size]

    def up_partial(values):
        widened = values.astype(F32)
        squares = 0.0
        for start in range(0, values.shape[1], LANES):
            lanes = widened[:, start : start + LANES]
            squares = squares + lanes * lanes
        product = dot((widened * gains).astype(BF16), up_weight, ((1,), (0,)))
        return jnp.concatenate([product.astype(BF16), squares.astype(BF16)], axis=1)

    def finish_pre(total):
        mean = jnp.sum(total[:, hidden_units:], axis=-1, keepdims=True) / features
        factor = lax.rsqrt(mean + epsilon)
        return total[:, :hidden_units] * factor, factor

    x_home = exchange(tokens)
    other = exchange(jnp.concatenate([cotangent, jnp.pad(gain, ((0, PAD - 1), (0, 0)))], axis=0))
    g_home, gain_rows = other[:rows], other[rows:]
    down_weight = dequant_cols(down_q, down_scale)
    x_home = after(x_home, down_weight)
    up_weight = dequant_rows(after(up_q, x_home), up_scale)
    gains = order(gain_rows, core_swap(gain_rows))[:1].astype(F32)
    gains_home = gain_rows[:1].astype(F32)

    halves_of = range(CHUNKS)

    x = gather_core(after(gather_chips(x_home), g_home))
    partials = [up_partial(chunk_of(x, h)) for h in halves_of]
    totals = [line(None, partial)[1] for partial in partials]
    g = gather_node(after(g_home, *partials))
    slopes = [
        dot(chunk_of(g, h), down_weight, ((1,), (1,))).astype(BF16) for h in halves_of
    ]
    hiddens = []
    for h in halves_of:
        hidden = jax.nn.silu(finish_pre(totals[h])[0]).astype(BF16)
        hidden, total = line(hidden, slopes[h])
        hiddens.append(hidden)
        slopes[h] = total.astype(BF16)
    updates = [dot(hidden, down_weight, ((1,), (0,))).astype(BF16) for hidden in hiddens]
    update = scatter_node(jnp.concatenate(updates, axis=0))
    x1_home = (x_home.astype(F32) + update).astype(BF16)

    x = gather_node(x1_home)
    packed = []
    for h in halves_of:
        slope, total = line(widen(slopes[h]), up_partial(chunk_of(x, h)))
        slopes[h] = slope[:, :hidden_units]
        pre, factor = finish_pre(total)
        packed.append(
            line(jnp.concatenate([pre.astype(BF16)] + split_pair(factor), axis=1), None)[0]
        )

    hidden_second, updates, backs, tails = [], [], [], []

    def hidden_of(half):
        pre = half[:, :hidden_units].astype(F32)
        hidden_second.append((pre * jax.nn.sigmoid(pre)).astype(BF16))
        updates.append(dot(hidden_second[-1], down_weight, ((1,), (0,))).astype(BF16))

    def back_of(half, slope):
        pre = half[:, :hidden_units].astype(F32)
        sigma = jax.nn.sigmoid(pre)
        pre_grad = slope.astype(F32) * sigma * (1.0 + pre * (1.0 - sigma))
        inner = jnp.sum(pre_grad * pre, axis=-1, keepdims=True)
        tails.append(jnp.concatenate(split_pair(inner), axis=1))
        backs.append(dot(pre_grad.astype(BF16), up_weight, ((1,), (1,))).astype(BF16))

    hidden_of(packed[0])
    back_of(packed[0], slopes[0])
    packed[1] = after(packed[1], backs[0])
    hidden_of(packed[1])
    update = scatter_core(jnp.concatenate(updates, axis=0))
    back_of(packed[1], after(slopes[1], update))
    both = scatter_core(jnp.concatenate(backs, axis=0), [jnp.concatenate(tails, axis=0)])
    others = swap_chips(update)
    x2_home = (x1_home.astype(F32) + sum_chips(update, others)).astype(BF16)
    result = exchange(x2_home)
    total = scatter_chips(after(both, x2_home))
    lanes = [take(half[:, hidden_units:], chip) for half in packed]
    factor = join_pair(jnp.concatenate(lanes, axis=0))
    inner = join_pair(total[:, cols:]) / (features * factor)
    back = factor * (total[:, :cols] * gains_home) - x1_home.astype(F32) * (factor**3 * inner)
    grad_home = (g_home.astype(F32) + back).astype(BF16)
    below = gather_node(after(grad_home, result))
    grad_down = dot(
        jnp.concatenate(hiddens + hidden_second, axis=0),
        jnp.concatenate([below, g], axis=0),
        ((0,), (0,)),
    ).astype(BF16)
    return (result, grad_down)


def solution(mesh):
    n_node, n_local = mesh.shape["node"], mesh.shape["local"]

    def per_device(*arrays):
        return body(n_node, n_local, *arrays)

    in_specs = (
        P("local", "node"),
        P("local", "node"),
        P(None, "node"),
        P("local", "node"),
        P("local", "node"),
        P("node", "local"),
        P("node", "local"),
    )
    out_specs = (P("local", "node"), P("node", "local"))
    return jax.shard_map(
        per_device, mesh=mesh, in_specs=in_specs, out_specs=out_specs, check_vma=False
    )
```

profile of v0, /device:TPU:2, one launch (start us, length us, event | category | flops | bytes accessed | tf_op | source)
XLA Modules:
  0.0 269.6 jit_solution(9406374479323916753)
XLA Ops:
  0.6 3.5 %collective-permute-start = (bf16[128,512]{1,0:T(8,128)(2,1)}, bf16[128,512]{1,0:T(8,128)(2,1)S(1)}, u32[]{:S(2)}, u32[]{:S(2)}) collective-permute-start(bf16[128,512]{1,0:T(8,128)(2,1)} %param.7), channel_id=1, source_target_pairs={{0,0},{1,8},{2,16},{3,24},{4,4},{5,12},{6,20},{7,28},{8,1},{9,9},{... | collective-permute-start | bytes 393224 | tf_op jit(solution)/shard_map/ppermute | solution.py:85
  5.0 3.3 %collective-permute-start.4 = (bf16[144,512]{1,0:T(8,128)(2,1)S(1)}, bf16[144,512]{1,0:T(8,128)(2,1)S(1)}, u32[]{:S(2)}, u32[]{:S(2)}) collective-permute-start(bf16[144,512]{1,0:T(8,128)(2,1)S(1)} %fusion.92), channel_id=1, source_target_pairs={{0,0},{1,8},{2,16},{3,24},{4,4},{5,12},{6,20},{7,28},{8,1},{9,9},{... | collective-permute-start | bytes 442376 | tf_op jit(solution)/shard_map/ppermute | solution.py:85
  10.0 6.8 %shard_map.86 = bf16[1792,1024]{1,0:T(8,128)(2,1)} custom-call(bf16[1792,1024]{1,0:T(8,128)(2,1)} %quanta_ref.1, bf16[1792,8]{1,0:T(8,128)(2,1)} %copy.26.scales_ref), custom_call_target="tpu_custom_call" | custom-call | flops 1835008 | bytes 7340032 | tf_op jit(solution)/shard_map/pallas_call | solution.py:34
  16.8 5.0 %collective-permute-done = bf16[128,512]{1,0:T(8,128)(2,1)S(1)} collective-permute-done((bf16[128,512]{1,0:T(8,128)(2,1)}, bf16[128,512]{1,0:T(8,128)(2,1)S(1)}, u32[]{:S(2)}, u32[]{:S(2)}) %collective-permute-start) | collective-permute-done | bytes 131104 | tf_op jit(solution)/shard_map/ppermute | solution.py:85
  21.9 3.5 %collective-permute-start.3 = (bf16[128,512]{1,0:T(8,128)(2,1)S(1)}, bf16[128,512]{1,0:T(8,128)(2,1)S(1)}, u32[]{:S(2)}, u32[]{:S(2)}) collective-permute-start(bf16[128,512]{1,0:T(8,128)(2,1)S(1)} %collective-permute-done), channel_id=1, source_target_pairs={{0,24},{4,28},{8,16},{12,20},{16,8},{20,12},{24,0},{28,4},{1,25},{... | collective-permute-start | bytes 393224 | tf_op jit(solution)/shard_map/ppermute | solution.py:91
  25.4 2.7 %collective-permute-done.1 = bf16[128,512]{1,0:T(8,128)(2,1)S(1)} collective-permute-done((bf16[128,512]{1,0:T(8,128)(2,1)S(1)}, bf16[128,512]{1,0:T(8,128)(2,1)S(1)}, u32[]{:S(2)}, u32[]{:S(2)}) %collective-permute-start.1) | collective-permute-done | bytes 131104 | tf_op jit(solution)/shard_map/ppermute | solution.py:91
  29.3 2.7 %fusion = bf16[1024,1792]{1,0:T(8,128)(2,1)S(1)} fusion(bf16[1024,1792]{1,0:T(8,128)(2,1)} %param.10, f32[8,1792]{1,0:T(8,128)S(1)} %convert_element_type.736), kind=kLoop, calls=%fused_computation.1 | loop fusion | flops 5505024 | bytes 7397376 | tf_op jit(solution)/shard_map/convert_element_type | solution.py:19
  39.4 2.0 collective-permute-start.10
  41.8 2.2 collective-permute-done.14
  45.5 2.8 %collective-permute-done.7 = bf16[64,1920]{1,0:T(8,128)(2,1)S(1)} collective-permute-done((bf16[64,1920]{1,0:T(8,128)(2,1)S(1)}, bf16[64,1920]{1,0:T(8,128)(2,1)S(1)}, u32[]{:S(2)}, u32[]{:S(2)}) %collective-permute-start.7) | collective-permute-done | bytes 245792 | tf_op jit(solution)/shard_map/ppermute | solution.py:99
  49.1 9.8 %collective-permute-done.22 = bf16[64,1920]{1,0:T(8,128)(2,1)S(1)} collective-permute-done((bf16[64,1920]{1,0:T(8,128)(2,1)S(1)}, bf16[64,1920]{1,0:T(8,128)(2,1)S(1)}, u32[]{:S(2)}, u32[]{:S(2)}) %collective-permute-start.22) | collective-permute-done | bytes 245792 | tf_op jit(solution)/shard_map/ppermute | solution.py:99
  60.6 6.1 %collective-permute-start.9 = (bf16[64,1920]{1,0:T(8,128)(2,1)S(1)}, bf16[64,1920]{1,0:T(8,128)(2,1)S(1)}, u32[]{:S(2)}, u32[]{:S(2)}) collective-permute-start(bf16[64,1920]{1,0:T(8,128)(2,1)S(1)} %get-tuple-element.54), channel_id=1, source_target_pairs={{0,1},{2,3},{1,0},{3,2},{4,5},{6,7},{5,4},{7,6},{8,9},{10,11},{9,8... | collective-permute-start | bytes 737288 | tf_op jit(solution)/shard_map/ppermute | solution.py:99
  66.9 4.2 %collective-permute-start.24 = (bf16[64,1920]{1,0:T(8,128)(2,1)S(1)}, bf16[64,1920]{1,0:T(8,128)(2,1)S(1)}, u32[]{:S(2)}, u32[]{:S(2)}) collective-permute-start(bf16[64,1920]{1,0:T(8,128)(2,1)S(1)} %get-tuple-element.56), channel_id=1, source_target_pairs={{0,1},{2,3},{1,0},{3,2},{4,5},{6,7},{5,4},{7,6},{8,9},{10,11},{9,8... | collective-permute-start | bytes 737288 | tf_op jit(solution)/shard_map/ppermute | solution.py:99
  75.6 4.6 %collective-permute-start.19 = (bf16[64,1792]{1,0:T(8,128)(2,1)S(1)}, bf16[64,1792]{1,0:T(8,128)(2,1)S(1)}, u32[]{:S(2)}, u32[]{:S(2)}) collective-permute-start(bf16[64,1792]{1,0:T(8,128)(2,1)S(1)} %get-tuple-element.29), channel_id=1, source_target_pairs={{0,1},{2,3},{1,0},{3,2},{4,5},{6,7},{5,4},{7,6},{8,9},{10,11},{9,8... | collective-permute-start | bytes 688136 | tf_op jit(solution)/shard_map/ppermute | solution.py:99
  81.4 3.5 %collective-permute-start.30 = (bf16[64,1792]{1,0:T(8,128)(2,1)S(1)}, bf16[64,1792]{1,0:T(8,128)(2,1)S(1)}, u32[]{:S(2)}, u32[]{:S(2)}) collective-permute-start(bf16[64,1792]{1,0:T(8,128)(2,1)S(1)} %get-tuple-element.31), channel_id=1, source_target_pairs={{0,1},{2,3},{1,0},{3,2},{4,5},{6,7},{5,4},{7,6},{8,9},{10,11},{9,8... | collective-permute-start | bytes 688136 | tf_op jit(solution)/shard_map/ppermute | solution.py:99
  86.9 2.1 collective-permute-start.17
  89.6 2.0 collective-permute-done.30
  91.8 2.1 collective-permute-start.28
  96.2 6.6 %collective-permute-start.21 = (bf16[64,1792]{1,0:T(8,128)(2,1)S(1)}, bf16[64,1792]{1,0:T(8,128)(2,1)S(1)}, u32[]{:S(2)}, u32[]{:S(2)}) collective-permute-start(bf16[64,1792]{1,0:T(8,128)(2,1)S(1)} %get-tuple-element.62), channel_id=1, source_target_pairs={{0,1},{2,3},{1,0},{3,2},{4,5},{6,7},{5,4},{7,6},{8,9},{10,11},{9,8... | collective-permute-start | bytes 688136 | tf_op jit(solution)/shard_map/ppermute | solution.py:99
  103.8 4.1 %collective-permute-start.32 = (bf16[64,1792]{1,0:T(8,128)(2,1)S(1)}, bf16[64,1792]{1,0:T(8,128)(2,1)S(1)}, u32[]{:S(2)}, u32[]{:S(2)}) collective-permute-start(bf16[64,1792]{1,0:T(8,128)(2,1)S(1)} %get-tuple-element.66), channel_id=1, source_target_pairs={{0,1},{2,3},{1,0},{3,2},{4,5},{6,7},{5,4},{7,6},{8,9},{10,11},{9,8... | collective-permute-start | bytes 688136 | tf_op jit(solution)/shard_map/ppermute | solution.py:99
  109.4 2.4 collective-permute-done.32
  113.8 2.1 collective-permute-start.41
  120.5 2.4 collective-permute-done.34
  122.9 2.1 collective-permute-start.56
  129.3 3.0 %collective-permute-done.37 = bf16[128,512]{1,0:T(8,128)(2,1)S(1)} collective-permute-done((bf16[128,512]{1,0:T(8,128)(2,1)S(1)}, bf16[128,512]{1,0:T(8,128)(2,1)S(1)}, u32[]{:S(2)}, u32[]{:S(2)}) %collective-permute-start.37) | collective-permute-done | bytes 131104 | tf_op jit(solution)/shard_map/ppermute | solution.py:91
  133.7 7.3 %collective-permute-start.47 = (bf16[64,1920]{1,0:T(8,128)(2,1)S(1)}, bf16[64,1920]{1,0:T(8,128)(2,1)S(1)}, u32[]{:S(2)}, u32[]{:S(2)}) collective-permute-start(bf16[64,1920]{1,0:T(8,128)(2,1)S(1)} %pad.12), channel_id=1, source_target_pairs={{0,1},{2,3},{1,0},{3,2},{4,5},{6,7},{5,4},{7,6},{8,9},{10,11},{9,8... | collective-permute-start | bytes 737288 | tf_op jit(solution)/shard_map/ppermute | solution.py:99
  142.0 3.5 %collective-permute-start.62 = (bf16[64,1920]{1,0:T(8,128)(2,1)S(1)}, bf16[64,1920]{1,0:T(8,128)(2,1)S(1)}, u32[]{:S(2)}, u32[]{:S(2)}) collective-permute-start(bf16[64,1920]{1,0:T(8,128)(2,1)S(1)} %pad.13), channel_id=1, source_target_pairs={{0,1},{2,3},{1,0},{3,2},{4,5},{6,7},{5,4},{7,6},{8,9},{10,11},{9,8... | collective-permute-start | bytes 737288 | tf_op jit(solution)/shard_map/ppermute | solution.py:99
  149.8 2.3 collective-permute-done.62
  152.3 2.4 collective-permute-start.59
  155.3 2.4 collective-permute-done.44
  158.6 6.6 %collective-permute-start.49 = (bf16[64,1920]{1,0:T(8,128)(2,1)S(1)}, bf16[64,1920]{1,0:T(8,128)(2,1)S(1)}, u32[]{:S(2)}, u32[]{:S(2)}) collective-permute-start(bf16[64,1920]{1,0:T(8,128)(2,1)S(1)} %get-tuple-element.44), channel_id=1, source_target_pairs={{0,1},{2,3},{1,0},{3,2},{4,5},{6,7},{5,4},{7,6},{8,9},{10,11},{9,8... | collective-permute-start | bytes 737288 | tf_op jit(solution)/shard_map/ppermute | solution.py:99
  166.1 4.4 %collective-permute-start.64 = (bf16[64,1920]{1,0:T(8,128)(2,1)S(1)}, bf16[64,1920]{1,0:T(8,128)(2,1)S(1)}, u32[]{:S(2)}, u32[]{:S(2)}) collective-permute-start(bf16[64,1920]{1,0:T(8,128)(2,1)S(1)} %get-tuple-element.51), channel_id=1, source_target_pairs={{0,1},{2,3},{1,0},{3,2},{4,5},{6,7},{5,4},{7,6},{8,9},{10,11},{9,8... | collective-permute-start | bytes 737288 | tf_op jit(solution)/shard_map/ppermute | solution.py:99
  170.7 2.2 collective-permute-start.46
  173.6 3.8 %collective-permute-done.64 = bf16[64,1920]{1,0:T(8,128)(2,1)S(1)} collective-permute-done((bf16[64,1920]{1,0:T(8,128)(2,1)S(1)}, bf16[64,1920]{1,0:T(8,128)(2,1)S(1)}, u32[]{:S(2)}, u32[]{:S(2)}) %collective-permute-start.64) | collective-permute-done | bytes 245792 | tf_op jit(solution)/shard_map/ppermute | solution.py:99
  178.3 2.0 collective-permute-start.61
  183.2 2.1 collective-permute-start.51
  189.7 2.1 collective-permute-start.66
  193.9 2.0 collective-permute-done.66
  196.8 9.8 %collective-permute-start.53 = (bf16[64,1920]{1,0:T(8,128)(2,1)S(1)}, bf16[64,1920]{1,0:T(8,128)(2,1)S(1)}, u32[]{:S(2)}, u32[]{:S(2)}) collective-permute-start(bf16[64,1920]{1,0:T(8,128)(2,1)S(1)} %collective-permute-done.52), channel_id=1, source_target_pairs={{0,1},{2,3},{1,0},{3,2},{4,5},{6,7},{5,4},{7,6},{8,9},{10,11},{9,8... | collective-permute-start | bytes 737288 | tf_op jit(solution)/shard_map/ppermute | solution.py:99
  206.8 2.0 collective-permute-start.70
  209.2 4.2 %collective-permute-done.53 = bf16[64,1920]{1,0:T(8,128)(2,1)S(1)} collective-permute-done((bf16[64,1920]{1,0:T(8,128)(2,1)S(1)}, bf16[64,1920]{1,0:T(8,128)(2,1)S(1)}, u32[]{:S(2)}, u32[]{:S(2)}) %collective-permute-start.53) | collective-permute-done | bytes 245792 | tf_op jit(solution)/shard_map/ppermute | solution.py:99
  213.6 3.3 %collective-permute-done.55 = bf16[64,1920]{1,0:T(8,128)(2,1)S(1)} collective-permute-done((bf16[64,1920]{1,0:T(8,128)(2,1)}, bf16[64,1920]{1,0:T(8,128)(2,1)S(1)}, u32[]{:S(2)}, u32[]{:S(2)}) %collective-permute-start.55) | collective-permute-done | bytes 245792 | tf_op jit(solution)/shard_map/ppermute | solution.py:99
  233.1 2.8 %collective-permute-done.72 = bf16[128,512]{1,0:T(8,128)(2,1)S(1)} collective-permute-done((bf16[128,512]{1,0:T(8,128)(2,1)S(1)}, bf16[128,512]{1,0:T(8,128)(2,1)S(1)}, u32[]{:S(2)}, u32[]{:S(2)}) %collective-permute-start.72) | collective-permute-done | bytes 131104 | tf_op jit(solution)/shard_map/ppermute | solution.py:91
  235.9 2.3 collective-permute-done.73
  242.3 5.0 %collective-permute-start.75 = (bf16[128,512]{1,0:T(8,128)(2,1)S(1)}, bf16[128,512]{1,0:T(8,128)(2,1)S(1)}, u32[]{:S(2)}, u32[]{:S(2)}) collective-permute-start(bf16[128,512]{1,0:T(8,128)(2,1)S(1)} %fusion.79), channel_id=1, source_target_pairs={{0,0},{1,8},{2,16},{3,24},{4,4},{5,12},{6,20},{7,28},{8,1},{9,9},{... | collective-permute-start | bytes 393224 | tf_op jit(solution)/shard_map/ppermute | solution.py:85
  249.6 5.0 %collective-permute-done.75 = bf16[128,512]{1,0:T(8,128)(2,1)S(1)} collective-permute-done((bf16[128,512]{1,0:T(8,128)(2,1)S(1)}, bf16[128,512]{1,0:T(8,128)(2,1)S(1)}, u32[]{:S(2)}, u32[]{:S(2)}) %collective-permute-start.75) | collective-permute-done | bytes 131104 | tf_op jit(solution)/shard_map/ppermute | solution.py:85
  255.2 2.8 %collective-permute-start.82 = (bf16[128,512]{1,0:T(8,128)(2,1)S(1)}, bf16[128,512]{1,0:T(8,128)(2,1)S(1)}, u32[]{:S(2)}, u32[]{:S(2)}) collective-permute-start(bf16[128,512]{1,0:T(8,128)(2,1)S(1)} %fusion.82), channel_id=1, source_target_pairs={{0,24},{4,28},{8,16},{12,20},{16,8},{20,12},{24,0},{28,4},{1,25},{... | collective-permute-start | bytes 393224 | tf_op jit(solution)/shard_map/ppermute | solution.py:91
  263.4 5.5 %convolution_convert_fusion = bf16[1792,1024]{1,0:T(8,128)(2,1)} fusion(bf16[256,1792]{1,0:T(8,128)(2,1)S(1)} %get-tuple-element.41, bf16[256,1792]{1,0:T(8,128)(2,1)S(1)} %get-tuple-element.39, bf16[256,1792]{1,0:T(8,128)(2,1)S(1)} %bitcast.357, bf16[256,1792]{1,0:T(8,128)(2,1)S(1)} %bitcast.355, bf16[512,1024]{1,0:T(8,128)(2,1)S(1)} %copy-done.5, ...), kind=kOutput, calls=%fused_computation.2 | convolution fusion | flops 3778805760 | bytes 9437184 | tf_op jit(solution)/shard_map/dot_general | solution.py:50
  (307 shorter events, 90.2 us)
Async XLA Ops:
  0.6 21.2 %collective-permute-start = (bf16[128,512]{1,0:T(8,128)(2,1)}, bf16[128,512]{1,0:T(8,128)(2,1)S(1)}, u32[]{:S(2)}, u32[]{:S(2)}) collective-permute-start(bf16[128,512]{1,0:T(8,128)(2,1)} %param.7), channel_id=1, source_target_pairs={{0,0},{1,8},{2,16},{3,24},{4,4},{5,12},{6,20},{7,28},{8,1},{9,9},{... | collective-permute-start | bytes 393224 | tf_op jit(solution)/shard_map/ppermute | solution.py:85
  5.0 20.4 %collective-permute-start.4 = (bf16[144,512]{1,0:T(8,128)(2,1)S(1)}, bf16[144,512]{1,0:T(8,128)(2,1)S(1)}, u32[]{:S(2)}, u32[]{:S(2)}) collective-permute-start(bf16[144,512]{1,0:T(8,128)(2,1)S(1)} %fusion.92), channel_id=1, source_target_pairs={{0,0},{1,8},{2,16},{3,24},{4,4},{5,12},{6,20},{7,28},{8,1},{9,9},{... | collective-permute-start | bytes 442376 | tf_op jit(solution)/shard_map/ppermute | solution.py:85
  39.4 9.0 %collective-permute-start.7 = (bf16[64,1920]{1,0:T(8,128)(2,1)S(1)}, bf16[64,1920]{1,0:T(8,128)(2,1)S(1)}, u32[]{:S(2)}, u32[]{:S(2)}) collective-permute-start(bf16[64,1920]{1,0:T(8,128)(2,1)S(1)} %dynamic-slice_bitcast_fusion.1), channel_id=1, source_target_pairs={{0,1},{2,3},{1,0},{3,2},{4,5},{6,7},{5,4},{7,6},{8,9},{10,11},{9,8... | collective-permute-start | bytes 737288 | tf_op jit(solution)/shard_map/ppermute | solution.py:99
  39.4 20.2 %collective-permute-start.10 = (bf16[64,1920]{1,0:T(8,128)(2,1)S(1)}, bf16[64,1920]{1,0:T(8,128)(2,1)S(1)}, u32[]{:S(2)}, u32[]{:S(2)}) collective-permute-start(bf16[64,1920]{1,0:T(8,128)(2,1)S(1)} %fusion.90), channel_id=1, source_target_pairs={{0,1},{2,3},{1,0},{3,2},{4,5},{6,7},{5,4},{7,6},{8,9},{10,11},{9,8... | collective-permute-start | bytes 737288 | tf_op jit(solution)/shard_map/ppermute | solution.py:99
  41.5 17.3 %collective-permute-start.22 = (bf16[64,1920]{1,0:T(8,128)(2,1)S(1)}, bf16[64,1920]{1,0:T(8,128)(2,1)S(1)}, u32[]{:S(2)}, u32[]{:S(2)}) collective-permute-start(bf16[64,1920]{1,0:T(8,128)(2,1)S(1)} %dynamic-slice_bitcast_fusion), channel_id=1, source_target_pairs={{0,1},{2,3},{1,0},{3,2},{4,5},{6,7},{5,4},{7,6},{8,9},{10,11},{9,8... | collective-permute-start | bytes 737288 | tf_op jit(solution)/shard_map/ppermute | solution.py:99
  44.0 22.7 %collective-permute-start.25 = (bf16[64,1920]{1,0:T(8,128)(2,1)S(1)}, bf16[64,1920]{1,0:T(8,128)(2,1)S(1)}, u32[]{:S(2)}, u32[]{:S(2)}) collective-permute-start(bf16[64,1920]{1,0:T(8,128)(2,1)S(1)} %fusion.91), channel_id=1, source_target_pairs={{0,1},{2,3},{1,0},{3,2},{4,5},{6,7},{5,4},{7,6},{8,9},{10,11},{9,8... | collective-permute-start | bytes 737288 | tf_op jit(solution)/shard_map/ppermute | solution.py:99
  45.5 26.2 %collective-permute-start.16 = (bf16[512,512]{1,0:T(8,128)(2,1)S(1)}, bf16[512,512]{1,0:T(8,128)(2,1)S(1)}, u32[]{:S(2)}, u32[]{:S(2)}) collective-permute-start(bf16[512,512]{1,0:T(8,128)(2,1)S(1)} %bitcast.349), channel_id=1, source_target_pairs={{0,4},{4,0},{8,12},{12,8},{16,20},{20,16},{24,28},{28,24},{1,5},{5... | collective-permute-start | bytes 1572872 | tf_op jit(solution)/shard_map/ppermute | solution.py:88
  48.4 11.2 %collective-permute-start.8 = (bf16[64,1920]{1,0:T(8,128)(2,1)S(1)}, bf16[64,1920]{1,0:T(8,128)(2,1)S(1)}, u32[]{:S(2)}, u32[]{:S(2)}) collective-permute-start(bf16[64,1920]{1,0:T(8,128)(2,1)S(1)} %fusion.57), channel_id=1, source_target_pairs={{1,2},{2,1},{5,6},{6,5},{9,10},{10,9},{13,14},{14,13},{17,18},{18,... | collective-permute-start | bytes 737288 | tf_op jit(solution)/shard_map/ppermute | solution.py:99
  59.8 14.6 %collective-permute-start.11 = (bf16[64,1920]{1,0:T(8,128)(2,1)S(1)}, bf16[64,1920]{1,0:T(8,128)(2,1)S(1)}, u32[]{:S(2)}, u32[]{:S(2)}) collective-permute-start(bf16[64,1920]{1,0:T(8,128)(2,1)S(1)} %get-tuple-element.55), channel_id=1, source_target_pairs={{1,2},{2,1},{5,6},{6,5},{9,10},{10,9},{13,14},{14,13},{17,18},{18,... | collective-permute-start | bytes 737288 | tf_op jit(solution)/shard_map/ppermute | solution.py:99
  60.6 13.8 %collective-permute-start.9 = (bf16[64,1920]{1,0:T(8,128)(2,1)S(1)}, bf16[64,1920]{1,0:T(8,128)(2,1)S(1)}, u32[]{:S(2)}, u32[]{:S(2)}) collective-permute-start(bf16[64,1920]{1,0:T(8,128)(2,1)S(1)} %get-tuple-element.54), channel_id=1, source_target_pairs={{0,1},{2,3},{1,0},{3,2},{4,5},{6,7},{5,4},{7,6},{8,9},{10,11},{9,8... | collective-permute-start | bytes 737288 | tf_op jit(solution)/shard_map/ppermute | solution.py:99
  66.9 13.3 %collective-permute-start.24 = (bf16[64,1920]{1,0:T(8,128)(2,1)S(1)}, bf16[64,1920]{1,0:T(8,128)(2,1)S(1)}, u32[]{:S(2)}, u32[]{:S(2)}) collective-permute-start(bf16[64,1920]{1,0:T(8,128)(2,1)S(1)} %get-tuple-element.56), channel_id=1, source_target_pairs={{0,1},{2,3},{1,0},{3,2},{4,5},{6,7},{5,4},{7,6},{8,9},{10,11},{9,8... | collective-permute-start | bytes 737288 | tf_op jit(solution)/shard_map/ppermute | solution.py:99
  71.0 9.2 %collective-permute-start.26 = (bf16[64,1920]{1,0:T(8,128)(2,1)S(1)}, bf16[64,1920]{1,0:T(8,128)(2,1)S(1)}, u32[]{:S(2)}, u32[]{:S(2)}) collective-permute-start(bf16[64,1920]{1,0:T(8,128)(2,1)S(1)} %get-tuple-element.57), channel_id=1, source_target_pairs={{1,2},{2,1},{5,6},{6,5},{9,10},{10,9},{13,14},{14,13},{17,18},{18,... | collective-permute-start | bytes 737288 | tf_op jit(solution)/shard_map/ppermute | solution.py:99
  74.9 10.0 %collective-permute-start.12 = (bf16[64,1792]{1,0:T(8,128)(2,1)S(1)}, bf16[64,1792]{1,0:T(8,128)(2,1)S(1)}, u32[]{:S(2)}, u32[]{:S(2)}) collective-permute-start(bf16[64,1792]{1,0:T(8,128)(2,1)S(1)} %get-tuple-element.29), channel_id=1, source_target_pairs={{1,2},{2,1},{5,6},{6,5},{9,10},{10,9},{13,14},{14,13},{17,18},{18,... | collective-permute-start | bytes 688136 | tf_op jit(solution)/shard_map/ppermute | solution.py:99
  75.6 11.1 %collective-permute-start.19 = (bf16[64,1792]{1,0:T(8,128)(2,1)S(1)}, bf16[64,1792]{1,0:T(8,128)(2,1)S(1)}, u32[]{:S(2)}, u32[]{:S(2)}) collective-permute-start(bf16[64,1792]{1,0:T(8,128)(2,1)S(1)} %get-tuple-element.29), channel_id=1, source_target_pairs={{0,1},{2,3},{1,0},{3,2},{4,5},{6,7},{5,4},{7,6},{8,9},{10,11},{9,8... | collective-permute-start | bytes 688136 | tf_op jit(solution)/shard_map/ppermute | solution.py:99
  80.7 8.9 %collective-permute-start.27 = (bf16[64,1792]{1,0:T(8,128)(2,1)S(1)}, bf16[64,1792]{1,0:T(8,128)(2,1)S(1)}, u32[]{:S(2)}, u32[]{:S(2)}) collective-permute-start(bf16[64,1792]{1,0:T(8,128)(2,1)S(1)} %get-tuple-element.31), channel_id=1, source_target_pairs={{1,2},{2,1},{5,6},{6,5},{9,10},{10,9},{13,14},{14,13},{17,18},{18,... | collective-permute-start | bytes 688136 | tf_op jit(solution)/shard_map/ppermute | solution.py:99
  81.4 10.3 %collective-permute-start.30 = (bf16[64,1792]{1,0:T(8,128)(2,1)S(1)}, bf16[64,1792]{1,0:T(8,128)(2,1)S(1)}, u32[]{:S(2)}, u32[]{:S(2)}) collective-permute-start(bf16[64,1792]{1,0:T(8,128)(2,1)S(1)} %get-tuple-element.31), channel_id=1, source_target_pairs={{0,1},{2,3},{1,0},{3,2},{4,5},{6,7},{5,4},{7,6},{8,9},{10,11},{9,8... | collective-permute-start | bytes 688136 | tf_op jit(solution)/shard_map/ppermute | solution.py:99
  91.8 11.0 %collective-permute-start.28 = (bf16[64,1792]{1,0:T(8,128)(2,1)S(1)}, bf16[64,1792]{1,0:T(8,128)(2,1)S(1)}, u32[]{:S(2)}, u32[]{:S(2)}) collective-permute-start(bf16[64,1792]{1,0:T(8,128)(2,1)S(1)} %get-tuple-element.69), channel_id=1, source_target_pairs={{0,1},{2,3},{1,0},{3,2},{4,5},{6,7},{5,4},{7,6},{8,9},{10,11},{9,8... | collective-permute-start | bytes 688136 | tf_op jit(solution)/shard_map/ppermute | solution.py:99
  93.9 8.9 %collective-permute-start.31 = (bf16[64,1792]{1,0:T(8,128)(2,1)S(1)}, bf16[64,1792]{1,0:T(8,128)(2,1)S(1)}, u32[]{:S(2)}, u32[]{:S(2)}) collective-permute-start(bf16[64,1792]{1,0:T(8,128)(2,1)S(1)} %get-tuple-element.68), channel_id=1, source_target_pairs={{1,2},{2,1},{5,6},{6,5},{9,10},{10,9},{13,14},{14,13},{17,18},{18,... | collective-permute-start | bytes 688136 | tf_op jit(solution)/shard_map/ppermute | solution.py:99
  95.5 12.4 %collective-permute-start.18 = (bf16[64,1792]{1,0:T(8,128)(2,1)S(1)}, bf16[64,1792]{1,0:T(8,128)(2,1)S(1)}, u32[]{:S(2)}, u32[]{:S(2)}) collective-permute-start(bf16[64,1792]{1,0:T(8,128)(2,1)S(1)} %get-tuple-element.63), channel_id=1, source_target_pairs={{1,2},{2,1},{5,6},{6,5},{9,10},{10,9},{13,14},{14,13},{17,18},{18,... | collective-permute-start | bytes 688136 | tf_op jit(solution)/shard_map/ppermute | solution.py:99
  96.2 11.7 %collective-permute-start.21 = (bf16[64,1792]{1,0:T(8,128)(2,1)S(1)}, bf16[64,1792]{1,0:T(8,128)(2,1)S(1)}, u32[]{:S(2)}, u32[]{:S(2)}) collective-permute-start(bf16[64,1792]{1,0:T(8,128)(2,1)S(1)} %get-tuple-element.62), channel_id=1, source_target_pairs={{0,1},{2,3},{1,0},{3,2},{4,5},{6,7},{5,4},{7,6},{8,9},{10,11},{9,8... | collective-permute-start | bytes 688136 | tf_op jit(solution)/shard_map/ppermute | solution.py:99
  113.8 14.1 %collective-permute-start.41 = (bf16[64,1792]{1,0:T(8,128)(2,1)S(1)}, bf16[64,1792]{1,0:T(8,128)(2,1)S(1)}, u32[]{:S(2)}, u32[]{:S(2)}) collective-permute-start(bf16[64,1792]{1,0:T(8,128)(2,1)S(1)} %get-tuple-element.58), channel_id=1, source_target_pairs={{0,1},{2,3},{1,0},{3,2},{4,5},{6,7},{5,4},{7,6},{8,9},{10,11},{9,8... | collective-permute-start | bytes 688136 | tf_op jit(solution)/shard_map/ppermute | solution.py:99
  115.8 12.0 %collective-permute-start.42 = (bf16[64,1792]{1,0:T(8,128)(2,1)S(1)}, bf16[64,1792]{1,0:T(8,128)(2,1)S(1)}, u32[]{:S(2)}, u32[]{:S(2)}) collective-permute-start(bf16[64,1792]{1,0:T(8,128)(2,1)S(1)} %get-tuple-element.59), channel_id=1, source_target_pairs={{1,2},{2,1},{5,6},{6,5},{9,10},{10,9},{13,14},{14,13},{17,18},{18,... | collective-permute-start | bytes 688136 | tf_op jit(solution)/shard_map/ppermute | solution.py:99
  122.9 18.3 %collective-permute-start.56 = (bf16[64,1792]{1,0:T(8,128)(2,1)S(1)}, bf16[64,1792]{1,0:T(8,128)(2,1)S(1)}, u32[]{:S(2)}, u32[]{:S(2)}) collective-permute-start(bf16[64,1792]{1,0:T(8,128)(2,1)S(1)} %get-tuple-element.60), channel_id=1, source_target_pairs={{0,1},{2,3},{1,0},{3,2},{4,5},{6,7},{5,4},{7,6},{8,9},{10,11},{9,8... | collective-permute-start | bytes 688136 | tf_op jit(solution)/shard_map/ppermute | solution.py:99
  126.4 14.8 %collective-permute-start.57 = (bf16[64,1792]{1,0:T(8,128)(2,1)S(1)}, bf16[64,1792]{1,0:T(8,128)(2,1)S(1)}, u32[]{:S(2)}, u32[]{:S(2)}) collective-permute-start(bf16[64,1792]{1,0:T(8,128)(2,1)S(1)} %get-tuple-element.61), channel_id=1, source_target_pairs={{1,2},{2,1},{5,6},{6,5},{9,10},{10,9},{13,14},{14,13},{17,18},{18,... | collective-permute-start | bytes 688136 | tf_op jit(solution)/shard_map/ppermute | solution.py:99
  128.0 20.7 %collective-permute-start.43 = (bf16[64,1920]{1,0:T(8,128)(2,1)S(1)}, bf16[64,1920]{1,0:T(8,128)(2,1)S(1)}, u32[]{:S(2)}, u32[]{:S(2)}) collective-permute-start(bf16[64,1920]{1,0:T(8,128)(2,1)S(1)} %pad.12), channel_id=1, source_target_pairs={{1,2},{2,1},{5,6},{6,5},{9,10},{10,9},{13,14},{14,13},{17,18},{18,... | collective-permute-start | bytes 737288 | tf_op jit(solution)/shard_map/ppermute | solution.py:99
  132.2 8.8 %collective-permute-start.39 = (bf16[128,512]{1,0:T(8,128)(2,1)S(1)}, bf16[128,512]{1,0:T(8,128)(2,1)S(1)}, u32[]{:S(2)}, u32[]{:S(2)}) collective-permute-start(bf16[128,512]{1,0:T(8,128)(2,1)S(1)} %fusion.89), channel_id=1, source_target_pairs={{0,24},{4,28},{8,16},{12,20},{16,8},{20,12},{24,0},{28,4},{1,25},{... | collective-permute-start | bytes 393224 | tf_op jit(solution)/shard_map/ppermute | solution.py:91
  133.7 15.0 %collective-permute-start.47 = (bf16[64,1920]{1,0:T(8,128)(2,1)S(1)}, bf16[64,1920]{1,0:T(8,128)(2,1)S(1)}, u32[]{:S(2)}, u32[]{:S(2)}) collective-permute-start(bf16[64,1920]{1,0:T(8,128)(2,1)S(1)} %pad.12), channel_id=1, source_target_pairs={{0,1},{2,3},{1,0},{3,2},{4,5},{6,7},{5,4},{7,6},{8,9},{10,11},{9,8... | collective-permute-start | bytes 737288 | tf_op jit(solution)/shard_map/ppermute | solution.py:99
  142.0 10.1 %collective-permute-start.62 = (bf16[64,1920]{1,0:T(8,128)(2,1)S(1)}, bf16[64,1920]{1,0:T(8,128)(2,1)S(1)}, u32[]{:S(2)}, u32[]{:S(2)}) collective-permute-start(bf16[64,1920]{1,0:T(8,128)(2,1)S(1)} %pad.13), channel_id=1, source_target_pairs={{0,1},{2,3},{1,0},{3,2},{4,5},{6,7},{5,4},{7,6},{8,9},{10,11},{9,8... | collective-permute-start | bytes 737288 | tf_op jit(solution)/shard_map/ppermute | solution.py:99
  148.9 8.9 %collective-permute-start.44 = (bf16[64,1920]{1,0:T(8,128)(2,1)S(1)}, bf16[64,1920]{1,0:T(8,128)(2,1)S(1)}, u32[]{:S(2)}, u32[]{:S(2)}) collective-permute-start(bf16[64,1920]{1,0:T(8,128)(2,1)S(1)} %get-tuple-element.47), channel_id=1, source_target_pairs={{0,1},{2,3},{1,0},{3,2},{4,5},{6,7},{5,4},{7,6},{8,9},{10,11},{9,8... | collective-permute-start | bytes 737288 | tf_op jit(solution)/shard_map/ppermute | solution.py:99
  149.0 8.8 %collective-permute-start.48 = (bf16[64,1920]{1,0:T(8,128)(2,1)S(1)}, bf16[64,1920]{1,0:T(8,128)(2,1)S(1)}, u32[]{:S(2)}, u32[]{:S(2)}) collective-permute-start(bf16[64,1920]{1,0:T(8,128)(2,1)S(1)} %get-tuple-element.46), channel_id=1, source_target_pairs={{1,2},{2,1},{5,6},{6,5},{9,10},{10,9},{13,14},{14,13},{17,18},{18,... | collective-permute-start | bytes 737288 | tf_op jit(solution)/shard_map/ppermute | solution.py:99
  152.3 13.0 %collective-permute-start.59 = (bf16[64,1920]{1,0:T(8,128)(2,1)S(1)}, bf16[64,1920]{1,0:T(8,128)(2,1)S(1)}, u32[]{:S(2)}, u32[]{:S(2)}) collective-permute-start(bf16[64,1920]{1,0:T(8,128)(2,1)S(1)} %get-tuple-element.52), channel_id=1, source_target_pairs={{0,1},{2,3},{1,0},{3,2},{4,5},{6,7},{5,4},{7,6},{8,9},{10,11},{9,8... | collective-permute-start | bytes 737288 | tf_op jit(solution)/shard_map/ppermute | solution.py:99
  154.7 10.6 %collective-permute-start.63 = (bf16[64,1920]{1,0:T(8,128)(2,1)S(1)}, bf16[64,1920]{1,0:T(8,128)(2,1)S(1)}, u32[]{:S(2)}, u32[]{:S(2)}) collective-permute-start(bf16[64,1920]{1,0:T(8,128)(2,1)S(1)} %get-tuple-element.53), channel_id=1, source_target_pairs={{1,2},{2,1},{5,6},{6,5},{9,10},{10,9},{13,14},{14,13},{17,18},{18,... | collective-permute-start | bytes 737288 | tf_op jit(solution)/shard_map/ppermute | solution.py:99
  157.9 12.6 %collective-permute-start.45 = (bf16[64,1920]{1,0:T(8,128)(2,1)S(1)}, bf16[64,1920]{1,0:T(8,128)(2,1)S(1)}, u32[]{:S(2)}, u32[]{:S(2)}) collective-permute-start(bf16[64,1920]{1,0:T(8,128)(2,1)S(1)} %get-tuple-element.45), channel_id=1, source_target_pairs={{1,2},{2,1},{5,6},{6,5},{9,10},{10,9},{13,14},{14,13},{17,18},{18,... | collective-permute-start | bytes 737288 | tf_op jit(solution)/shard_map/ppermute | solution.py:99
  158.6 11.9 %collective-permute-start.49 = (bf16[64,1920]{1,0:T(8,128)(2,1)S(1)}, bf16[64,1920]{1,0:T(8,128)(2,1)S(1)}, u32[]{:S(2)}, u32[]{:S(2)}) collective-permute-start(bf16[64,1920]{1,0:T(8,128)(2,1)S(1)} %get-tuple-element.44), channel_id=1, source_target_pairs={{0,1},{2,3},{1,0},{3,2},{4,5},{6,7},{5,4},{7,6},{8,9},{10,11},{9,8... | collective-permute-start | bytes 737288 | tf_op jit(solution)/shard_map/ppermute | solution.py:99
  166.1 11.3 %collective-permute-start.64 = (bf16[64,1920]{1,0:T(8,128)(2,1)S(1)}, bf16[64,1920]{1,0:T(8,128)(2,1)S(1)}, u32[]{:S(2)}, u32[]{:S(2)}) collective-permute-start(bf16[64,1920]{1,0:T(8,128)(2,1)S(1)} %get-tuple-element.51), channel_id=1, source_target_pairs={{0,1},{2,3},{1,0},{3,2},{4,5},{6,7},{5,4},{7,6},{8,9},{10,11},{9,8... | collective-permute-start | bytes 737288 | tf_op jit(solution)/shard_map/ppermute | solution.py:99
  170.7 12.0 %collective-permute-start.46 = (bf16[64,1920]{1,0:T(8,128)(2,1)S(1)}, bf16[64,1920]{1,0:T(8,128)(2,1)S(1)}, u32[]{:S(2)}, u32[]{:S(2)}) collective-permute-start(bf16[64,1920]{1,0:T(8,128)(2,1)S(1)} %get-tuple-element.42), channel_id=1, source_target_pairs={{0,1},{2,3},{1,0},{3,2},{4,5},{6,7},{5,4},{7,6},{8,9},{10,11},{9,8... | collective-permute-start | bytes 737288 | tf_op jit(solution)/shard_map/ppermute | solution.py:99
  172.9 9.8 %collective-permute-start.50 = (bf16[64,1920]{1,0:T(8,128)(2,1)S(1)}, bf16[64,1920]{1,0:T(8,128)(2,1)S(1)}, u32[]{:S(2)}, u32[]{:S(2)}) collective-permute-start(bf16[64,1920]{1,0:T(8,128)(2,1)S(1)} %get-tuple-element.43), channel_id=1, source_target_pairs={{1,2},{2,1},{5,6},{6,5},{9,10},{10,9},{13,14},{14,13},{17,18},{18,... | collective-permute-start | bytes 737288 | tf_op jit(solution)/shard_map/ppermute | solution.py:99
  178.3 9.7 %collective-permute-start.61 = (bf16[64,1920]{1,0:T(8,128)(2,1)}, bf16[64,1920]{1,0:T(8,128)(2,1)}, u32[]{:S(2)}, u32[]{:S(2)}) collective-permute-start(bf16[64,1920]{1,0:T(8,128)(2,1)} %get-tuple-element.48), channel_id=1, source_target_pairs={{0,1},{2,3},{1,0},{3,2},{4,5},{6,7},{5,4},{7,6},{8,9},{10,11},{9,8... | collective-permute-start | bytes 737288 | tf_op jit(solution)/shard_map/ppermute | solution.py:99
  183.2 9.9 %collective-permute-start.51 = (bf16[64,1920]{1,0:T(8,128)(2,1)S(1)}, bf16[64,1920]{1,0:T(8,128)(2,1)S(1)}, u32[]{:S(2)}, u32[]{:S(2)}) collective-permute-start(bf16[64,1920]{1,0:T(8,128)(2,1)S(1)} %concatenate.97), channel_id=1, source_target_pairs={{0,1},{2,3},{1,0},{3,2},{4,5},{6,7},{5,4},{7,6},{8,9},{10,11},{9,8... | collective-permute-start | bytes 737288 | tf_op jit(solution)/shard_map/ppermute | solution.py:99
  185.3 21.4 %collective-permute-start.54 = (bf16[64,1920]{1,0:T(8,128)(2,1)S(1)}, bf16[64,1920]{1,0:T(8,128)(2,1)}, u32[]{:S(2)}, u32[]{:S(2)}) collective-permute-start(bf16[64,1920]{1,0:T(8,128)(2,1)S(1)} %concatenate.97), channel_id=1, source_target_pairs={{1,2},{2,1},{5,6},{6,5},{9,10},{10,9},{13,14},{14,13},{17,18},{18,... | collective-permute-start | bytes 737288 | tf_op jit(solution)/shard_map/ppermute | solution.py:99
  191.7 15.1 %collective-permute-start.69 = (bf16[64,1920]{1,0:T(8,128)(2,1)S(1)}, bf16[64,1920]{1,0:T(8,128)(2,1)S(1)}, u32[]{:S(2)}, u32[]{:S(2)}) collective-permute-start(bf16[64,1920]{1,0:T(8,128)(2,1)S(1)} %concatenate.99), channel_id=1, source_target_pairs={{1,2},{2,1},{5,6},{6,5},{9,10},{10,9},{13,14},{14,13},{17,18},{18,... | collective-permute-start | bytes 737288 | tf_op jit(solution)/shard_map/ppermute | solution.py:99
  195.9 12.9 %collective-permute-start.67 = (bf16[64,1920]{1,0:T(8,128)(2,1)S(1)}, bf16[64,1920]{1,0:T(8,128)(2,1)S(1)}, u32[]{:S(2)}, u32[]{:S(2)}) collective-permute-start(bf16[64,1920]{1,0:T(8,128)(2,1)S(1)} %collective-permute-done.66), channel_id=1, source_target_pairs={{1,2},{2,1},{5,6},{6,5},{9,10},{10,9},{13,14},{14,13},{17,18},{18,... | collective-permute-start | bytes 737288 | tf_op jit(solution)/shard_map/ppermute | solution.py:99
  196.8 16.6 %collective-permute-start.53 = (bf16[64,1920]{1,0:T(8,128)(2,1)S(1)}, bf16[64,1920]{1,0:T(8,128)(2,1)S(1)}, u32[]{:S(2)}, u32[]{:S(2)}) collective-permute-start(bf16[64,1920]{1,0:T(8,128)(2,1)S(1)} %collective-permute-done.52), channel_id=1, source_target_pairs={{0,1},{2,3},{1,0},{3,2},{4,5},{6,7},{5,4},{7,6},{8,9},{10,11},{9,8... | collective-permute-start | bytes 737288 | tf_op jit(solution)/shard_map/ppermute | solution.py:99
  206.7 10.1 %collective-permute-start.55 = (bf16[64,1920]{1,0:T(8,128)(2,1)}, bf16[64,1920]{1,0:T(8,128)(2,1)S(1)}, u32[]{:S(2)}, u32[]{:S(2)}) collective-permute-start(bf16[64,1920]{1,0:T(8,128)(2,1)} %collective-permute-done.54), channel_id=1, source_target_pairs={{0,1},{2,3},{1,0},{3,2},{4,5},{6,7},{5,4},{7,6},{8,9},{10,11},{9,8... | collective-permute-start | bytes 737288 | tf_op jit(solution)/shard_map/ppermute | solution.py:99
  206.8 15.4 %collective-permute-start.70 = (bf16[64,1920]{1,0:T(8,128)(2,1)S(1)}, bf16[64,1920]{1,0:T(8,128)(2,1)S(1)}, u32[]{:S(2)}, u32[]{:S(2)}) collective-permute-start(bf16[64,1920]{1,0:T(8,128)(2,1)S(1)} %collective-permute-done.69), channel_id=1, source_target_pairs={{0,1},{2,3},{1,0},{3,2},{4,5},{6,7},{5,4},{7,6},{8,9},{10,11},{9,8... | collective-permute-start | bytes 737288 | tf_op jit(solution)/shard_map/ppermute | solution.py:99
  208.8 13.3 %collective-permute-start.68 = (bf16[64,1920]{1,0:T(8,128)(2,1)S(1)}, bf16[64,1920]{1,0:T(8,128)(2,1)S(1)}, u32[]{:S(2)}, u32[]{:S(2)}) collective-permute-start(bf16[64,1920]{1,0:T(8,128)(2,1)S(1)} %collective-permute-done.67), channel_id=1, source_target_pairs={{0,1},{2,3},{1,0},{3,2},{4,5},{6,7},{5,4},{7,6},{8,9},{10,11},{9,8... | collective-permute-start | bytes 737288 | tf_op jit(solution)/shard_map/ppermute | solution.py:99
  229.3 9.1 %collective-permute-start.76 = (bf16[512,640]{1,0:T(8,128)(2,1)S(1)}, bf16[512,640]{1,0:T(8,128)(2,1)S(1)}, u32[]{:S(2)}, u32[]{:S(2)}) collective-permute-start(bf16[512,640]{1,0:T(8,128)(2,1)S(1)} %pad_maximum_fusion.4), channel_id=1, source_target_pairs={{0,4},{4,0},{8,12},{12,8},{16,20},{20,16},{24,28},{28,24},{1,5},{5... | collective-permute-start | bytes 1966088 | tf_op jit(solution)/shard_map/ppermute | solution.py:88
  242.3 12.3 %collective-permute-start.75 = (bf16[128,512]{1,0:T(8,128)(2,1)S(1)}, bf16[128,512]{1,0:T(8,128)(2,1)S(1)}, u32[]{:S(2)}, u32[]{:S(2)}) collective-permute-start(bf16[128,512]{1,0:T(8,128)(2,1)S(1)} %fusion.79), channel_id=1, source_target_pairs={{0,0},{1,8},{2,16},{3,24},{4,4},{5,12},{6,20},{7,28},{8,1},{9,9},{... | collective-permute-start | bytes 393224 | tf_op jit(solution)/shard_map/ppermute | solution.py:85
  (49 other events, 448.8 us)
where the time goes:
time: 274 us; the launch traced here: 270 us
  starting transfers between devices  139 us (51%)
  waiting for transfers between devices  77.8 us (28%)
  matrix products  20.1 us (7%)
  other arithmetic  18.7 us (7%)
  Pallas kernels  6.77 us (2%)
  local copies, waits for them, and re-layouts  5.18 us (2%)
    ppermute x52, starting transfers between devices, pair_swap(): return lax.ppermute(block, 'local', pairs + [(t, s) for s, t in pairs])  103 us
    ppermute x52, waiting for transfers between devices, pair_swap(): return lax.ppermute(block, 'local', pairs + [(t, s) for s, t in pairs])  40.5 us
    ppermute x21, waiting for transfers between devices, chip_swap(): lax.ppermute(block, 'node', [(n, n ^ 2 * shift) for n in range(n_node)])  24.5 us
    ppermute x21, starting transfers between devices, chip_swap(): lax.ppermute(block, 'node', [(n, n ^ 2 * shift) for n in range(n_node)])  23.2 us
    dot_general x13, matrix products, dot(): lax.dot_general(left, right, (dims, ((), ())), preferred_element_type=F32)  20.1 us
    ppermute x3, starting transfers between devices, exchange(): return lax.ppermute(block, ('node', 'local'), swap)  11.7 us
    ppermute x3, waiting for transfers between devices, exchange(): return lax.ppermute(block, ('node', 'local'), swap)  9.99 us
    pallas_call x1, Pallas kernels, dequant_cols(): pl.pallas_call(scale_columns, grid=(rows // tile,), in_specs=[pl.BlockSpe...  6.77 us
  transfers between devices with their start and end apart: 84, of which 32 were waited for; matrix products, arithmetic and copies ran while one was open for 10% of the time, Pallas kernels for 3%

commit v1 on v0

--- a/solution.py
+++ b/solution.py
@@ -179,6 +179,8 @@
                     adds = jnp.where(even, adds_left, adds_right)
                     to_second = jnp.where(adds, to_second.astype(F32), zero)
                     to_second = (first.astype(F32) + to_second).astype(BF16)
+            if first is not None and step == (2 if block is None else last - 1 if partial is None else 0):
+                to_first = after(to_first, first)
             used = None
             if block is None:
                 used = lambda s, step=step: s < step or s + 1 > last - step

time: 274 us -> 272 us (level)
  waiting for transfers between devices: 77.8 us -> 66.5 us
  starting transfers between devices: 139 us -> 148 us
    ppermute x52, waiting for transfers between devices: 40.5 us -> 22.3 us  [pair_swap(): return lax.ppermute(block, 'local', pairs + [(t, s) for s, t in pairs])]
    ppermute x52, starting transfers between devices: 103 us -> 113 us  [pair_swap(): return lax.ppermute(block, 'local', pairs + [(t, s) for s, t in pairs])]
    ppermute x21, waiting for transfers between devices: 24.5 us -> 31.4 us  [chip_swap(): lax.ppermute(block, 'node', [(n, n ^ 2 * shift) for n in range(n_node)])]
where the time goes in v1:
time: 272 us; the launch traced here: 268 us
  starting transfers between devices  148 us (54%)
  waiting for transfers between devices  66.5 us (24%)
  matrix products  20.1 us (7%)
  other arithmetic  19.7 us (7%)
  Pallas kernels  6.77 us (2%)
  local copies, waits for them, and re-layouts  5.18 us (2%)
    ppermute x52, starting transfers between devices, pair_swap(): return lax.ppermute(block, 'local', pairs + [(t, s) for s, t in pairs])  113 us
    ppermute x21, waiting for transfers between devices, chip_swap(): lax.ppermute(block, 'node', [(n, n ^ 2 * shift) for n in range(n_node)])  31.4 us
    ppermute x21, starting transfers between devices, chip_swap(): lax.ppermute(block, 'node', [(n, n ^ 2 * shift) for n in range(n_node)])  23 us
    ppermute x52, waiting for transfers between devices, pair_swap(): return lax.ppermute(block, 'local', pairs + [(t, s) for s, t in pairs])  22.3 us
    dot_general x13, matrix products, dot(): lax.dot_general(left, right, (dims, ((), ())), preferred_element_type=F32)  20.1 us
    ppermute x3, starting transfers between devices, exchange(): return lax.ppermute(block, ('node', 'local'), swap)  11.2 us
    ppermute x3, waiting for transfers between devices, exchange(): return lax.ppermute(block, ('node', 'local'), swap)  9.33 us
    pallas_call x1, Pallas kernels, dequant_cols(): pl.pallas_call(scale_columns, grid=(rows // tile,), in_specs=[pl.BlockSpe...  6.77 us
  transfers between devices with their start and end apart: 84, of which 32 were waited for; matrix products, arithmetic and copies ran while one was open for 10% of the time, Pallas kernels for 3%

profile of v1, /device:TPU:2, one launch (start us, length us, event | category | flops | bytes accessed | tf_op | source)
XLA Modules:
  0.0 268.5 jit_solution(14655969297476754112)
XLA Ops:
  0.6 3.5 %collective-permute-start = (bf16[128,512]{1,0:T(8,128)(2,1)}, bf16[128,512]{1,0:T(8,128)(2,1)S(1)}, u32[]{:S(2)}, u32[]{:S(2)}) collective-permute-start(bf16[128,512]{1,0:T(8,128)(2,1)} %param.7), channel_id=1, source_target_pairs={{0,0},{1,8},{2,16},{3,24},{4,4},{5,12},{6,20},{7,28},{8,1},{9,9},{... | collective-permute-start | bytes 393224 | tf_op jit(solution)/shard_map/ppermute | solution.py:85
  5.0 3.3 %collective-permute-start.4 = (bf16[144,512]{1,0:T(8,128)(2,1)S(1)}, bf16[144,512]{1,0:T(8,128)(2,1)S(1)}, u32[]{:S(2)}, u32[]{:S(2)}) collective-permute-start(bf16[144,512]{1,0:T(8,128)(2,1)S(1)} %fusion.92), channel_id=1, source_target_pairs={{0,0},{1,8},{2,16},{3,24},{4,4},{5,12},{6,20},{7,28},{8,1},{9,9},{... | collective-permute-start | bytes 442376 | tf_op jit(solution)/shard_map/ppermute | solution.py:85
  10.0 6.8 %shard_map.86 = bf16[1792,1024]{1,0:T(8,128)(2,1)} custom-call(bf16[1792,1024]{1,0:T(8,128)(2,1)} %quanta_ref.1, bf16[1792,8]{1,0:T(8,128)(2,1)} %copy.26.scales_ref), custom_call_target="tpu_custom_call" | custom-call | flops 1835008 | bytes 7340032 | tf_op jit(solution)/shard_map/pallas_call | solution.py:34
  16.8 5.0 %collective-permute-done = bf16[128,512]{1,0:T(8,128)(2,1)S(1)} collective-permute-done((bf16[128,512]{1,0:T(8,128)(2,1)}, bf16[128,512]{1,0:T(8,128)(2,1)S(1)}, u32[]{:S(2)}, u32[]{:S(2)}) %collective-permute-start) | collective-permute-done | bytes 131104 | tf_op jit(solution)/shard_map/ppermute | solution.py:85
  21.9 3.5 %collective-permute-start.3 = (bf16[128,512]{1,0:T(8,128)(2,1)S(1)}, bf16[128,512]{1,0:T(8,128)(2,1)S(1)}, u32[]{:S(2)}, u32[]{:S(2)}) collective-permute-start(bf16[128,512]{1,0:T(8,128)(2,1)S(1)} %collective-permute-done), channel_id=1, source_target_pairs={{0,24},{4,28},{8,16},{12,20},{16,8},{20,12},{24,0},{28,4},{1,25},{... | collective-permute-start | bytes 393224 | tf_op jit(solution)/shard_map/ppermute | solution.py:91
  25.4 2.7 %collective-permute-done.1 = bf16[128,512]{1,0:T(8,128)(2,1)S(1)} collective-permute-done((bf16[128,512]{1,0:T(8,128)(2,1)S(1)}, bf16[128,512]{1,0:T(8,128)(2,1)S(1)}, u32[]{:S(2)}, u32[]{:S(2)}) %collective-permute-start.1) | collective-permute-done | bytes 131104 | tf_op jit(solution)/shard_map/ppermute | solution.py:91
  29.3 2.7 %fusion = bf16[1024,1792]{1,0:T(8,128)(2,1)S(1)} fusion(bf16[1024,1792]{1,0:T(8,128)(2,1)} %param.10, f32[8,1792]{1,0:T(8,128)S(1)} %convert_element_type.736), kind=kLoop, calls=%fused_computation.1 | loop fusion | flops 5505024 | bytes 7397376 | tf_op jit(solution)/shard_map/convert_element_type | solution.py:19
  39.4 2.0 collective-permute-start.7
  41.6 2.4 collective-permute-done.14
  45.5 2.8 %collective-permute-done.22 = bf16[64,1920]{1,0:T(8,128)(2,1)S(1)} collective-permute-done((bf16[64,1920]{1,0:T(8,128)(2,1)S(1)}, bf16[64,1920]{1,0:T(8,128)(2,1)S(1)}, u32[]{:S(2)}, u32[]{:S(2)}) %collective-permute-start.22) | collective-permute-done | bytes 245792 | tf_op jit(solution)/shard_map/ppermute | solution.py:99
  49.1 4.7 %collective-permute-start.25 = (bf16[64,1920]{1,0:T(8,128)(2,1)S(1)}, bf16[64,1920]{1,0:T(8,128)(2,1)S(1)}, u32[]{:S(2)}, u32[]{:S(2)}) collective-permute-start(bf16[64,1920]{1,0:T(8,128)(2,1)S(1)} %fusion.91), channel_id=1, source_target_pairs={{0,1},{2,3},{1,0},{3,2},{4,5},{6,7},{5,4},{7,6},{8,9},{10,11},{9,8... | collective-permute-start | bytes 737288 | tf_op jit(solution)/shard_map/ppermute | solution.py:99
  54.5 4.5 %collective-permute-start.10 = (bf16[64,1920]{1,0:T(8,128)(2,1)S(1)}, bf16[64,1920]{1,0:T(8,128)(2,1)S(1)}, u32[]{:S(2)}, u32[]{:S(2)}) collective-permute-start(bf16[64,1920]{1,0:T(8,128)(2,1)S(1)} %fusion.90), channel_id=1, source_target_pairs={{0,1},{2,3},{1,0},{3,2},{4,5},{6,7},{5,4},{7,6},{8,9},{10,11},{9,8... | collective-permute-start | bytes 737288 | tf_op jit(solution)/shard_map/ppermute | solution.py:99
  60.1 5.0 %collective-permute-start.24 = (bf16[64,1920]{1,0:T(8,128)(2,1)S(1)}, bf16[64,1920]{1,0:T(8,128)(2,1)S(1)}, u32[]{:S(2)}, u32[]{:S(2)}) collective-permute-start(bf16[64,1920]{1,0:T(8,128)(2,1)S(1)} %get-tuple-element.64), channel_id=1, source_target_pairs={{0,1},{2,3},{1,0},{3,2},{4,5},{6,7},{5,4},{7,6},{8,9},{10,11},{9,8... | collective-permute-start | bytes 737288 | tf_op jit(solution)/shard_map/ppermute | solution.py:99
  65.9 4.2 %collective-permute-start.9 = (bf16[64,1920]{1,0:T(8,128)(2,1)S(1)}, bf16[64,1920]{1,0:T(8,128)(2,1)S(1)}, u32[]{:S(2)}, u32[]{:S(2)}) collective-permute-start(bf16[64,1920]{1,0:T(8,128)(2,1)S(1)} %get-tuple-element.62), channel_id=1, source_target_pairs={{0,1},{2,3},{1,0},{3,2},{4,5},{6,7},{5,4},{7,6},{8,9},{10,11},{9,8... | collective-permute-start | bytes 737288 | tf_op jit(solution)/shard_map/ppermute | solution.py:99
  77.4 2.3 collective-permute-start.19
  82.7 6.0 %collective-permute-start.28 = (bf16[64,1792]{1,0:T(8,128)(2,1)S(1)}, bf16[64,1792]{1,0:T(8,128)(2,1)S(1)}, u32[]{:S(2)}, u32[]{:S(2)}) collective-permute-start(bf16[64,1792]{1,0:T(8,128)(2,1)S(1)} %get-tuple-element.77), channel_id=1, source_target_pairs={{0,1},{2,3},{1,0},{3,2},{4,5},{6,7},{5,4},{7,6},{8,9},{10,11},{9,8... | collective-permute-start | bytes 688136 | tf_op jit(solution)/shard_map/ppermute | solution.py:99
  89.6 4.1 %collective-permute-start.17 = (bf16[64,1792]{1,0:T(8,128)(2,1)S(1)}, bf16[64,1792]{1,0:T(8,128)(2,1)S(1)}, u32[]{:S(2)}, u32[]{:S(2)}) collective-permute-start(bf16[64,1792]{1,0:T(8,128)(2,1)S(1)} %get-tuple-element.73), channel_id=1, source_target_pairs={{0,1},{2,3},{1,0},{3,2},{4,5},{6,7},{5,4},{7,6},{8,9},{10,11},{9,8... | collective-permute-start | bytes 688136 | tf_op jit(solution)/shard_map/ppermute | solution.py:99
  94.5 4.2 %collective-permute-start.32 = (bf16[64,1792]{1,0:T(8,128)(2,1)S(1)}, bf16[64,1792]{1,0:T(8,128)(2,1)S(1)}, u32[]{:S(2)}, u32[]{:S(2)}) collective-permute-start(bf16[64,1792]{1,0:T(8,128)(2,1)S(1)} %get-tuple-element.74), channel_id=1, source_target_pairs={{0,1},{2,3},{1,0},{3,2},{4,5},{6,7},{5,4},{7,6},{8,9},{10,11},{9,8... | collective-permute-start | bytes 688136 | tf_op jit(solution)/shard_map/ppermute | solution.py:99
  100.1 4.3 %collective-permute-start.21 = (bf16[64,1792]{1,0:T(8,128)(2,1)S(1)}, bf16[64,1792]{1,0:T(8,128)(2,1)S(1)}, u32[]{:S(2)}, u32[]{:S(2)}) collective-permute-start(bf16[64,1792]{1,0:T(8,128)(2,1)S(1)} %get-tuple-element.70), channel_id=1, source_target_pairs={{0,1},{2,3},{1,0},{3,2},{4,5},{6,7},{5,4},{7,6},{8,9},{10,11},{9,8... | collective-permute-start | bytes 688136 | tf_op jit(solution)/shard_map/ppermute | solution.py:99
  106.0 2.4 collective-permute-done.21
  111.0 4.0 %collective-permute-start.56 = (bf16[64,1792]{1,0:T(8,128)(2,1)S(1)}, bf16[64,1792]{1,0:T(8,128)(2,1)S(1)}, u32[]{:S(2)}, u32[]{:S(2)}) collective-permute-start(bf16[64,1792]{1,0:T(8,128)(2,1)S(1)} %get-tuple-element.68), channel_id=1, source_target_pairs={{0,1},{2,3},{1,0},{3,2},{4,5},{6,7},{5,4},{7,6},{8,9},{10,11},{9,8... | collective-permute-start | bytes 688136 | tf_op jit(solution)/shard_map/ppermute | solution.py:99
  116.0 2.3 collective-permute-start.35
  119.0 3.6 %collective-permute-done.36 = bf16[128,512]{1,0:T(8,128)(2,1)S(1)} collective-permute-done((bf16[128,512]{1,0:T(8,128)(2,1)S(1)}, bf16[128,512]{1,0:T(8,128)(2,1)S(1)}, u32[]{:S(2)}, u32[]{:S(2)}) %collective-permute-start.36) | collective-permute-done | bytes 131104 | tf_op jit(solution)/shard_map/ppermute | solution.py:91
  128.4 2.7 collective-permute-done.37
  131.2 3.6 %collective-permute-done.38 = bf16[128,512]{1,0:T(8,128)(2,1)S(1)} collective-permute-done((bf16[128,512]{1,0:T(8,128)(2,1)S(1)}, bf16[128,512]{1,0:T(8,128)(2,1)S(1)}, u32[]{:S(2)}, u32[]{:S(2)}) %collective-permute-start.38) | collective-permute-done | bytes 131104 | tf_op jit(solution)/shard_map/ppermute | solution.py:91
  134.7 3.5 %collective-permute-start.62 = (bf16[64,1920]{1,0:T(8,128)(2,1)S(1)}, bf16[64,1920]{1,0:T(8,128)(2,1)S(1)}, u32[]{:S(2)}, u32[]{:S(2)}) collective-permute-start(bf16[64,1920]{1,0:T(8,128)(2,1)S(1)} %pad.13), channel_id=1, source_target_pairs={{0,1},{2,3},{1,0},{3,2},{4,5},{6,7},{5,4},{7,6},{8,9},{10,11},{9,8... | collective-permute-start | bytes 737288 | tf_op jit(solution)/shard_map/ppermute | solution.py:99
  144.6 2.5 collective-permute-start.59
  148.8 4.8 %collective-permute-start.44 = (bf16[64,1920]{1,0:T(8,128)(2,1)S(1)}, bf16[64,1920]{1,0:T(8,128)(2,1)S(1)}, u32[]{:S(2)}, u32[]{:S(2)}) collective-permute-start(bf16[64,1920]{1,0:T(8,128)(2,1)S(1)} %get-tuple-element.55), channel_id=1, source_target_pairs={{0,1},{2,3},{1,0},{3,2},{4,5},{6,7},{5,4},{7,6},{8,9},{10,11},{9,8... | collective-permute-start | bytes 737288 | tf_op jit(solution)/shard_map/ppermute | solution.py:99
  154.5 6.5 %collective-permute-start.64 = (bf16[64,1920]{1,0:T(8,128)(2,1)S(1)}, bf16[64,1920]{1,0:T(8,128)(2,1)S(1)}, u32[]{:S(2)}, u32[]{:S(2)}) collective-permute-start(bf16[64,1920]{1,0:T(8,128)(2,1)S(1)} %get-tuple-element.59), channel_id=1, source_target_pairs={{0,1},{2,3},{1,0},{3,2},{4,5},{6,7},{5,4},{7,6},{8,9},{10,11},{9,8... | collective-permute-start | bytes 737288 | tf_op jit(solution)/shard_map/ppermute | solution.py:99
  161.9 4.4 %collective-permute-start.49 = (bf16[64,1920]{1,0:T(8,128)(2,1)S(1)}, bf16[64,1920]{1,0:T(8,128)(2,1)S(1)}, u32[]{:S(2)}, u32[]{:S(2)}) collective-permute-start(bf16[64,1920]{1,0:T(8,128)(2,1)S(1)} %get-tuple-element.52), channel_id=1, source_target_pairs={{0,1},{2,3},{1,0},{3,2},{4,5},{6,7},{5,4},{7,6},{8,9},{10,11},{9,8... | collective-permute-start | bytes 737288 | tf_op jit(solution)/shard_map/ppermute | solution.py:99
  168.6 4.1 %collective-permute-start.61 = (bf16[64,1920]{1,0:T(8,128)(2,1)}, bf16[64,1920]{1,0:T(8,128)(2,1)}, u32[]{:S(2)}, u32[]{:S(2)}) collective-permute-start(bf16[64,1920]{1,0:T(8,128)(2,1)} %get-tuple-element.56), channel_id=1, source_target_pairs={{0,1},{2,3},{1,0},{3,2},{4,5},{6,7},{5,4},{7,6},{8,9},{10,11},{9,8... | collective-permute-start | bytes 737288 | tf_op jit(solution)/shard_map/ppermute | solution.py:99
  173.6 3.0 %collective-permute-start.46 = (bf16[64,1920]{1,0:T(8,128)(2,1)S(1)}, bf16[64,1920]{1,0:T(8,128)(2,1)S(1)}, u32[]{:S(2)}, u32[]{:S(2)}) collective-permute-start(bf16[64,1920]{1,0:T(8,128)(2,1)S(1)} %get-tuple-element.50), channel_id=1, source_target_pairs={{0,1},{2,3},{1,0},{3,2},{4,5},{6,7},{5,4},{7,6},{8,9},{10,11},{9,8... | collective-permute-start | bytes 737288 | tf_op jit(solution)/shard_map/ppermute | solution.py:99
  177.6 4.9 %collective-permute-done.46 = bf16[64,1920]{1,0:T(8,128)(2,1)S(1)} collective-permute-done((bf16[64,1920]{1,0:T(8,128)(2,1)S(1)}, bf16[64,1920]{1,0:T(8,128)(2,1)S(1)}, u32[]{:S(2)}, u32[]{:S(2)}) %collective-permute-start.46) | collective-permute-done | bytes 245792 | tf_op jit(solution)/shard_map/ppermute | solution.py:99
  183.0 1.9 collective-permute-start.51
  191.6 4.4 %collective-permute-start.54 = (bf16[64,1920]{1,0:T(8,128)(2,1)}, bf16[64,1920]{1,0:T(8,128)(2,1)S(1)}, u32[]{:S(2)}, u32[]{:S(2)}) collective-permute-start(bf16[64,1920]{1,0:T(8,128)(2,1)} %collective-permute-done.53), channel_id=1, source_target_pairs={{0,1},{2,3},{1,0},{3,2},{4,5},{6,7},{5,4},{7,6},{8,9},{10,11},{9,8... | collective-permute-start | bytes 737288 | tf_op jit(solution)/shard_map/ppermute | solution.py:99
  197.1 3.7 %collective-permute-start.69 = (bf16[64,1920]{1,0:T(8,128)(2,1)S(1)}, bf16[64,1920]{1,0:T(8,128)(2,1)S(1)}, u32[]{:S(2)}, u32[]{:S(2)}) collective-permute-start(bf16[64,1920]{1,0:T(8,128)(2,1)S(1)} %collective-permute-done.68), channel_id=1, source_target_pairs={{0,1},{2,3},{1,0},{3,2},{4,5},{6,7},{5,4},{7,6},{8,9},{10,11},{9,8... | collective-permute-start | bytes 737288 | tf_op jit(solution)/shard_map/ppermute | solution.py:99
  200.8 1.9 collective-permute-done.54
  202.7 3.3 %collective-permute-start.55 = (bf16[64,1920]{1,0:T(8,128)(2,1)S(1)}, bf16[64,1920]{1,0:T(8,128)(2,1)S(1)}, u32[]{:S(2)}, u32[]{:S(2)}) collective-permute-start(bf16[64,1920]{1,0:T(8,128)(2,1)S(1)} %collective-permute-done.52), channel_id=1, source_target_pairs={{0,1},{2,3},{1,0},{3,2},{4,5},{6,7},{5,4},{7,6},{8,9},{10,11},{9,8... | collective-permute-start | bytes 737288 | tf_op jit(solution)/shard_map/ppermute | solution.py:99
  208.0 2.3 collective-permute-start.70
  210.2 3.0 %collective-permute-done.55 = bf16[64,1920]{1,0:T(8,128)(2,1)S(1)} collective-permute-done((bf16[64,1920]{1,0:T(8,128)(2,1)S(1)}, bf16[64,1920]{1,0:T(8,128)(2,1)S(1)}, u32[]{:S(2)}, u32[]{:S(2)}) %collective-permute-start.55) | collective-permute-done | bytes 245792 | tf_op jit(solution)/shard_map/ppermute | solution.py:99
  229.8 3.7 %collective-permute-done.74 = bf16[128,512]{1,0:T(8,128)(2,1)S(1)} collective-permute-done((bf16[128,512]{1,0:T(8,128)(2,1)S(1)}, bf16[128,512]{1,0:T(8,128)(2,1)S(1)}, u32[]{:S(2)}, u32[]{:S(2)}) %collective-permute-start.74) | collective-permute-done | bytes 131104 | tf_op jit(solution)/shard_map/ppermute | solution.py:91
  233.6 2.2 collective-permute-done.73
  239.8 4.4 %collective-permute-start.75 = (bf16[128,512]{1,0:T(8,128)(2,1)S(1)}, bf16[128,512]{1,0:T(8,128)(2,1)S(1)}, u32[]{:S(2)}, u32[]{:S(2)}) collective-permute-start(bf16[128,512]{1,0:T(8,128)(2,1)S(1)} %fusion.79), channel_id=1, source_target_pairs={{0,0},{1,8},{2,16},{3,24},{4,4},{5,12},{6,20},{7,28},{8,1},{9,9},{... | collective-permute-start | bytes 393224 | tf_op jit(solution)/shard_map/ppermute | solution.py:85
  244.3 2.5 collective-permute-done.78
  248.6 4.3 %collective-permute-done.75 = bf16[128,512]{1,0:T(8,128)(2,1)S(1)} collective-permute-done((bf16[128,512]{1,0:T(8,128)(2,1)S(1)}, bf16[128,512]{1,0:T(8,128)(2,1)S(1)}, u32[]{:S(2)}, u32[]{:S(2)}) %collective-permute-start.75) | collective-permute-done | bytes 131104 | tf_op jit(solution)/shard_map/ppermute | solution.py:85
  253.2 3.1 %collective-permute-start.82 = (bf16[128,512]{1,0:T(8,128)(2,1)S(1)}, bf16[128,512]{1,0:T(8,128)(2,1)S(1)}, u32[]{:S(2)}, u32[]{:S(2)}) collective-permute-start(bf16[128,512]{1,0:T(8,128)(2,1)S(1)} %fusion.82), channel_id=1, source_target_pairs={{0,24},{4,28},{8,16},{12,20},{16,8},{20,12},{24,0},{28,4},{1,25},{... | collective-permute-start | bytes 393224 | tf_op jit(solution)/shard_map/ppermute | solution.py:91
  256.4 2.2 collective-permute-done.80
  262.3 5.5 %convolution_convert_fusion = bf16[1792,1024]{1,0:T(8,128)(2,1)} fusion(bf16[256,1792]{1,0:T(8,128)(2,1)S(1)} %get-tuple-element.49, bf16[256,1792]{1,0:T(8,128)(2,1)S(1)} %get-tuple-element.47, bf16[256,1792]{1,0:T(8,128)(2,1)S(1)} %bitcast.355, bf16[256,1792]{1,0:T(8,128)(2,1)S(1)} %bitcast.357, bf16[512,1024]{1,0:T(8,128)(2,1)S(1)} %copy-done.5, ...), kind=kOutput, calls=%fused_computation.2 | convolution fusion | flops 3778805760 | bytes 9437184 | tf_op jit(solution)/shard_map/dot_general | solution.py:50
  (307 shorter events, 91.5 us)
Async XLA Ops:
  0.6 21.2 %collective-permute-start = (bf16[128,512]{1,0:T(8,128)(2,1)}, bf16[128,512]{1,0:T(8,128)(2,1)S(1)}, u32[]{:S(2)}, u32[]{:S(2)}) collective-permute-start(bf16[128,512]{1,0:T(8,128)(2,1)} %param.7), channel_id=1, source_target_pairs={{0,0},{1,8},{2,16},{3,24},{4,4},{5,12},{6,20},{7,28},{8,1},{9,9},{... | collective-permute-start | bytes 393224 | tf_op jit(solution)/shard_map/ppermute | solution.py:85
  5.0 20.4 %collective-permute-start.4 = (bf16[144,512]{1,0:T(8,128)(2,1)S(1)}, bf16[144,512]{1,0:T(8,128)(2,1)S(1)}, u32[]{:S(2)}, u32[]{:S(2)}) collective-permute-start(bf16[144,512]{1,0:T(8,128)(2,1)S(1)} %fusion.92), channel_id=1, source_target_pairs={{0,0},{1,8},{2,16},{3,24},{4,4},{5,12},{6,20},{7,28},{8,1},{9,9},{... | collective-permute-start | bytes 442376 | tf_op jit(solution)/shard_map/ppermute | solution.py:85
  39.4 9.0 %collective-permute-start.22 = (bf16[64,1920]{1,0:T(8,128)(2,1)S(1)}, bf16[64,1920]{1,0:T(8,128)(2,1)S(1)}, u32[]{:S(2)}, u32[]{:S(2)}) collective-permute-start(bf16[64,1920]{1,0:T(8,128)(2,1)S(1)} %dynamic-slice_bitcast_fusion), channel_id=1, source_target_pairs={{0,1},{2,3},{1,0},{3,2},{4,5},{6,7},{5,4},{7,6},{8,9},{10,11},{9,8... | collective-permute-start | bytes 737288 | tf_op jit(solution)/shard_map/ppermute | solution.py:99
  39.4 14.3 %collective-permute-start.7 = (bf16[64,1920]{1,0:T(8,128)(2,1)S(1)}, bf16[64,1920]{1,0:T(8,128)(2,1)S(1)}, u32[]{:S(2)}, u32[]{:S(2)}) collective-permute-start(bf16[64,1920]{1,0:T(8,128)(2,1)S(1)} %dynamic-slice_bitcast_fusion.1), channel_id=1, source_target_pairs={{0,1},{2,3},{1,0},{3,2},{4,5},{6,7},{5,4},{7,6},{8,9},{10,11},{9,8... | collective-permute-start | bytes 737288 | tf_op jit(solution)/shard_map/ppermute | solution.py:99
  45.5 24.6 %collective-permute-start.16 = (bf16[512,512]{1,0:T(8,128)(2,1)S(1)}, bf16[512,512]{1,0:T(8,128)(2,1)S(1)}, u32[]{:S(2)}, u32[]{:S(2)}) collective-permute-start(bf16[512,512]{1,0:T(8,128)(2,1)S(1)} %bitcast.349), channel_id=1, source_target_pairs={{0,4},{4,0},{8,12},{12,8},{16,20},{20,16},{24,28},{28,24},{1,5},{5... | collective-permute-start | bytes 1572872 | tf_op jit(solution)/shard_map/ppermute | solution.py:88
  48.4 10.6 %collective-permute-start.23 = (bf16[64,1920]{1,0:T(8,128)(2,1)S(1)}, bf16[64,1920]{1,0:T(8,128)(2,1)S(1)}, u32[]{:S(2)}, u32[]{:S(2)}) collective-permute-start(bf16[64,1920]{1,0:T(8,128)(2,1)S(1)} %fusion.54), channel_id=1, source_target_pairs={{1,2},{2,1},{5,6},{6,5},{9,10},{10,9},{13,14},{14,13},{17,18},{18,... | collective-permute-start | bytes 737288 | tf_op jit(solution)/shard_map/ppermute | solution.py:99
  49.1 10.0 %collective-permute-start.25 = (bf16[64,1920]{1,0:T(8,128)(2,1)S(1)}, bf16[64,1920]{1,0:T(8,128)(2,1)S(1)}, u32[]{:S(2)}, u32[]{:S(2)}) collective-permute-start(bf16[64,1920]{1,0:T(8,128)(2,1)S(1)} %fusion.91), channel_id=1, source_target_pairs={{0,1},{2,3},{1,0},{3,2},{4,5},{6,7},{5,4},{7,6},{8,9},{10,11},{9,8... | collective-permute-start | bytes 737288 | tf_op jit(solution)/shard_map/ppermute | solution.py:99
  53.9 11.2 %collective-permute-start.8 = (bf16[64,1920]{1,0:T(8,128)(2,1)S(1)}, bf16[64,1920]{1,0:T(8,128)(2,1)S(1)}, u32[]{:S(2)}, u32[]{:S(2)}) collective-permute-start(bf16[64,1920]{1,0:T(8,128)(2,1)S(1)} %fusion.57), channel_id=1, source_target_pairs={{1,2},{2,1},{5,6},{6,5},{9,10},{10,9},{13,14},{14,13},{17,18},{18,... | collective-permute-start | bytes 737288 | tf_op jit(solution)/shard_map/ppermute | solution.py:99
  54.5 10.5 %collective-permute-start.10 = (bf16[64,1920]{1,0:T(8,128)(2,1)S(1)}, bf16[64,1920]{1,0:T(8,128)(2,1)S(1)}, u32[]{:S(2)}, u32[]{:S(2)}) collective-permute-start(bf16[64,1920]{1,0:T(8,128)(2,1)S(1)} %fusion.90), channel_id=1, source_target_pairs={{0,1},{2,3},{1,0},{3,2},{4,5},{6,7},{5,4},{7,6},{8,9},{10,11},{9,8... | collective-permute-start | bytes 737288 | tf_op jit(solution)/shard_map/ppermute | solution.py:99
  59.3 13.5 %collective-permute-start.26 = (bf16[64,1920]{1,0:T(8,128)(2,1)S(1)}, bf16[64,1920]{1,0:T(8,128)(2,1)S(1)}, u32[]{:S(2)}, u32[]{:S(2)}) collective-permute-start(bf16[64,1920]{1,0:T(8,128)(2,1)S(1)} %get-tuple-element.65), channel_id=1, source_target_pairs={{1,2},{2,1},{5,6},{6,5},{9,10},{10,9},{13,14},{14,13},{17,18},{18,... | collective-permute-start | bytes 737288 | tf_op jit(solution)/shard_map/ppermute | solution.py:99
  60.1 12.7 %collective-permute-start.24 = (bf16[64,1920]{1,0:T(8,128)(2,1)S(1)}, bf16[64,1920]{1,0:T(8,128)(2,1)S(1)}, u32[]{:S(2)}, u32[]{:S(2)}) collective-permute-start(bf16[64,1920]{1,0:T(8,128)(2,1)S(1)} %get-tuple-element.64), channel_id=1, source_target_pairs={{0,1},{2,3},{1,0},{3,2},{4,5},{6,7},{5,4},{7,6},{8,9},{10,11},{9,8... | collective-permute-start | bytes 737288 | tf_op jit(solution)/shard_map/ppermute | solution.py:99
  65.2 9.9 %collective-permute-start.11 = (bf16[64,1920]{1,0:T(8,128)(2,1)S(1)}, bf16[64,1920]{1,0:T(8,128)(2,1)S(1)}, u32[]{:S(2)}, u32[]{:S(2)}) collective-permute-start(bf16[64,1920]{1,0:T(8,128)(2,1)S(1)} %get-tuple-element.63), channel_id=1, source_target_pairs={{1,2},{2,1},{5,6},{6,5},{9,10},{10,9},{13,14},{14,13},{17,18},{18,... | collective-permute-start | bytes 737288 | tf_op jit(solution)/shard_map/ppermute | solution.py:99
  65.9 11.0 %collective-permute-start.9 = (bf16[64,1920]{1,0:T(8,128)(2,1)S(1)}, bf16[64,1920]{1,0:T(8,128)(2,1)S(1)}, u32[]{:S(2)}, u32[]{:S(2)}) collective-permute-start(bf16[64,1920]{1,0:T(8,128)(2,1)S(1)} %get-tuple-element.62), channel_id=1, source_target_pairs={{0,1},{2,3},{1,0},{3,2},{4,5},{6,7},{5,4},{7,6},{8,9},{10,11},{9,8... | collective-permute-start | bytes 737288 | tf_op jit(solution)/shard_map/ppermute | solution.py:99
  77.4 11.3 %collective-permute-start.19 = (bf16[64,1792]{1,0:T(8,128)(2,1)S(1)}, bf16[64,1792]{1,0:T(8,128)(2,1)S(1)}, u32[]{:S(2)}, u32[]{:S(2)}) collective-permute-start(bf16[64,1792]{1,0:T(8,128)(2,1)S(1)} %get-tuple-element.37), channel_id=1, source_target_pairs={{0,1},{2,3},{1,0},{3,2},{4,5},{6,7},{5,4},{7,6},{8,9},{10,11},{9,8... | collective-permute-start | bytes 688136 | tf_op jit(solution)/shard_map/ppermute | solution.py:99
  79.7 9.0 %collective-permute-start.12 = (bf16[64,1792]{1,0:T(8,128)(2,1)S(1)}, bf16[64,1792]{1,0:T(8,128)(2,1)S(1)}, u32[]{:S(2)}, u32[]{:S(2)}) collective-permute-start(bf16[64,1792]{1,0:T(8,128)(2,1)S(1)} %get-tuple-element.37), channel_id=1, source_target_pairs={{1,2},{2,1},{5,6},{6,5},{9,10},{10,9},{13,14},{14,13},{17,18},{18,... | collective-permute-start | bytes 688136 | tf_op jit(solution)/shard_map/ppermute | solution.py:99
  82.0 11.6 %collective-permute-start.31 = (bf16[64,1792]{1,0:T(8,128)(2,1)S(1)}, bf16[64,1792]{1,0:T(8,128)(2,1)S(1)}, u32[]{:S(2)}, u32[]{:S(2)}) collective-permute-start(bf16[64,1792]{1,0:T(8,128)(2,1)S(1)} %get-tuple-element.76), channel_id=1, source_target_pairs={{1,2},{2,1},{5,6},{6,5},{9,10},{10,9},{13,14},{14,13},{17,18},{18,... | collective-permute-start | bytes 688136 | tf_op jit(solution)/shard_map/ppermute | solution.py:99
  82.7 11.0 %collective-permute-start.28 = (bf16[64,1792]{1,0:T(8,128)(2,1)S(1)}, bf16[64,1792]{1,0:T(8,128)(2,1)S(1)}, u32[]{:S(2)}, u32[]{:S(2)}) collective-permute-start(bf16[64,1792]{1,0:T(8,128)(2,1)S(1)} %get-tuple-element.77), channel_id=1, source_target_pairs={{0,1},{2,3},{1,0},{3,2},{4,5},{6,7},{5,4},{7,6},{8,9},{10,11},{9,8... | collective-permute-start | bytes 688136 | tf_op jit(solution)/shard_map/ppermute | solution.py:99
  88.9 9.8 %collective-permute-start.20 = (bf16[64,1792]{1,0:T(8,128)(2,1)S(1)}, bf16[64,1792]{1,0:T(8,128)(2,1)S(1)}, u32[]{:S(2)}, u32[]{:S(2)}) collective-permute-start(bf16[64,1792]{1,0:T(8,128)(2,1)S(1)} %get-tuple-element.72), channel_id=1, source_target_pairs={{1,2},{2,1},{5,6},{6,5},{9,10},{10,9},{13,14},{14,13},{17,18},{18,... | collective-permute-start | bytes 688136 | tf_op jit(solution)/shard_map/ppermute | solution.py:99
  89.6 9.5 %collective-permute-start.17 = (bf16[64,1792]{1,0:T(8,128)(2,1)S(1)}, bf16[64,1792]{1,0:T(8,128)(2,1)S(1)}, u32[]{:S(2)}, u32[]{:S(2)}) collective-permute-start(bf16[64,1792]{1,0:T(8,128)(2,1)S(1)} %get-tuple-element.73), channel_id=1, source_target_pairs={{0,1},{2,3},{1,0},{3,2},{4,5},{6,7},{5,4},{7,6},{8,9},{10,11},{9,8... | collective-permute-start | bytes 688136 | tf_op jit(solution)/shard_map/ppermute | solution.py:99
  93.8 10.6 %collective-permute-start.29 = (bf16[64,1792]{1,0:T(8,128)(2,1)S(1)}, bf16[64,1792]{1,0:T(8,128)(2,1)S(1)}, u32[]{:S(2)}, u32[]{:S(2)}) collective-permute-start(bf16[64,1792]{1,0:T(8,128)(2,1)S(1)} %get-tuple-element.75), channel_id=1, source_target_pairs={{1,2},{2,1},{5,6},{6,5},{9,10},{10,9},{13,14},{14,13},{17,18},{18,... | collective-permute-start | bytes 688136 | tf_op jit(solution)/shard_map/ppermute | solution.py:99
  94.5 9.9 %collective-permute-start.32 = (bf16[64,1792]{1,0:T(8,128)(2,1)S(1)}, bf16[64,1792]{1,0:T(8,128)(2,1)S(1)}, u32[]{:S(2)}, u32[]{:S(2)}) collective-permute-start(bf16[64,1792]{1,0:T(8,128)(2,1)S(1)} %get-tuple-element.74), channel_id=1, source_target_pairs={{0,1},{2,3},{1,0},{3,2},{4,5},{6,7},{5,4},{7,6},{8,9},{10,11},{9,8... | collective-permute-start | bytes 688136 | tf_op jit(solution)/shard_map/ppermute | solution.py:99
  110.3 17.1 %collective-permute-start.57 = (bf16[64,1792]{1,0:T(8,128)(2,1)S(1)}, bf16[64,1792]{1,0:T(8,128)(2,1)S(1)}, u32[]{:S(2)}, u32[]{:S(2)}) collective-permute-start(bf16[64,1792]{1,0:T(8,128)(2,1)S(1)} %get-tuple-element.69), channel_id=1, source_target_pairs={{1,2},{2,1},{5,6},{6,5},{9,10},{10,9},{13,14},{14,13},{17,18},{18,... | collective-permute-start | bytes 688136 | tf_op jit(solution)/shard_map/ppermute | solution.py:99
  111.0 16.4 %collective-permute-start.56 = (bf16[64,1792]{1,0:T(8,128)(2,1)S(1)}, bf16[64,1792]{1,0:T(8,128)(2,1)S(1)}, u32[]{:S(2)}, u32[]{:S(2)}) collective-permute-start(bf16[64,1792]{1,0:T(8,128)(2,1)S(1)} %get-tuple-element.68), channel_id=1, source_target_pairs={{0,1},{2,3},{1,0},{3,2},{4,5},{6,7},{5,4},{7,6},{8,9},{10,11},{9,8... | collective-permute-start | bytes 688136 | tf_op jit(solution)/shard_map/ppermute | solution.py:99
  122.7 15.7 %collective-permute-start.42 = (bf16[64,1792]{1,0:T(8,128)(2,1)S(1)}, bf16[64,1792]{1,0:T(8,128)(2,1)S(1)}, u32[]{:S(2)}, u32[]{:S(2)}) collective-permute-start(bf16[64,1792]{1,0:T(8,128)(2,1)S(1)} %get-tuple-element.67), channel_id=1, source_target_pairs={{1,2},{2,1},{5,6},{6,5},{9,10},{10,9},{13,14},{14,13},{17,18},{18,... | collective-permute-start | bytes 688136 | tf_op jit(solution)/shard_map/ppermute | solution.py:99
  124.4 14.0 %collective-permute-start.41 = (bf16[64,1792]{1,0:T(8,128)(2,1)S(1)}, bf16[64,1792]{1,0:T(8,128)(2,1)S(1)}, u32[]{:S(2)}, u32[]{:S(2)}) collective-permute-start(bf16[64,1792]{1,0:T(8,128)(2,1)S(1)} %get-tuple-element.66), channel_id=1, source_target_pairs={{0,1},{2,3},{1,0},{3,2},{4,5},{6,7},{5,4},{7,6},{8,9},{10,11},{9,8... | collective-permute-start | bytes 688136 | tf_op jit(solution)/shard_map/ppermute | solution.py:99
  127.6 15.6 %collective-permute-start.58 = (bf16[64,1920]{1,0:T(8,128)(2,1)S(1)}, bf16[64,1920]{1,0:T(8,128)(2,1)S(1)}, u32[]{:S(2)}, u32[]{:S(2)}) collective-permute-start(bf16[64,1920]{1,0:T(8,128)(2,1)S(1)} %pad.13), channel_id=1, source_target_pairs={{1,2},{2,1},{5,6},{6,5},{9,10},{10,9},{13,14},{14,13},{17,18},{18,... | collective-permute-start | bytes 737288 | tf_op jit(solution)/shard_map/ppermute | solution.py:99
  134.7 9.7 %collective-permute-start.62 = (bf16[64,1920]{1,0:T(8,128)(2,1)S(1)}, bf16[64,1920]{1,0:T(8,128)(2,1)S(1)}, u32[]{:S(2)}, u32[]{:S(2)}) collective-permute-start(bf16[64,1920]{1,0:T(8,128)(2,1)S(1)} %pad.13), channel_id=1, source_target_pairs={{0,1},{2,3},{1,0},{3,2},{4,5},{6,7},{5,4},{7,6},{8,9},{10,11},{9,8... | collective-permute-start | bytes 737288 | tf_op jit(solution)/shard_map/ppermute | solution.py:99
  138.5 9.5 %collective-permute-start.47 = (bf16[64,1920]{1,0:T(8,128)(2,1)S(1)}, bf16[64,1920]{1,0:T(8,128)(2,1)S(1)}, u32[]{:S(2)}, u32[]{:S(2)}) collective-permute-start(bf16[64,1920]{1,0:T(8,128)(2,1)S(1)} %pad.12), channel_id=1, source_target_pairs={{0,1},{2,3},{1,0},{3,2},{4,5},{6,7},{5,4},{7,6},{8,9},{10,11},{9,8... | collective-permute-start | bytes 737288 | tf_op jit(solution)/shard_map/ppermute | solution.py:99
  138.6 9.4 %collective-permute-start.43 = (bf16[64,1920]{1,0:T(8,128)(2,1)S(1)}, bf16[64,1920]{1,0:T(8,128)(2,1)S(1)}, u32[]{:S(2)}, u32[]{:S(2)}) collective-permute-start(bf16[64,1920]{1,0:T(8,128)(2,1)S(1)} %pad.12), channel_id=1, source_target_pairs={{1,2},{2,1},{5,6},{6,5},{9,10},{10,9},{13,14},{14,13},{17,18},{18,... | collective-permute-start | bytes 737288 | tf_op jit(solution)/shard_map/ppermute | solution.py:99
  144.6 9.1 %collective-permute-start.59 = (bf16[64,1920]{1,0:T(8,128)(2,1)S(1)}, bf16[64,1920]{1,0:T(8,128)(2,1)S(1)}, u32[]{:S(2)}, u32[]{:S(2)}) collective-permute-start(bf16[64,1920]{1,0:T(8,128)(2,1)S(1)} %get-tuple-element.60), channel_id=1, source_target_pairs={{0,1},{2,3},{1,0},{3,2},{4,5},{6,7},{5,4},{7,6},{8,9},{10,11},{9,8... | collective-permute-start | bytes 737288 | tf_op jit(solution)/shard_map/ppermute | solution.py:99
  148.2 12.9 %collective-permute-start.48 = (bf16[64,1920]{1,0:T(8,128)(2,1)S(1)}, bf16[64,1920]{1,0:T(8,128)(2,1)S(1)}, u32[]{:S(2)}, u32[]{:S(2)}) collective-permute-start(bf16[64,1920]{1,0:T(8,128)(2,1)S(1)} %get-tuple-element.54), channel_id=1, source_target_pairs={{1,2},{2,1},{5,6},{6,5},{9,10},{10,9},{13,14},{14,13},{17,18},{18,... | collective-permute-start | bytes 737288 | tf_op jit(solution)/shard_map/ppermute | solution.py:99
  148.8 12.2 %collective-permute-start.44 = (bf16[64,1920]{1,0:T(8,128)(2,1)S(1)}, bf16[64,1920]{1,0:T(8,128)(2,1)S(1)}, u32[]{:S(2)}, u32[]{:S(2)}) collective-permute-start(bf16[64,1920]{1,0:T(8,128)(2,1)S(1)} %get-tuple-element.55), channel_id=1, source_target_pairs={{0,1},{2,3},{1,0},{3,2},{4,5},{6,7},{5,4},{7,6},{8,9},{10,11},{9,8... | collective-permute-start | bytes 737288 | tf_op jit(solution)/shard_map/ppermute | solution.py:99
  153.8 12.5 %collective-permute-start.60 = (bf16[64,1920]{1,0:T(8,128)(2,1)S(1)}, bf16[64,1920]{1,0:T(8,128)(2,1)S(1)}, u32[]{:S(2)}, u32[]{:S(2)}) collective-permute-start(bf16[64,1920]{1,0:T(8,128)(2,1)S(1)} %get-tuple-element.58), channel_id=1, source_target_pairs={{1,2},{2,1},{5,6},{6,5},{9,10},{10,9},{13,14},{14,13},{17,18},{18,... | collective-permute-start | bytes 737288 | tf_op jit(solution)/shard_map/ppermute | solution.py:99
  154.5 11.8 %collective-permute-start.64 = (bf16[64,1920]{1,0:T(8,128)(2,1)S(1)}, bf16[64,1920]{1,0:T(8,128)(2,1)S(1)}, u32[]{:S(2)}, u32[]{:S(2)}) collective-permute-start(bf16[64,1920]{1,0:T(8,128)(2,1)S(1)} %get-tuple-element.59), channel_id=1, source_target_pairs={{0,1},{2,3},{1,0},{3,2},{4,5},{6,7},{5,4},{7,6},{8,9},{10,11},{9,8... | collective-permute-start | bytes 737288 | tf_op jit(solution)/shard_map/ppermute | solution.py:99
  161.2 11.6 %collective-permute-start.45 = (bf16[64,1920]{1,0:T(8,128)(2,1)S(1)}, bf16[64,1920]{1,0:T(8,128)(2,1)S(1)}, u32[]{:S(2)}, u32[]{:S(2)}) collective-permute-start(bf16[64,1920]{1,0:T(8,128)(2,1)S(1)} %get-tuple-element.53), channel_id=1, source_target_pairs={{1,2},{2,1},{5,6},{6,5},{9,10},{10,9},{13,14},{14,13},{17,18},{18,... | collective-permute-start | bytes 737288 | tf_op jit(solution)/shard_map/ppermute | solution.py:99
  161.9 10.9 %collective-permute-start.49 = (bf16[64,1920]{1,0:T(8,128)(2,1)S(1)}, bf16[64,1920]{1,0:T(8,128)(2,1)S(1)}, u32[]{:S(2)}, u32[]{:S(2)}) collective-permute-start(bf16[64,1920]{1,0:T(8,128)(2,1)S(1)} %get-tuple-element.52), channel_id=1, source_target_pairs={{0,1},{2,3},{1,0},{3,2},{4,5},{6,7},{5,4},{7,6},{8,9},{10,11},{9,8... | collective-permute-start | bytes 737288 | tf_op jit(solution)/shard_map/ppermute | solution.py:99
  167.3 19.0 %collective-permute-start.65 = (bf16[64,1920]{1,0:T(8,128)(2,1)}, bf16[64,1920]{1,0:T(8,128)(2,1)}, u32[]{:S(2)}, u32[]{:S(2)}) collective-permute-start(bf16[64,1920]{1,0:T(8,128)(2,1)} %get-tuple-element.57), channel_id=1, source_target_pairs={{1,2},{2,1},{5,6},{6,5},{9,10},{10,9},{13,14},{14,13},{17,18},{18,... | collective-permute-start | bytes 737288 | tf_op jit(solution)/shard_map/ppermute | solution.py:99
  168.6 17.6 %collective-permute-start.61 = (bf16[64,1920]{1,0:T(8,128)(2,1)}, bf16[64,1920]{1,0:T(8,128)(2,1)}, u32[]{:S(2)}, u32[]{:S(2)}) collective-permute-start(bf16[64,1920]{1,0:T(8,128)(2,1)} %get-tuple-element.56), channel_id=1, source_target_pairs={{0,1},{2,3},{1,0},{3,2},{4,5},{6,7},{5,4},{7,6},{8,9},{10,11},{9,8... | collective-permute-start | bytes 737288 | tf_op jit(solution)/shard_map/ppermute | solution.py:99
  190.9 9.9 %collective-permute-start.52 = (bf16[64,1920]{1,0:T(8,128)(2,1)}, bf16[64,1920]{1,0:T(8,128)(2,1)S(1)}, u32[]{:S(2)}, u32[]{:S(2)}) collective-permute-start(bf16[64,1920]{1,0:T(8,128)(2,1)} %collective-permute-done.51), channel_id=1, source_target_pairs={{1,2},{2,1},{5,6},{6,5},{9,10},{10,9},{13,14},{14,13},{17,18},{18,... | collective-permute-start | bytes 737288 | tf_op jit(solution)/shard_map/ppermute | solution.py:99
  191.6 11.1 %collective-permute-start.54 = (bf16[64,1920]{1,0:T(8,128)(2,1)}, bf16[64,1920]{1,0:T(8,128)(2,1)S(1)}, u32[]{:S(2)}, u32[]{:S(2)}) collective-permute-start(bf16[64,1920]{1,0:T(8,128)(2,1)} %collective-permute-done.53), channel_id=1, source_target_pairs={{0,1},{2,3},{1,0},{3,2},{4,5},{6,7},{5,4},{7,6},{8,9},{10,11},{9,8... | collective-permute-start | bytes 737288 | tf_op jit(solution)/shard_map/ppermute | solution.py:99
  196.1 10.1 %collective-permute-start.67 = (bf16[64,1920]{1,0:T(8,128)(2,1)S(1)}, bf16[64,1920]{1,0:T(8,128)(2,1)S(1)}, u32[]{:S(2)}, u32[]{:S(2)}) collective-permute-start(bf16[64,1920]{1,0:T(8,128)(2,1)S(1)} %collective-permute-done.66), channel_id=1, source_target_pairs={{1,2},{2,1},{5,6},{6,5},{9,10},{10,9},{13,14},{14,13},{17,18},{18,... | collective-permute-start | bytes 737288 | tf_op jit(solution)/shard_map/ppermute | solution.py:99
  197.1 10.8 %collective-permute-start.69 = (bf16[64,1920]{1,0:T(8,128)(2,1)S(1)}, bf16[64,1920]{1,0:T(8,128)(2,1)S(1)}, u32[]{:S(2)}, u32[]{:S(2)}) collective-permute-start(bf16[64,1920]{1,0:T(8,128)(2,1)S(1)} %collective-permute-done.68), channel_id=1, source_target_pairs={{0,1},{2,3},{1,0},{3,2},{4,5},{6,7},{5,4},{7,6},{8,9},{10,11},{9,8... | collective-permute-start | bytes 737288 | tf_op jit(solution)/shard_map/ppermute | solution.py:99
  202.7 10.5 %collective-permute-start.55 = (bf16[64,1920]{1,0:T(8,128)(2,1)S(1)}, bf16[64,1920]{1,0:T(8,128)(2,1)S(1)}, u32[]{:S(2)}, u32[]{:S(2)}) collective-permute-start(bf16[64,1920]{1,0:T(8,128)(2,1)S(1)} %collective-permute-done.52), channel_id=1, source_target_pairs={{0,1},{2,3},{1,0},{3,2},{4,5},{6,7},{5,4},{7,6},{8,9},{10,11},{9,8... | collective-permute-start | bytes 737288 | tf_op jit(solution)/shard_map/ppermute | solution.py:99
  208.0 10.8 %collective-permute-start.70 = (bf16[64,1920]{1,0:T(8,128)(2,1)S(1)}, bf16[64,1920]{1,0:T(8,128)(2,1)S(1)}, u32[]{:S(2)}, u32[]{:S(2)}) collective-permute-start(bf16[64,1920]{1,0:T(8,128)(2,1)S(1)} %collective-permute-done.67), channel_id=1, source_target_pairs={{0,1},{2,3},{1,0},{3,2},{4,5},{6,7},{5,4},{7,6},{8,9},{10,11},{9,8... | collective-permute-start | bytes 737288 | tf_op jit(solution)/shard_map/ppermute | solution.py:99
  226.0 9.9 %collective-permute-start.76 = (bf16[512,640]{1,0:T(8,128)(2,1)S(1)}, bf16[512,640]{1,0:T(8,128)(2,1)S(1)}, u32[]{:S(2)}, u32[]{:S(2)}) collective-permute-start(bf16[512,640]{1,0:T(8,128)(2,1)S(1)} %pad_maximum_fusion.4), channel_id=1, source_target_pairs={{0,4},{4,0},{8,12},{12,8},{16,20},{20,16},{24,28},{28,24},{1,5},{5... | collective-permute-start | bytes 1966088 | tf_op jit(solution)/shard_map/ppermute | solution.py:88
  238.0 8.9 %collective-permute-start.78 = (bf16[128,640]{1,0:T(8,128)(2,1)S(1)}, bf16[128,640]{1,0:T(8,128)(2,1)S(1)}, u32[]{:S(2)}, u32[]{:S(2)}) collective-permute-start(bf16[128,640]{1,0:T(8,128)(2,1)S(1)} %bitcast.362), channel_id=1, source_target_pairs={{0,16},{4,20},{8,24},{12,28},{16,0},{20,4},{24,8},{28,12},{1,17},{... | collective-permute-start | bytes 491528 | tf_op jit(solution)/shard_map/ppermute | solution.py:91
  238.6 9.5 %collective-permute-start.77 = (bf16[128,640]{1,0:T(8,128)(2,1)S(1)}, bf16[128,640]{1,0:T(8,128)(2,1)S(1)}, u32[]{:S(2)}, u32[]{:S(2)}) collective-permute-start(bf16[128,640]{1,0:T(8,128)(2,1)S(1)} %bitcast.361), channel_id=1, source_target_pairs={{0,8},{4,12},{8,0},{12,4},{16,24},{20,28},{24,16},{28,20},{1,9},{5... | collective-permute-start | bytes 491528 | tf_op jit(solution)/shard_map/ppermute | solution.py:91
  239.8 13.0 %collective-permute-start.75 = (bf16[128,512]{1,0:T(8,128)(2,1)S(1)}, bf16[128,512]{1,0:T(8,128)(2,1)S(1)}, u32[]{:S(2)}, u32[]{:S(2)}) collective-permute-start(bf16[128,512]{1,0:T(8,128)(2,1)S(1)} %fusion.79), channel_id=1, source_target_pairs={{0,0},{1,8},{2,16},{3,24},{4,4},{5,12},{6,20},{7,28},{8,1},{9,9},{... | collective-permute-start | bytes 393224 | tf_op jit(solution)/shard_map/ppermute | solution.py:85
  (49 other events, 441.7 us)

commit v2 on v1

--- a/solution.py
+++ b/solution.py
@@ -13,10 +13,27 @@
 BF16 = jnp.bfloat16
 
 
+def scale_rows(quanta_ref, scales_ref, out_ref):
+    out_ref[...] = (quanta_ref[...].astype(F32) * scales_ref[0]).astype(BF16)
+
+
 def dequant_rows(quanta, scales):
+    rows, columns = quanta.shape
     blocks = scales.shape[0]
-    widened = quanta.astype(F32).reshape(blocks, quanta.shape[0] // blocks, quanta.shape[1])
-    return (widened * scales.astype(F32)[:, None, :]).reshape(quanta.shape).astype(BF16)
+    tile = rows // blocks
+    return pl.pallas_call(
+        scale_rows,
+        grid=(blocks,),
+        in_specs=[
+            pl.BlockSpec((tile, columns), lambda i: (i, 0)),
+            pl.BlockSpec((1, 1, columns), lambda i: (i, 0, 0)),
+        ],
+        out_specs=pl.BlockSpec((tile, columns), lambda i: (i, 0)),
+        out_shape=jax.ShapeDtypeStruct((rows, columns), BF16),
+        cost_estimate=pl.CostEstimate(
+            flops=rows * columns, bytes_accessed=4 * rows * columns, transcendentals=0
+        ),
+    )(quanta, scales.astype(F32).reshape(blocks, 1, columns))
 
 
 def scale_columns(quanta_ref, scales_ref, out_ref):
@@ -28,16 +45,29 @@
         out_ref[:, columns] = (quanta_ref[:, columns].astype(F32) * scale).astype(BF16)
 
 
+def scale_columns_across(quanta_ref, scales_ref, out_ref):
+    blocks = scales_ref.shape[0]
+    width = quanta_ref.shape[1] // blocks
+    scales = scales_ref[...].astype(F32).T
+    for block in range(blocks):
+        columns = slice(block * width, (block + 1) * width)
+        scale = scales[:, block : block + 1]
+        out_ref[:, columns] = (quanta_ref[:, columns].astype(F32) * scale).astype(BF16)
+
+
 def dequant_cols(quanta, scales):
     rows, columns = quanta.shape
-    tile = ROW_TILE if rows % ROW_TILE == 0 else rows
+    blocks = scales.shape[1]
+    if rows % ROW_TILE == 0 and blocks % 8 == 0:
+        tile, kernel, scales = ROW_TILE, scale_columns_across, scales.T
+        scales_spec = pl.BlockSpec((blocks, tile), lambda i: (0, i))
+    else:
+        tile, kernel = rows, scale_columns
+        scales_spec = pl.BlockSpec((tile, blocks), lambda i: (i, 0))
     return pl.pallas_call(
-        scale_columns,
+        kernel,
         grid=(rows // tile,),
-        in_specs=[
-            pl.BlockSpec((tile, columns), lambda i: (i, 0)),
-            pl.BlockSpec((tile, scales.shape[1]), lambda i: (i, 0)),
-        ],
+        in_specs=[pl.BlockSpec((tile, columns), lambda i: (i, 0)), scales_spec],
         out_specs=pl.BlockSpec((tile, columns), lambda i: (i, 0)),
         out_shape=jax.ShapeDtypeStruct((rows, columns), BF16),
         cost_estimate=pl.CostEstimate(

time: 272 us -> 278 us (1.022)
  Pallas kernels: 6.77 us -> 13.5 us
  other arithmetic: 19.7 us -> 15.9 us
    pallas_call x1 -> x2, Pallas kernels: 6.77 us -> 13.5 us  [the longest x1 6.94 us: dequant_cols(): pl.pallas_call(kernel, grid=(rows // tile,), in_specs=[pl.BlockSpec((tile...]
  transfers between devices with their start and end apart: 84 -> 84, of which waited for: 32 -> 32; matrix products, arithmetic and copies ran while one was open for 10% -> 8% of each run, Pallas kernels for 3% -> 5%
where the time goes in v2:
time: 278 us; the launch traced here: 274 us
  starting transfers between devices  148 us (53%)
  waiting for transfers between devices  69.1 us (25%)
  matrix products  20 us (7%)
  other arithmetic  15.9 us (6%)
  Pallas kernels  13.5 us (5%)
  local copies, waits for them, and re-layouts  5.68 us (2%)
    ppermute x52, starting transfers between devices, pair_swap(): return lax.ppermute(block, 'local', pairs + [(t, s) for s, t in pairs])  112 us
    ppermute x21, waiting for transfers between devices, chip_swap(): lax.ppermute(block, 'node', [(n, n ^ 2 * shift) for n in range(n_node)])  31.1 us
    ppermute x52, waiting for transfers between devices, pair_swap(): return lax.ppermute(block, 'local', pairs + [(t, s) for s, t in pairs])  23.7 us
    ppermute x21, starting transfers between devices, chip_swap(): lax.ppermute(block, 'node', [(n, n ^ 2 * shift) for n in range(n_node)])  23.5 us
    dot_general x13, matrix products, dot(): lax.dot_general(left, right, (dims, ((), ())), preferred_element_type=F32)  20 us
    ppermute x3, starting transfers between devices, exchange(): return lax.ppermute(block, ('node', 'local'), swap)  10.9 us
    ppermute x3, waiting for transfers between devices, exchange(): return lax.ppermute(block, ('node', 'local'), swap)  10.8 us
    pallas_call x1, Pallas kernels, dequant_cols(): pl.pallas_call(kernel, grid=(rows // tile,), in_specs=[pl.BlockSpec((tile...  6.94 us
  transfers between devices with their start and end apart: 84, of which 32 were waited for; matrix products, arithmetic and copies ran while one was open for 8% of the time, Pallas kernels for 5%

profile of v2, /device:TPU:2, one launch (start us, length us, event | category | flops | bytes accessed | tf_op | source)
XLA Modules:
  0.0 273.8 jit_solution(18183816706110969930)
XLA Ops:
  0.6 3.5 %collective-permute-start = (bf16[128,512]{1,0:T(8,128)(2,1)}, bf16[128,512]{1,0:T(8,128)(2,1)S(1)}, u32[]{:S(2)}, u32[]{:S(2)}) collective-permute-start(bf16[128,512]{1,0:T(8,128)(2,1)} %param.7), channel_id=1, source_target_pairs={{0,0},{1,8},{2,16},{3,24},{4,4},{5,12},{6,20},{7,28},{8,1},{9,9},{... | collective-permute-start | bytes 393224 | tf_op jit(solution)/shard_map/ppermute | solution.py:115
  5.0 3.3 %collective-permute-start.4 = (bf16[144,512]{1,0:T(8,128)(2,1)S(1)}, bf16[144,512]{1,0:T(8,128)(2,1)S(1)}, u32[]{:S(2)}, u32[]{:S(2)}) collective-permute-start(bf16[144,512]{1,0:T(8,128)(2,1)S(1)} %fusion.91), channel_id=1, source_target_pairs={{0,0},{1,8},{2,16},{3,24},{4,4},{5,12},{6,20},{7,28},{8,1},{9,9},{... | collective-permute-start | bytes 442376 | tf_op jit(solution)/shard_map/ppermute | solution.py:115
  8.3 6.9 %shard_map.86 = bf16[1792,1024]{1,0:T(8,128)(2,1)} custom-call(bf16[1792,1024]{1,0:T(8,128)(2,1)} %quanta_ref.1, bf16[8,1792]{1,0:T(8,128)(2,1)} %bitcast.381), custom_call_target="tpu_custom_call" | custom-call | flops 1835008 | bytes 7340032 | tf_op jit(solution)/shard_map/pallas_call | solution.py:67
  15.3 6.6 %collective-permute-done = bf16[128,512]{1,0:T(8,128)(2,1)S(1)} collective-permute-done((bf16[128,512]{1,0:T(8,128)(2,1)}, bf16[128,512]{1,0:T(8,128)(2,1)S(1)}, u32[]{:S(2)}, u32[]{:S(2)}) %collective-permute-start) | collective-permute-done | bytes 131104 | tf_op jit(solution)/shard_map/ppermute | solution.py:115
  21.9 3.5 %collective-permute-start.3 = (bf16[128,512]{1,0:T(8,128)(2,1)S(1)}, bf16[128,512]{1,0:T(8,128)(2,1)S(1)}, u32[]{:S(2)}, u32[]{:S(2)}) collective-permute-start(bf16[128,512]{1,0:T(8,128)(2,1)S(1)} %collective-permute-done), channel_id=1, source_target_pairs={{0,24},{4,28},{8,16},{12,20},{16,8},{20,12},{24,0},{28,4},{1,25},{... | collective-permute-start | bytes 393224 | tf_op jit(solution)/shard_map/ppermute | solution.py:121
  25.4 2.7 collective-permute-done.1
  29.5 6.5 %shard_map.87 = bf16[1024,1792]{1,0:T(8,128)(2,1)} custom-call(bf16[1024,1792]{1,0:T(8,128)(2,1)} %quanta_ref.2, f32[8,1,1792]{2,1,0:T(1,128)} %reshape.621.scales_ref), custom_call_target="tpu_custom_call" | custom-call | flops 1835008 | bytes 7340032 | tf_op jit(solution)/shard_map/pallas_call | solution.py:24
  40.8 2.1 collective-permute-start.13
  47.4 2.4 collective-permute-done.14
  51.4 2.8 %collective-permute-done.22 = bf16[64,1920]{1,0:T(8,128)(2,1)S(1)} collective-permute-done((bf16[64,1920]{1,0:T(8,128)(2,1)S(1)}, bf16[64,1920]{1,0:T(8,128)(2,1)S(1)}, u32[]{:S(2)}, u32[]{:S(2)}) %collective-permute-start.22) | collective-permute-done | bytes 245792 | tf_op jit(solution)/shard_map/ppermute | solution.py:129
  54.9 4.7 %collective-permute-start.25 = (bf16[64,1920]{1,0:T(8,128)(2,1)S(1)}, bf16[64,1920]{1,0:T(8,128)(2,1)S(1)}, u32[]{:S(2)}, u32[]{:S(2)}) collective-permute-start(bf16[64,1920]{1,0:T(8,128)(2,1)S(1)} %fusion.90), channel_id=1, source_target_pairs={{0,1},{2,3},{1,0},{3,2},{4,5},{6,7},{5,4},{7,6},{8,9},{10,11},{9,8... | collective-permute-start | bytes 737288 | tf_op jit(solution)/shard_map/ppermute | solution.py:129
  60.4 4.5 %collective-permute-start.10 = (bf16[64,1920]{1,0:T(8,128)(2,1)S(1)}, bf16[64,1920]{1,0:T(8,128)(2,1)S(1)}, u32[]{:S(2)}, u32[]{:S(2)}) collective-permute-start(bf16[64,1920]{1,0:T(8,128)(2,1)S(1)} %fusion.89), channel_id=1, source_target_pairs={{0,1},{2,3},{1,0},{3,2},{4,5},{6,7},{5,4},{7,6},{8,9},{10,11},{9,8... | collective-permute-start | bytes 737288 | tf_op jit(solution)/shard_map/ppermute | solution.py:129
  66.0 5.0 %collective-permute-start.24 = (bf16[64,1920]{1,0:T(8,128)(2,1)S(1)}, bf16[64,1920]{1,0:T(8,128)(2,1)S(1)}, u32[]{:S(2)}, u32[]{:S(2)}) collective-permute-start(bf16[64,1920]{1,0:T(8,128)(2,1)S(1)} %get-tuple-element.64), channel_id=1, source_target_pairs={{0,1},{2,3},{1,0},{3,2},{4,5},{6,7},{5,4},{7,6},{8,9},{10,11},{9,8... | collective-permute-start | bytes 737288 | tf_op jit(solution)/shard_map/ppermute | solution.py:129
  71.8 4.2 %collective-permute-start.9 = (bf16[64,1920]{1,0:T(8,128)(2,1)S(1)}, bf16[64,1920]{1,0:T(8,128)(2,1)S(1)}, u32[]{:S(2)}, u32[]{:S(2)}) collective-permute-start(bf16[64,1920]{1,0:T(8,128)(2,1)S(1)} %get-tuple-element.62), channel_id=1, source_target_pairs={{0,1},{2,3},{1,0},{3,2},{4,5},{6,7},{5,4},{7,6},{8,9},{10,11},{9,8... | collective-permute-start | bytes 737288 | tf_op jit(solution)/shard_map/ppermute | solution.py:129
  83.3 2.3 collective-permute-start.19
  88.6 6.0 %collective-permute-start.28 = (bf16[64,1792]{1,0:T(8,128)(2,1)S(1)}, bf16[64,1792]{1,0:T(8,128)(2,1)S(1)}, u32[]{:S(2)}, u32[]{:S(2)}) collective-permute-start(bf16[64,1792]{1,0:T(8,128)(2,1)S(1)} %get-tuple-element.77), channel_id=1, source_target_pairs={{0,1},{2,3},{1,0},{3,2},{4,5},{6,7},{5,4},{7,6},{8,9},{10,11},{9,8... | collective-permute-start | bytes 688136 | tf_op jit(solution)/shard_map/ppermute | solution.py:129
  95.4 4.1 %collective-permute-start.17 = (bf16[64,1792]{1,0:T(8,128)(2,1)S(1)}, bf16[64,1792]{1,0:T(8,128)(2,1)S(1)}, u32[]{:S(2)}, u32[]{:S(2)}) collective-permute-start(bf16[64,1792]{1,0:T(8,128)(2,1)S(1)} %get-tuple-element.73), channel_id=1, source_target_pairs={{0,1},{2,3},{1,0},{3,2},{4,5},{6,7},{5,4},{7,6},{8,9},{10,11},{9,8... | collective-permute-start | bytes 688136 | tf_op jit(solution)/shard_map/ppermute | solution.py:129
  100.4 4.0 %collective-permute-start.32 = (bf16[64,1792]{1,0:T(8,128)(2,1)S(1)}, bf16[64,1792]{1,0:T(8,128)(2,1)S(1)}, u32[]{:S(2)}, u32[]{:S(2)}) collective-permute-start(bf16[64,1792]{1,0:T(8,128)(2,1)S(1)} %get-tuple-element.74), channel_id=1, source_target_pairs={{0,1},{2,3},{1,0},{3,2},{4,5},{6,7},{5,4},{7,6},{8,9},{10,11},{9,8... | collective-permute-start | bytes 688136 | tf_op jit(solution)/shard_map/ppermute | solution.py:129
  106.0 4.1 %collective-permute-start.21 = (bf16[64,1792]{1,0:T(8,128)(2,1)S(1)}, bf16[64,1792]{1,0:T(8,128)(2,1)S(1)}, u32[]{:S(2)}, u32[]{:S(2)}) collective-permute-start(bf16[64,1792]{1,0:T(8,128)(2,1)S(1)} %get-tuple-element.70), channel_id=1, source_target_pairs={{0,1},{2,3},{1,0},{3,2},{4,5},{6,7},{5,4},{7,6},{8,9},{10,11},{9,8... | collective-permute-start | bytes 688136 | tf_op jit(solution)/shard_map/ppermute | solution.py:129
  111.8 2.4 collective-permute-done.21
  116.8 4.2 %collective-permute-start.56 = (bf16[64,1792]{1,0:T(8,128)(2,1)S(1)}, bf16[64,1792]{1,0:T(8,128)(2,1)S(1)}, u32[]{:S(2)}, u32[]{:S(2)}) collective-permute-start(bf16[64,1792]{1,0:T(8,128)(2,1)S(1)} %get-tuple-element.68), channel_id=1, source_target_pairs={{0,1},{2,3},{1,0},{3,2},{4,5},{6,7},{5,4},{7,6},{8,9},{10,11},{9,8... | collective-permute-start | bytes 688136 | tf_op jit(solution)/shard_map/ppermute | solution.py:129
  121.7 2.5 collective-permute-start.35
  125.0 3.6 %collective-permute-done.36 = bf16[128,512]{1,0:T(8,128)(2,1)S(1)} collective-permute-done((bf16[128,512]{1,0:T(8,128)(2,1)S(1)}, bf16[128,512]{1,0:T(8,128)(2,1)S(1)}, u32[]{:S(2)}, u32[]{:S(2)}) %collective-permute-start.36) | collective-permute-done | bytes 131104 | tf_op jit(solution)/shard_map/ppermute | solution.py:121
  134.3 2.6 collective-permute-done.37
  137.0 3.6 %collective-permute-done.38 = bf16[128,512]{1,0:T(8,128)(2,1)S(1)} collective-permute-done((bf16[128,512]{1,0:T(8,128)(2,1)S(1)}, bf16[128,512]{1,0:T(8,128)(2,1)S(1)}, u32[]{:S(2)}, u32[]{:S(2)}) %collective-permute-start.38) | collective-permute-done | bytes 131104 | tf_op jit(solution)/shard_map/ppermute | solution.py:121
  140.5 3.4 %collective-permute-start.62 = (bf16[64,1920]{1,0:T(8,128)(2,1)S(1)}, bf16[64,1920]{1,0:T(8,128)(2,1)S(1)}, u32[]{:S(2)}, u32[]{:S(2)}) collective-permute-start(bf16[64,1920]{1,0:T(8,128)(2,1)S(1)} %pad.13), channel_id=1, source_target_pairs={{0,1},{2,3},{1,0},{3,2},{4,5},{6,7},{5,4},{7,6},{8,9},{10,11},{9,8... | collective-permute-start | bytes 737288 | tf_op jit(solution)/shard_map/ppermute | solution.py:129
  150.3 2.5 collective-permute-start.59
  154.6 5.0 %collective-permute-start.44 = (bf16[64,1920]{1,0:T(8,128)(2,1)S(1)}, bf16[64,1920]{1,0:T(8,128)(2,1)S(1)}, u32[]{:S(2)}, u32[]{:S(2)}) collective-permute-start(bf16[64,1920]{1,0:T(8,128)(2,1)S(1)} %get-tuple-element.55), channel_id=1, source_target_pairs={{0,1},{2,3},{1,0},{3,2},{4,5},{6,7},{5,4},{7,6},{8,9},{10,11},{9,8... | collective-permute-start | bytes 737288 | tf_op jit(solution)/shard_map/ppermute | solution.py:129
  160.4 6.5 %collective-permute-start.64 = (bf16[64,1920]{1,0:T(8,128)(2,1)S(1)}, bf16[64,1920]{1,0:T(8,128)(2,1)S(1)}, u32[]{:S(2)}, u32[]{:S(2)}) collective-permute-start(bf16[64,1920]{1,0:T(8,128)(2,1)S(1)} %get-tuple-element.59), channel_id=1, source_target_pairs={{0,1},{2,3},{1,0},{3,2},{4,5},{6,7},{5,4},{7,6},{8,9},{10,11},{9,8... | collective-permute-start | bytes 737288 | tf_op jit(solution)/shard_map/ppermute | solution.py:129
  167.8 4.4 %collective-permute-start.49 = (bf16[64,1920]{1,0:T(8,128)(2,1)S(1)}, bf16[64,1920]{1,0:T(8,128)(2,1)S(1)}, u32[]{:S(2)}, u32[]{:S(2)}) collective-permute-start(bf16[64,1920]{1,0:T(8,128)(2,1)S(1)} %get-tuple-element.52), channel_id=1, source_target_pairs={{0,1},{2,3},{1,0},{3,2},{4,5},{6,7},{5,4},{7,6},{8,9},{10,11},{9,8... | collective-permute-start | bytes 737288 | tf_op jit(solution)/shard_map/ppermute | solution.py:129
  174.5 4.1 %collective-permute-start.61 = (bf16[64,1920]{1,0:T(8,128)(2,1)}, bf16[64,1920]{1,0:T(8,128)(2,1)}, u32[]{:S(2)}, u32[]{:S(2)}) collective-permute-start(bf16[64,1920]{1,0:T(8,128)(2,1)} %get-tuple-element.56), channel_id=1, source_target_pairs={{0,1},{2,3},{1,0},{3,2},{4,5},{6,7},{5,4},{7,6},{8,9},{10,11},{9,8... | collective-permute-start | bytes 737288 | tf_op jit(solution)/shard_map/ppermute | solution.py:129
  179.5 3.0 %collective-permute-start.46 = (bf16[64,1920]{1,0:T(8,128)(2,1)S(1)}, bf16[64,1920]{1,0:T(8,128)(2,1)S(1)}, u32[]{:S(2)}, u32[]{:S(2)}) collective-permute-start(bf16[64,1920]{1,0:T(8,128)(2,1)S(1)} %get-tuple-element.50), channel_id=1, source_target_pairs={{0,1},{2,3},{1,0},{3,2},{4,5},{6,7},{5,4},{7,6},{8,9},{10,11},{9,8... | collective-permute-start | bytes 737288 | tf_op jit(solution)/shard_map/ppermute | solution.py:129
  183.4 4.7 %collective-permute-done.46 = bf16[64,1920]{1,0:T(8,128)(2,1)S(1)} collective-permute-done((bf16[64,1920]{1,0:T(8,128)(2,1)S(1)}, bf16[64,1920]{1,0:T(8,128)(2,1)S(1)}, u32[]{:S(2)}, u32[]{:S(2)}) %collective-permute-start.46) | collective-permute-done | bytes 245792 | tf_op jit(solution)/shard_map/ppermute | solution.py:129
  196.9 5.3 %collective-permute-start.54 = (bf16[64,1920]{1,0:T(8,128)(2,1)}, bf16[64,1920]{1,0:T(8,128)(2,1)S(1)}, u32[]{:S(2)}, u32[]{:S(2)}) collective-permute-start(bf16[64,1920]{1,0:T(8,128)(2,1)} %collective-permute-done.53), channel_id=1, source_target_pairs={{0,1},{2,3},{1,0},{3,2},{4,5},{6,7},{5,4},{7,6},{8,9},{10,11},{9,8... | collective-permute-start | bytes 737288 | tf_op jit(solution)/shard_map/ppermute | solution.py:129
  203.5 3.2 %collective-permute-start.69 = (bf16[64,1920]{1,0:T(8,128)(2,1)S(1)}, bf16[64,1920]{1,0:T(8,128)(2,1)S(1)}, u32[]{:S(2)}, u32[]{:S(2)}) collective-permute-start(bf16[64,1920]{1,0:T(8,128)(2,1)S(1)} %collective-permute-done.68), channel_id=1, source_target_pairs={{0,1},{2,3},{1,0},{3,2},{4,5},{6,7},{5,4},{7,6},{8,9},{10,11},{9,8... | collective-permute-start | bytes 737288 | tf_op jit(solution)/shard_map/ppermute | solution.py:129
  206.6 2.6 collective-permute-done.54
  209.2 2.5 collective-permute-start.55
  211.9 2.6 collective-permute-done.69
  214.5 2.1 collective-permute-start.70
  216.6 3.2 %collective-permute-done.55 = bf16[64,1920]{1,0:T(8,128)(2,1)S(1)} collective-permute-done((bf16[64,1920]{1,0:T(8,128)(2,1)S(1)}, bf16[64,1920]{1,0:T(8,128)(2,1)S(1)}, u32[]{:S(2)}, u32[]{:S(2)}) %collective-permute-start.55) | collective-permute-done | bytes 245792 | tf_op jit(solution)/shard_map/ppermute | solution.py:129
  235.4 3.7 %collective-permute-done.74 = bf16[128,512]{1,0:T(8,128)(2,1)S(1)} collective-permute-done((bf16[128,512]{1,0:T(8,128)(2,1)S(1)}, bf16[128,512]{1,0:T(8,128)(2,1)S(1)}, u32[]{:S(2)}, u32[]{:S(2)}) %collective-permute-start.74) | collective-permute-done | bytes 131104 | tf_op jit(solution)/shard_map/ppermute | solution.py:121
  239.1 2.0 collective-permute-done.73
  245.2 4.1 %collective-permute-start.75 = (bf16[128,512]{1,0:T(8,128)(2,1)S(1)}, bf16[128,512]{1,0:T(8,128)(2,1)S(1)}, u32[]{:S(2)}, u32[]{:S(2)}) collective-permute-start(bf16[128,512]{1,0:T(8,128)(2,1)S(1)} %fusion.78), channel_id=1, source_target_pairs={{0,0},{1,8},{2,16},{3,24},{4,4},{5,12},{6,20},{7,28},{8,1},{9,9},{... | collective-permute-start | bytes 393224 | tf_op jit(solution)/shard_map/ppermute | solution.py:115
  249.7 2.3 collective-permute-done.78
  253.8 4.2 %collective-permute-done.75 = bf16[128,512]{1,0:T(8,128)(2,1)S(1)} collective-permute-done((bf16[128,512]{1,0:T(8,128)(2,1)S(1)}, bf16[128,512]{1,0:T(8,128)(2,1)S(1)}, u32[]{:S(2)}, u32[]{:S(2)}) %collective-permute-start.75) | collective-permute-done | bytes 131104 | tf_op jit(solution)/shard_map/ppermute | solution.py:115
  258.1 3.4 %collective-permute-start.82 = (bf16[128,512]{1,0:T(8,128)(2,1)S(1)}, bf16[128,512]{1,0:T(8,128)(2,1)S(1)}, u32[]{:S(2)}, u32[]{:S(2)}) collective-permute-start(bf16[128,512]{1,0:T(8,128)(2,1)S(1)} %fusion.81), channel_id=1, source_target_pairs={{0,24},{4,28},{8,16},{12,20},{16,8},{20,12},{24,0},{28,4},{1,25},{... | collective-permute-start | bytes 393224 | tf_op jit(solution)/shard_map/ppermute | solution.py:121
  261.5 2.4 collective-permute-done.80
  267.7 5.5 %convolution_convert_fusion = bf16[1792,1024]{1,0:T(8,128)(2,1)} fusion(bf16[256,1792]{1,0:T(8,128)(2,1)S(1)} %get-tuple-element.49, bf16[256,1792]{1,0:T(8,128)(2,1)S(1)} %get-tuple-element.47, bf16[256,1792]{1,0:T(8,128)(2,1)S(1)} %bitcast.352, bf16[256,1792]{1,0:T(8,128)(2,1)S(1)} %bitcast.354, bf16[512,1024]{1,0:T(8,128)(2,1)S(1)} %copy-done.5, ...), kind=kOutput, calls=%fused_computation | convolution fusion | flops 3778805760 | bytes 9437184 | tf_op jit(solution)/shard_map/dot_general | solution.py:80
  (306 shorter events, 90.7 us)
Async XLA Ops:
  0.6 21.2 %collective-permute-start = (bf16[128,512]{1,0:T(8,128)(2,1)}, bf16[128,512]{1,0:T(8,128)(2,1)S(1)}, u32[]{:S(2)}, u32[]{:S(2)}) collective-permute-start(bf16[128,512]{1,0:T(8,128)(2,1)} %param.7), channel_id=1, source_target_pairs={{0,0},{1,8},{2,16},{3,24},{4,4},{5,12},{6,20},{7,28},{8,1},{9,9},{... | collective-permute-start | bytes 393224 | tf_op jit(solution)/shard_map/ppermute | solution.py:115
  5.0 20.4 %collective-permute-start.4 = (bf16[144,512]{1,0:T(8,128)(2,1)S(1)}, bf16[144,512]{1,0:T(8,128)(2,1)S(1)}, u32[]{:S(2)}, u32[]{:S(2)}) collective-permute-start(bf16[144,512]{1,0:T(8,128)(2,1)S(1)} %fusion.91), channel_id=1, source_target_pairs={{0,0},{1,8},{2,16},{3,24},{4,4},{5,12},{6,20},{7,28},{8,1},{9,9},{... | collective-permute-start | bytes 442376 | tf_op jit(solution)/shard_map/ppermute | solution.py:115
  45.2 9.0 %collective-permute-start.22 = (bf16[64,1920]{1,0:T(8,128)(2,1)S(1)}, bf16[64,1920]{1,0:T(8,128)(2,1)S(1)}, u32[]{:S(2)}, u32[]{:S(2)}) collective-permute-start(bf16[64,1920]{1,0:T(8,128)(2,1)S(1)} %dynamic-slice_bitcast_fusion), channel_id=1, source_target_pairs={{0,1},{2,3},{1,0},{3,2},{4,5},{6,7},{5,4},{7,6},{8,9},{10,11},{9,8... | collective-permute-start | bytes 737288 | tf_op jit(solution)/shard_map/ppermute | solution.py:129
  45.3 14.3 %collective-permute-start.7 = (bf16[64,1920]{1,0:T(8,128)(2,1)S(1)}, bf16[64,1920]{1,0:T(8,128)(2,1)S(1)}, u32[]{:S(2)}, u32[]{:S(2)}) collective-permute-start(bf16[64,1920]{1,0:T(8,128)(2,1)S(1)} %dynamic-slice_bitcast_fusion.1), channel_id=1, source_target_pairs={{0,1},{2,3},{1,0},{3,2},{4,5},{6,7},{5,4},{7,6},{8,9},{10,11},{9,8... | collective-permute-start | bytes 737288 | tf_op jit(solution)/shard_map/ppermute | solution.py:129
  51.3 24.6 %collective-permute-start.16 = (bf16[512,512]{1,0:T(8,128)(2,1)S(1)}, bf16[512,512]{1,0:T(8,128)(2,1)S(1)}, u32[]{:S(2)}, u32[]{:S(2)}) collective-permute-start(bf16[512,512]{1,0:T(8,128)(2,1)S(1)} %bitcast.346), channel_id=1, source_target_pairs={{0,4},{4,0},{8,12},{12,8},{16,20},{20,16},{24,28},{28,24},{1,5},{5... | collective-permute-start | bytes 1572872 | tf_op jit(solution)/shard_map/ppermute | solution.py:118
  54.3 10.7 %collective-permute-start.23 = (bf16[64,1920]{1,0:T(8,128)(2,1)S(1)}, bf16[64,1920]{1,0:T(8,128)(2,1)S(1)}, u32[]{:S(2)}, u32[]{:S(2)}) collective-permute-start(bf16[64,1920]{1,0:T(8,128)(2,1)S(1)} %fusion.53), channel_id=1, source_target_pairs={{1,2},{2,1},{5,6},{6,5},{9,10},{10,9},{13,14},{14,13},{17,18},{18,... | collective-permute-start | bytes 737288 | tf_op jit(solution)/shard_map/ppermute | solution.py:129
  54.9 10.0 %collective-permute-start.25 = (bf16[64,1920]{1,0:T(8,128)(2,1)S(1)}, bf16[64,1920]{1,0:T(8,128)(2,1)S(1)}, u32[]{:S(2)}, u32[]{:S(2)}) collective-permute-start(bf16[64,1920]{1,0:T(8,128)(2,1)S(1)} %fusion.90), channel_id=1, source_target_pairs={{0,1},{2,3},{1,0},{3,2},{4,5},{6,7},{5,4},{7,6},{8,9},{10,11},{9,8... | collective-permute-start | bytes 737288 | tf_op jit(solution)/shard_map/ppermute | solution.py:129
  59.7 11.2 %collective-permute-start.8 = (bf16[64,1920]{1,0:T(8,128)(2,1)S(1)}, bf16[64,1920]{1,0:T(8,128)(2,1)S(1)}, u32[]{:S(2)}, u32[]{:S(2)}) collective-permute-start(bf16[64,1920]{1,0:T(8,128)(2,1)S(1)} %fusion.56), channel_id=1, source_target_pairs={{1,2},{2,1},{5,6},{6,5},{9,10},{10,9},{13,14},{14,13},{17,18},{18,... | collective-permute-start | bytes 737288 | tf_op jit(solution)/shard_map/ppermute | solution.py:129
  60.4 10.5 %collective-permute-start.10 = (bf16[64,1920]{1,0:T(8,128)(2,1)S(1)}, bf16[64,1920]{1,0:T(8,128)(2,1)S(1)}, u32[]{:S(2)}, u32[]{:S(2)}) collective-permute-start(bf16[64,1920]{1,0:T(8,128)(2,1)S(1)} %fusion.89), channel_id=1, source_target_pairs={{0,1},{2,3},{1,0},{3,2},{4,5},{6,7},{5,4},{7,6},{8,9},{10,11},{9,8... | collective-permute-start | bytes 737288 | tf_op jit(solution)/shard_map/ppermute | solution.py:129
  65.1 13.5 %collective-permute-start.26 = (bf16[64,1920]{1,0:T(8,128)(2,1)S(1)}, bf16[64,1920]{1,0:T(8,128)(2,1)S(1)}, u32[]{:S(2)}, u32[]{:S(2)}) collective-permute-start(bf16[64,1920]{1,0:T(8,128)(2,1)S(1)} %get-tuple-element.65), channel_id=1, source_target_pairs={{1,2},{2,1},{5,6},{6,5},{9,10},{10,9},{13,14},{14,13},{17,18},{18,... | collective-permute-start | bytes 737288 | tf_op jit(solution)/shard_map/ppermute | solution.py:129
  66.0 12.7 %collective-permute-start.24 = (bf16[64,1920]{1,0:T(8,128)(2,1)S(1)}, bf16[64,1920]{1,0:T(8,128)(2,1)S(1)}, u32[]{:S(2)}, u32[]{:S(2)}) collective-permute-start(bf16[64,1920]{1,0:T(8,128)(2,1)S(1)} %get-tuple-element.64), channel_id=1, source_target_pairs={{0,1},{2,3},{1,0},{3,2},{4,5},{6,7},{5,4},{7,6},{8,9},{10,11},{9,8... | collective-permute-start | bytes 737288 | tf_op jit(solution)/shard_map/ppermute | solution.py:129
  71.1 9.9 %collective-permute-start.11 = (bf16[64,1920]{1,0:T(8,128)(2,1)S(1)}, bf16[64,1920]{1,0:T(8,128)(2,1)S(1)}, u32[]{:S(2)}, u32[]{:S(2)}) collective-permute-start(bf16[64,1920]{1,0:T(8,128)(2,1)S(1)} %get-tuple-element.63), channel_id=1, source_target_pairs={{1,2},{2,1},{5,6},{6,5},{9,10},{10,9},{13,14},{14,13},{17,18},{18,... | collective-permute-start | bytes 737288 | tf_op jit(solution)/shard_map/ppermute | solution.py:129
  71.8 11.0 %collective-permute-start.9 = (bf16[64,1920]{1,0:T(8,128)(2,1)S(1)}, bf16[64,1920]{1,0:T(8,128)(2,1)S(1)}, u32[]{:S(2)}, u32[]{:S(2)}) collective-permute-start(bf16[64,1920]{1,0:T(8,128)(2,1)S(1)} %get-tuple-element.62), channel_id=1, source_target_pairs={{0,1},{2,3},{1,0},{3,2},{4,5},{6,7},{5,4},{7,6},{8,9},{10,11},{9,8... | collective-permute-start | bytes 737288 | tf_op jit(solution)/shard_map/ppermute | solution.py:129
  83.3 11.2 %collective-permute-start.19 = (bf16[64,1792]{1,0:T(8,128)(2,1)S(1)}, bf16[64,1792]{1,0:T(8,128)(2,1)S(1)}, u32[]{:S(2)}, u32[]{:S(2)}) collective-permute-start(bf16[64,1792]{1,0:T(8,128)(2,1)S(1)} %get-tuple-element.37), channel_id=1, source_target_pairs={{0,1},{2,3},{1,0},{3,2},{4,5},{6,7},{5,4},{7,6},{8,9},{10,11},{9,8... | collective-permute-start | bytes 688136 | tf_op jit(solution)/shard_map/ppermute | solution.py:129
  85.6 8.9 %collective-permute-start.12 = (bf16[64,1792]{1,0:T(8,128)(2,1)S(1)}, bf16[64,1792]{1,0:T(8,128)(2,1)S(1)}, u32[]{:S(2)}, u32[]{:S(2)}) collective-permute-start(bf16[64,1792]{1,0:T(8,128)(2,1)S(1)} %get-tuple-element.37), channel_id=1, source_target_pairs={{1,2},{2,1},{5,6},{6,5},{9,10},{10,9},{13,14},{14,13},{17,18},{18,... | collective-permute-start | bytes 688136 | tf_op jit(solution)/shard_map/ppermute | solution.py:129
  87.9 11.6 %collective-permute-start.31 = (bf16[64,1792]{1,0:T(8,128)(2,1)S(1)}, bf16[64,1792]{1,0:T(8,128)(2,1)S(1)}, u32[]{:S(2)}, u32[]{:S(2)}) collective-permute-start(bf16[64,1792]{1,0:T(8,128)(2,1)S(1)} %get-tuple-element.76), channel_id=1, source_target_pairs={{1,2},{2,1},{5,6},{6,5},{9,10},{10,9},{13,14},{14,13},{17,18},{18,... | collective-permute-start | bytes 688136 | tf_op jit(solution)/shard_map/ppermute | solution.py:129
  88.6 11.0 %collective-permute-start.28 = (bf16[64,1792]{1,0:T(8,128)(2,1)S(1)}, bf16[64,1792]{1,0:T(8,128)(2,1)S(1)}, u32[]{:S(2)}, u32[]{:S(2)}) collective-permute-start(bf16[64,1792]{1,0:T(8,128)(2,1)S(1)} %get-tuple-element.77), channel_id=1, source_target_pairs={{0,1},{2,3},{1,0},{3,2},{4,5},{6,7},{5,4},{7,6},{8,9},{10,11},{9,8... | collective-permute-start | bytes 688136 | tf_op jit(solution)/shard_map/ppermute | solution.py:129
  94.7 9.8 %collective-permute-start.20 = (bf16[64,1792]{1,0:T(8,128)(2,1)S(1)}, bf16[64,1792]{1,0:T(8,128)(2,1)S(1)}, u32[]{:S(2)}, u32[]{:S(2)}) collective-permute-start(bf16[64,1792]{1,0:T(8,128)(2,1)S(1)} %get-tuple-element.72), channel_id=1, source_target_pairs={{1,2},{2,1},{5,6},{6,5},{9,10},{10,9},{13,14},{14,13},{17,18},{18,... | collective-permute-start | bytes 688136 | tf_op jit(solution)/shard_map/ppermute | solution.py:129
  95.4 9.7 %collective-permute-start.17 = (bf16[64,1792]{1,0:T(8,128)(2,1)S(1)}, bf16[64,1792]{1,0:T(8,128)(2,1)S(1)}, u32[]{:S(2)}, u32[]{:S(2)}) collective-permute-start(bf16[64,1792]{1,0:T(8,128)(2,1)S(1)} %get-tuple-element.73), channel_id=1, source_target_pairs={{0,1},{2,3},{1,0},{3,2},{4,5},{6,7},{5,4},{7,6},{8,9},{10,11},{9,8... | collective-permute-start | bytes 688136 | tf_op jit(solution)/shard_map/ppermute | solution.py:129
  99.8 10.4 %collective-permute-start.29 = (bf16[64,1792]{1,0:T(8,128)(2,1)S(1)}, bf16[64,1792]{1,0:T(8,128)(2,1)S(1)}, u32[]{:S(2)}, u32[]{:S(2)}) collective-permute-start(bf16[64,1792]{1,0:T(8,128)(2,1)S(1)} %get-tuple-element.75), channel_id=1, source_target_pairs={{1,2},{2,1},{5,6},{6,5},{9,10},{10,9},{13,14},{14,13},{17,18},{18,... | collective-permute-start | bytes 688136 | tf_op jit(solution)/shard_map/ppermute | solution.py:129
  100.4 9.8 %collective-permute-start.32 = (bf16[64,1792]{1,0:T(8,128)(2,1)S(1)}, bf16[64,1792]{1,0:T(8,128)(2,1)S(1)}, u32[]{:S(2)}, u32[]{:S(2)}) collective-permute-start(bf16[64,1792]{1,0:T(8,128)(2,1)S(1)} %get-tuple-element.74), channel_id=1, source_target_pairs={{0,1},{2,3},{1,0},{3,2},{4,5},{6,7},{5,4},{7,6},{8,9},{10,11},{9,8... | collective-permute-start | bytes 688136 | tf_op jit(solution)/shard_map/ppermute | solution.py:129
  116.1 17.2 %collective-permute-start.57 = (bf16[64,1792]{1,0:T(8,128)(2,1)S(1)}, bf16[64,1792]{1,0:T(8,128)(2,1)S(1)}, u32[]{:S(2)}, u32[]{:S(2)}) collective-permute-start(bf16[64,1792]{1,0:T(8,128)(2,1)S(1)} %get-tuple-element.69), channel_id=1, source_target_pairs={{1,2},{2,1},{5,6},{6,5},{9,10},{10,9},{13,14},{14,13},{17,18},{18,... | collective-permute-start | bytes 688136 | tf_op jit(solution)/shard_map/ppermute | solution.py:129
  116.8 16.5 %collective-permute-start.56 = (bf16[64,1792]{1,0:T(8,128)(2,1)S(1)}, bf16[64,1792]{1,0:T(8,128)(2,1)S(1)}, u32[]{:S(2)}, u32[]{:S(2)}) collective-permute-start(bf16[64,1792]{1,0:T(8,128)(2,1)S(1)} %get-tuple-element.68), channel_id=1, source_target_pairs={{0,1},{2,3},{1,0},{3,2},{4,5},{6,7},{5,4},{7,6},{8,9},{10,11},{9,8... | collective-permute-start | bytes 688136 | tf_op jit(solution)/shard_map/ppermute | solution.py:129
  128.6 15.5 %collective-permute-start.42 = (bf16[64,1792]{1,0:T(8,128)(2,1)S(1)}, bf16[64,1792]{1,0:T(8,128)(2,1)S(1)}, u32[]{:S(2)}, u32[]{:S(2)}) collective-permute-start(bf16[64,1792]{1,0:T(8,128)(2,1)S(1)} %get-tuple-element.67), channel_id=1, source_target_pairs={{1,2},{2,1},{5,6},{6,5},{9,10},{10,9},{13,14},{14,13},{17,18},{18,... | collective-permute-start | bytes 688136 | tf_op jit(solution)/shard_map/ppermute | solution.py:129
  130.3 13.8 %collective-permute-start.41 = (bf16[64,1792]{1,0:T(8,128)(2,1)S(1)}, bf16[64,1792]{1,0:T(8,128)(2,1)S(1)}, u32[]{:S(2)}, u32[]{:S(2)}) collective-permute-start(bf16[64,1792]{1,0:T(8,128)(2,1)S(1)} %get-tuple-element.66), channel_id=1, source_target_pairs={{0,1},{2,3},{1,0},{3,2},{4,5},{6,7},{5,4},{7,6},{8,9},{10,11},{9,8... | collective-permute-start | bytes 688136 | tf_op jit(solution)/shard_map/ppermute | solution.py:129
  133.4 15.5 %collective-permute-start.58 = (bf16[64,1920]{1,0:T(8,128)(2,1)S(1)}, bf16[64,1920]{1,0:T(8,128)(2,1)S(1)}, u32[]{:S(2)}, u32[]{:S(2)}) collective-permute-start(bf16[64,1920]{1,0:T(8,128)(2,1)S(1)} %pad.13), channel_id=1, source_target_pairs={{1,2},{2,1},{5,6},{6,5},{9,10},{10,9},{13,14},{14,13},{17,18},{18,... | collective-permute-start | bytes 737288 | tf_op jit(solution)/shard_map/ppermute | solution.py:129
  140.5 9.6 %collective-permute-start.62 = (bf16[64,1920]{1,0:T(8,128)(2,1)S(1)}, bf16[64,1920]{1,0:T(8,128)(2,1)S(1)}, u32[]{:S(2)}, u32[]{:S(2)}) collective-permute-start(bf16[64,1920]{1,0:T(8,128)(2,1)S(1)} %pad.13), channel_id=1, source_target_pairs={{0,1},{2,3},{1,0},{3,2},{4,5},{6,7},{5,4},{7,6},{8,9},{10,11},{9,8... | collective-permute-start | bytes 737288 | tf_op jit(solution)/shard_map/ppermute | solution.py:129
  144.3 9.5 %collective-permute-start.47 = (bf16[64,1920]{1,0:T(8,128)(2,1)S(1)}, bf16[64,1920]{1,0:T(8,128)(2,1)S(1)}, u32[]{:S(2)}, u32[]{:S(2)}) collective-permute-start(bf16[64,1920]{1,0:T(8,128)(2,1)S(1)} %pad.12), channel_id=1, source_target_pairs={{0,1},{2,3},{1,0},{3,2},{4,5},{6,7},{5,4},{7,6},{8,9},{10,11},{9,8... | collective-permute-start | bytes 737288 | tf_op jit(solution)/shard_map/ppermute | solution.py:129
  144.3 9.4 %collective-permute-start.43 = (bf16[64,1920]{1,0:T(8,128)(2,1)S(1)}, bf16[64,1920]{1,0:T(8,128)(2,1)S(1)}, u32[]{:S(2)}, u32[]{:S(2)}) collective-permute-start(bf16[64,1920]{1,0:T(8,128)(2,1)S(1)} %pad.12), channel_id=1, source_target_pairs={{1,2},{2,1},{5,6},{6,5},{9,10},{10,9},{13,14},{14,13},{17,18},{18,... | collective-permute-start | bytes 737288 | tf_op jit(solution)/shard_map/ppermute | solution.py:129
  150.3 9.2 %collective-permute-start.59 = (bf16[64,1920]{1,0:T(8,128)(2,1)S(1)}, bf16[64,1920]{1,0:T(8,128)(2,1)S(1)}, u32[]{:S(2)}, u32[]{:S(2)}) collective-permute-start(bf16[64,1920]{1,0:T(8,128)(2,1)S(1)} %get-tuple-element.60), channel_id=1, source_target_pairs={{0,1},{2,3},{1,0},{3,2},{4,5},{6,7},{5,4},{7,6},{8,9},{10,11},{9,8... | collective-permute-start | bytes 737288 | tf_op jit(solution)/shard_map/ppermute | solution.py:129
  153.9 13.0 %collective-permute-start.48 = (bf16[64,1920]{1,0:T(8,128)(2,1)S(1)}, bf16[64,1920]{1,0:T(8,128)(2,1)S(1)}, u32[]{:S(2)}, u32[]{:S(2)}) collective-permute-start(bf16[64,1920]{1,0:T(8,128)(2,1)S(1)} %get-tuple-element.54), channel_id=1, source_target_pairs={{1,2},{2,1},{5,6},{6,5},{9,10},{10,9},{13,14},{14,13},{17,18},{18,... | collective-permute-start | bytes 737288 | tf_op jit(solution)/shard_map/ppermute | solution.py:129
  154.6 12.3 %collective-permute-start.44 = (bf16[64,1920]{1,0:T(8,128)(2,1)S(1)}, bf16[64,1920]{1,0:T(8,128)(2,1)S(1)}, u32[]{:S(2)}, u32[]{:S(2)}) collective-permute-start(bf16[64,1920]{1,0:T(8,128)(2,1)S(1)} %get-tuple-element.55), channel_id=1, source_target_pairs={{0,1},{2,3},{1,0},{3,2},{4,5},{6,7},{5,4},{7,6},{8,9},{10,11},{9,8... | collective-permute-start | bytes 737288 | tf_op jit(solution)/shard_map/ppermute | solution.py:129
  159.7 12.5 %collective-permute-start.60 = (bf16[64,1920]{1,0:T(8,128)(2,1)S(1)}, bf16[64,1920]{1,0:T(8,128)(2,1)S(1)}, u32[]{:S(2)}, u32[]{:S(2)}) collective-permute-start(bf16[64,1920]{1,0:T(8,128)(2,1)S(1)} %get-tuple-element.58), channel_id=1, source_target_pairs={{1,2},{2,1},{5,6},{6,5},{9,10},{10,9},{13,14},{14,13},{17,18},{18,... | collective-permute-start | bytes 737288 | tf_op jit(solution)/shard_map/ppermute | solution.py:129
  160.4 11.8 %collective-permute-start.64 = (bf16[64,1920]{1,0:T(8,128)(2,1)S(1)}, bf16[64,1920]{1,0:T(8,128)(2,1)S(1)}, u32[]{:S(2)}, u32[]{:S(2)}) collective-permute-start(bf16[64,1920]{1,0:T(8,128)(2,1)S(1)} %get-tuple-element.59), channel_id=1, source_target_pairs={{0,1},{2,3},{1,0},{3,2},{4,5},{6,7},{5,4},{7,6},{8,9},{10,11},{9,8... | collective-permute-start | bytes 737288 | tf_op jit(solution)/shard_map/ppermute | solution.py:129
  167.1 11.6 %collective-permute-start.45 = (bf16[64,1920]{1,0:T(8,128)(2,1)S(1)}, bf16[64,1920]{1,0:T(8,128)(2,1)S(1)}, u32[]{:S(2)}, u32[]{:S(2)}) collective-permute-start(bf16[64,1920]{1,0:T(8,128)(2,1)S(1)} %get-tuple-element.53), channel_id=1, source_target_pairs={{1,2},{2,1},{5,6},{6,5},{9,10},{10,9},{13,14},{14,13},{17,18},{18,... | collective-permute-start | bytes 737288 | tf_op jit(solution)/shard_map/ppermute | solution.py:129
  167.8 10.9 %collective-permute-start.49 = (bf16[64,1920]{1,0:T(8,128)(2,1)S(1)}, bf16[64,1920]{1,0:T(8,128)(2,1)S(1)}, u32[]{:S(2)}, u32[]{:S(2)}) collective-permute-start(bf16[64,1920]{1,0:T(8,128)(2,1)S(1)} %get-tuple-element.52), channel_id=1, source_target_pairs={{0,1},{2,3},{1,0},{3,2},{4,5},{6,7},{5,4},{7,6},{8,9},{10,11},{9,8... | collective-permute-start | bytes 737288 | tf_op jit(solution)/shard_map/ppermute | solution.py:129
  173.2 18.7 %collective-permute-start.65 = (bf16[64,1920]{1,0:T(8,128)(2,1)}, bf16[64,1920]{1,0:T(8,128)(2,1)}, u32[]{:S(2)}, u32[]{:S(2)}) collective-permute-start(bf16[64,1920]{1,0:T(8,128)(2,1)} %get-tuple-element.57), channel_id=1, source_target_pairs={{1,2},{2,1},{5,6},{6,5},{9,10},{10,9},{13,14},{14,13},{17,18},{18,... | collective-permute-start | bytes 737288 | tf_op jit(solution)/shard_map/ppermute | solution.py:129
  174.5 17.4 %collective-permute-start.61 = (bf16[64,1920]{1,0:T(8,128)(2,1)}, bf16[64,1920]{1,0:T(8,128)(2,1)}, u32[]{:S(2)}, u32[]{:S(2)}) collective-permute-start(bf16[64,1920]{1,0:T(8,128)(2,1)} %get-tuple-element.56), channel_id=1, source_target_pairs={{0,1},{2,3},{1,0},{3,2},{4,5},{6,7},{5,4},{7,6},{8,9},{10,11},{9,8... | collective-permute-start | bytes 737288 | tf_op jit(solution)/shard_map/ppermute | solution.py:129
  196.3 10.4 %collective-permute-start.52 = (bf16[64,1920]{1,0:T(8,128)(2,1)S(1)}, bf16[64,1920]{1,0:T(8,128)(2,1)S(1)}, u32[]{:S(2)}, u32[]{:S(2)}) collective-permute-start(bf16[64,1920]{1,0:T(8,128)(2,1)S(1)} %collective-permute-done.51), channel_id=1, source_target_pairs={{1,2},{2,1},{5,6},{6,5},{9,10},{10,9},{13,14},{14,13},{17,18},{18,... | collective-permute-start | bytes 737288 | tf_op jit(solution)/shard_map/ppermute | solution.py:129
  196.9 12.3 %collective-permute-start.54 = (bf16[64,1920]{1,0:T(8,128)(2,1)}, bf16[64,1920]{1,0:T(8,128)(2,1)S(1)}, u32[]{:S(2)}, u32[]{:S(2)}) collective-permute-start(bf16[64,1920]{1,0:T(8,128)(2,1)} %collective-permute-done.53), channel_id=1, source_target_pairs={{0,1},{2,3},{1,0},{3,2},{4,5},{6,7},{5,4},{7,6},{8,9},{10,11},{9,8... | collective-permute-start | bytes 737288 | tf_op jit(solution)/shard_map/ppermute | solution.py:129
  202.4 9.4 %collective-permute-start.67 = (bf16[64,1920]{1,0:T(8,128)(2,1)S(1)}, bf16[64,1920]{1,0:T(8,128)(2,1)S(1)}, u32[]{:S(2)}, u32[]{:S(2)}) collective-permute-start(bf16[64,1920]{1,0:T(8,128)(2,1)S(1)} %collective-permute-done.66), channel_id=1, source_target_pairs={{1,2},{2,1},{5,6},{6,5},{9,10},{10,9},{13,14},{14,13},{17,18},{18,... | collective-permute-start | bytes 737288 | tf_op jit(solution)/shard_map/ppermute | solution.py:129
  203.5 11.0 %collective-permute-start.69 = (bf16[64,1920]{1,0:T(8,128)(2,1)S(1)}, bf16[64,1920]{1,0:T(8,128)(2,1)S(1)}, u32[]{:S(2)}, u32[]{:S(2)}) collective-permute-start(bf16[64,1920]{1,0:T(8,128)(2,1)S(1)} %collective-permute-done.68), channel_id=1, source_target_pairs={{0,1},{2,3},{1,0},{3,2},{4,5},{6,7},{5,4},{7,6},{8,9},{10,11},{9,8... | collective-permute-start | bytes 737288 | tf_op jit(solution)/shard_map/ppermute | solution.py:129
  209.2 10.5 %collective-permute-start.55 = (bf16[64,1920]{1,0:T(8,128)(2,1)S(1)}, bf16[64,1920]{1,0:T(8,128)(2,1)S(1)}, u32[]{:S(2)}, u32[]{:S(2)}) collective-permute-start(bf16[64,1920]{1,0:T(8,128)(2,1)S(1)} %collective-permute-done.52), channel_id=1, source_target_pairs={{0,1},{2,3},{1,0},{3,2},{4,5},{6,7},{5,4},{7,6},{8,9},{10,11},{9,8... | collective-permute-start | bytes 737288 | tf_op jit(solution)/shard_map/ppermute | solution.py:129
  214.5 9.9 %collective-permute-start.70 = (bf16[64,1920]{1,0:T(8,128)(2,1)S(1)}, bf16[64,1920]{1,0:T(8,128)(2,1)S(1)}, u32[]{:S(2)}, u32[]{:S(2)}) collective-permute-start(bf16[64,1920]{1,0:T(8,128)(2,1)S(1)} %collective-permute-done.67), channel_id=1, source_target_pairs={{0,1},{2,3},{1,0},{3,2},{4,5},{6,7},{5,4},{7,6},{8,9},{10,11},{9,8... | collective-permute-start | bytes 737288 | tf_op jit(solution)/shard_map/ppermute | solution.py:129
  231.5 9.7 %collective-permute-start.76 = (bf16[512,640]{1,0:T(8,128)(2,1)S(1)}, bf16[512,640]{1,0:T(8,128)(2,1)S(1)}, u32[]{:S(2)}, u32[]{:S(2)}) collective-permute-start(bf16[512,640]{1,0:T(8,128)(2,1)S(1)} %pad_maximum_fusion.4), channel_id=1, source_target_pairs={{0,4},{4,0},{8,12},{12,8},{16,20},{20,16},{24,28},{28,24},{1,5},{5... | collective-permute-start | bytes 1966088 | tf_op jit(solution)/shard_map/ppermute | solution.py:118
  242.8 9.2 %collective-permute-start.78 = (bf16[128,640]{1,0:T(8,128)(2,1)S(1)}, bf16[128,640]{1,0:T(8,128)(2,1)S(1)}, u32[]{:S(2)}, u32[]{:S(2)}) collective-permute-start(bf16[128,640]{1,0:T(8,128)(2,1)S(1)} %bitcast.359), channel_id=1, source_target_pairs={{0,16},{4,20},{8,24},{12,28},{16,0},{20,4},{24,8},{28,12},{1,17},{... | collective-permute-start | bytes 491528 | tf_op jit(solution)/shard_map/ppermute | solution.py:121
  243.8 9.5 %collective-permute-start.77 = (bf16[128,640]{1,0:T(8,128)(2,1)S(1)}, bf16[128,640]{1,0:T(8,128)(2,1)S(1)}, u32[]{:S(2)}, u32[]{:S(2)}) collective-permute-start(bf16[128,640]{1,0:T(8,128)(2,1)S(1)} %bitcast.358), channel_id=1, source_target_pairs={{0,8},{4,12},{8,0},{12,4},{16,24},{20,28},{24,16},{28,20},{1,9},{5... | collective-permute-start | bytes 491528 | tf_op jit(solution)/shard_map/ppermute | solution.py:121
  245.2 12.8 %collective-permute-start.75 = (bf16[128,512]{1,0:T(8,128)(2,1)S(1)}, bf16[128,512]{1,0:T(8,128)(2,1)S(1)}, u32[]{:S(2)}, u32[]{:S(2)}) collective-permute-start(bf16[128,512]{1,0:T(8,128)(2,1)S(1)} %fusion.78), channel_id=1, source_target_pairs={{0,0},{1,8},{2,16},{3,24},{4,4},{5,12},{6,20},{7,28},{8,1},{9,9},{... | collective-permute-start | bytes 393224 | tf_op jit(solution)/shard_map/ppermute | solution.py:115
  (49 other events, 349.4 us)

commit v3 on v1

--- a/solution.py
+++ b/solution.py
@@ -119,11 +119,14 @@
             jnp.concatenate([other, own], axis=1),
         )
 
-    def gather_chips(block):
+    def gather_chips(block, *others):
         mine = jnp.zeros((block.shape[0] * chips, block.shape[1]), block.dtype)
         mine = put(mine, block, chip)
         for shift in range(1, chips):
-            mine = put(mine, chip_swap(block, shift), chip ^ shift)
+            arrived = chip_swap(block, shift)
+            if others:
+                arrived = after(arrived, *others)
+            mine = put(mine, arrived, chip ^ shift)
         return mine
 
     def gather_core(mine):
@@ -202,7 +205,7 @@
                 left = jnp.where(even, firsts[ahead - 1], seconds[ahead - 1])
                 piece = jnp.where(z >= behind, right, left)
                 out = put(out, piece, (z + ahead) % n_local)
-        return out, total
+        return out, total, firsts[0]
 
     def widen(block):
         return jnp.pad(block, ((0, 0), (0, LANES)))
@@ -238,15 +241,19 @@
 
     x = gather_core(after(gather_chips(x_home), g_home))
     partials = [up_partial(chunk_of(x, h)) for h in halves_of]
-    totals = [line(None, partial)[1] for partial in partials]
-    g = gather_node(after(g_home, *partials))
+    totals, seen = [], []
+    for partial in partials:
+        _, total, arrived = line(None, partial)
+        totals.append(total)
+        seen.append(arrived)
+    g = gather_core(gather_chips(after(g_home, *partials), *seen))
     slopes = [
         dot(chunk_of(g, h), down_weight, ((1,), (1,))).astype(BF16) for h in halves_of
     ]
     hiddens = []
     for h in halves_of:
         hidden = jax.nn.silu(finish_pre(totals[h])[0]).astype(BF16)
-        hidden, total = line(hidden, slopes[h])
+        hidden, total, _ = line(hidden, slopes[h])
         hiddens.append(hidden)
         slopes[h] = total.astype(BF16)
     updates = [dot(hidden, down_weight, ((1,), (0,))).astype(BF16) for hidden in hiddens]
@@ -256,7 +263,7 @@
     x = gather_node(x1_home)
     packed = []
     for h in halves_of:
-        slope, total = line(widen(slopes[h]), up_partial(chunk_of(x, h)))
+        slope, total, _ = line(widen(slopes[h]), up_partial(chunk_of(x, h)))
         slopes[h] = slope[:, :hidden_units]
         pre, factor = finish_pre(total)
         packed.append(
@@ -288,7 +295,7 @@
     others = swap_chips(update)
     x2_home = (x1_home.astype(F32) + sum_chips(update, others)).astype(BF16)
     result = exchange(x2_home)
-    total = scatter_chips(after(both, x2_home))
+    total = sum_chips(both, [after(other, x2_home) for other in swap_chips(both)])
     lanes = [take(half[:, hidden_units:], chip) for half in packed]
     factor = join_pair(jnp.concatenate(lanes, axis=0))
     inner = join_pair(total[:, cols:]) / (features * factor)

time: 272 us -> 271 us (level)
  starting transfers between devices: 148 us -> 142 us
  waiting for transfers between devices: 66.5 us -> 70.5 us
    ppermute x52, waiting for transfers between devices: 22.3 us -> 32.2 us  [pair_swap(): return lax.ppermute(block, 'local', pairs + [(t, s) for s, t in pairs])]
    ppermute x21, waiting for transfers between devices: 31.4 us -> 23.7 us  [chip_swap(): lax.ppermute(block, 'node', [(n, n ^ 2 * shift) for n in range(n_node)])]
    ppermute x52, starting transfers between devices: 113 us -> 109 us  [pair_swap(): return lax.ppermute(block, 'local', pairs + [(t, s) for s, t in pairs])]
  transfers between devices with their start and end apart: 84 -> 84, of which waited for: 32 -> 28; matrix products, arithmetic and copies ran while one was open for 10% -> 10% of each run, Pallas kernels for 3% -> 3%
where the time goes in v3:
time: 271 us; the launch traced here: 267 us
  starting transfers between devices  142 us (52%)
  waiting for transfers between devices  70.5 us (26%)
  matrix products  20 us (7%)
  other arithmetic  19.7 us (7%)
  Pallas kernels  6.77 us (2%)
  local copies, waits for them, and re-layouts  5.2 us (2%)
    ppermute x52, starting transfers between devices, pair_swap(): return lax.ppermute(block, 'local', pairs + [(t, s) for s, t in pairs])  109 us
    ppermute x52, waiting for transfers between devices, pair_swap(): return lax.ppermute(block, 'local', pairs + [(t, s) for s, t in pairs])  32.2 us
    ppermute x21, waiting for transfers between devices, chip_swap(): lax.ppermute(block, 'node', [(n, n ^ 2 * shift) for n in range(n_node)])  23.7 us
    ppermute x21, starting transfers between devices, chip_swap(): lax.ppermute(block, 'node', [(n, n ^ 2 * shift) for n in range(n_node)])  22.2 us
    dot_general x13, matrix products, dot(): lax.dot_general(left, right, (dims, ((), ())), preferred_element_type=F32)  20 us
    ppermute x3, waiting for transfers between devices, exchange(): return lax.ppermute(block, ('node', 'local'), swap)  11 us
    ppermute x3, starting transfers between devices, exchange(): return lax.ppermute(block, ('node', 'local'), swap)  10.5 us
    pallas_call x1, Pallas kernels, dequant_cols(): pl.pallas_call(scale_columns, grid=(rows // tile,), in_specs=[pl.BlockSpe...  6.77 us
  transfers between devices with their start and end apart: 84, of which 28 were waited for; matrix products, arithmetic and copies ran while one was open for 10% of the time, Pallas kernels for 3%

profile of v3, /device:TPU:2, one launch (start us, length us, event | category | flops | bytes accessed | tf_op | source)
XLA Modules:
  0.0 266.7 jit_solution(17610591987867995157)
XLA Ops:
  0.6 3.5 %collective-permute-start = (bf16[128,512]{1,0:T(8,128)(2,1)}, bf16[128,512]{1,0:T(8,128)(2,1)S(1)}, u32[]{:S(2)}, u32[]{:S(2)}) collective-permute-start(bf16[128,512]{1,0:T(8,128)(2,1)} %param.7), channel_id=1, source_target_pairs={{0,0},{1,8},{2,16},{3,24},{4,4},{5,12},{6,20},{7,28},{8,1},{9,9},{... | collective-permute-start | bytes 393224 | tf_op jit(solution)/shard_map/ppermute | solution.py:85
  5.0 3.3 %collective-permute-start.4 = (bf16[144,512]{1,0:T(8,128)(2,1)S(1)}, bf16[144,512]{1,0:T(8,128)(2,1)S(1)}, u32[]{:S(2)}, u32[]{:S(2)}) collective-permute-start(bf16[144,512]{1,0:T(8,128)(2,1)S(1)} %fusion.92), channel_id=1, source_target_pairs={{0,0},{1,8},{2,16},{3,24},{4,4},{5,12},{6,20},{7,28},{8,1},{9,9},{... | collective-permute-start | bytes 442376 | tf_op jit(solution)/shard_map/ppermute | solution.py:85
  10.0 6.8 %shard_map.86 = bf16[1792,1024]{1,0:T(8,128)(2,1)} custom-call(bf16[1792,1024]{1,0:T(8,128)(2,1)} %quanta_ref.1, bf16[1792,8]{1,0:T(8,128)(2,1)} %copy.26.scales_ref), custom_call_target="tpu_custom_call" | custom-call | flops 1835008 | bytes 7340032 | tf_op jit(solution)/shard_map/pallas_call | solution.py:34
  16.8 5.0 %collective-permute-done = bf16[128,512]{1,0:T(8,128)(2,1)S(1)} collective-permute-done((bf16[128,512]{1,0:T(8,128)(2,1)}, bf16[128,512]{1,0:T(8,128)(2,1)S(1)}, u32[]{:S(2)}, u32[]{:S(2)}) %collective-permute-start) | collective-permute-done | bytes 131104 | tf_op jit(solution)/shard_map/ppermute | solution.py:85
  21.9 3.5 %collective-permute-start.3 = (bf16[128,512]{1,0:T(8,128)(2,1)S(1)}, bf16[128,512]{1,0:T(8,128)(2,1)S(1)}, u32[]{:S(2)}, u32[]{:S(2)}) collective-permute-start(bf16[128,512]{1,0:T(8,128)(2,1)S(1)} %collective-permute-done), channel_id=1, source_target_pairs={{0,24},{4,28},{8,16},{12,20},{16,8},{20,12},{24,0},{28,4},{1,25},{... | collective-permute-start | bytes 393224 | tf_op jit(solution)/shard_map/ppermute | solution.py:91
  25.4 2.7 %collective-permute-done.1 = bf16[128,512]{1,0:T(8,128)(2,1)S(1)} collective-permute-done((bf16[128,512]{1,0:T(8,128)(2,1)S(1)}, bf16[128,512]{1,0:T(8,128)(2,1)S(1)}, u32[]{:S(2)}, u32[]{:S(2)}) %collective-permute-start.1) | collective-permute-done | bytes 131104 | tf_op jit(solution)/shard_map/ppermute | solution.py:91
  29.3 2.7 %fusion = bf16[1024,1792]{1,0:T(8,128)(2,1)S(1)} fusion(bf16[1024,1792]{1,0:T(8,128)(2,1)} %param.10, f32[8,1792]{1,0:T(8,128)S(1)} %convert_element_type.736), kind=kLoop, calls=%fused_computation.1 | loop fusion | flops 5505024 | bytes 7397376 | tf_op jit(solution)/shard_map/convert_element_type | solution.py:19
  39.3 2.1 collective-permute-start.7
  41.6 6.6 %collective-permute-done.14 = bf16[64,1920]{1,0:T(8,128)(2,1)S(1)} collective-permute-done((bf16[64,1920]{1,0:T(8,128)(2,1)S(1)}, bf16[64,1920]{1,0:T(8,128)(2,1)S(1)}, u32[]{:S(2)}, u32[]{:S(2)}) %collective-permute-start.14) | collective-permute-done | bytes 245792 | tf_op jit(solution)/shard_map/ppermute | solution.py:99
  48.9 4.7 %collective-permute-start.25 = (bf16[64,1920]{1,0:T(8,128)(2,1)S(1)}, bf16[64,1920]{1,0:T(8,128)(2,1)S(1)}, u32[]{:S(2)}, u32[]{:S(2)}) collective-permute-start(bf16[64,1920]{1,0:T(8,128)(2,1)S(1)} %fusion.91), channel_id=1, source_target_pairs={{0,1},{2,3},{1,0},{3,2},{4,5},{6,7},{5,4},{7,6},{8,9},{10,11},{9,8... | collective-permute-start | bytes 737288 | tf_op jit(solution)/shard_map/ppermute | solution.py:99
  54.6 4.5 %collective-permute-start.10 = (bf16[64,1920]{1,0:T(8,128)(2,1)S(1)}, bf16[64,1920]{1,0:T(8,128)(2,1)S(1)}, u32[]{:S(2)}, u32[]{:S(2)}) collective-permute-start(bf16[64,1920]{1,0:T(8,128)(2,1)S(1)} %fusion.90), channel_id=1, source_target_pairs={{0,1},{2,3},{1,0},{3,2},{4,5},{6,7},{5,4},{7,6},{8,9},{10,11},{9,8... | collective-permute-start | bytes 737288 | tf_op jit(solution)/shard_map/ppermute | solution.py:99
  59.9 2.8 %collective-permute-start.24 = (bf16[64,1920]{1,0:T(8,128)(2,1)S(1)}, bf16[64,1920]{1,0:T(8,128)(2,1)S(1)}, u32[]{:S(2)}, u32[]{:S(2)}) collective-permute-start(bf16[64,1920]{1,0:T(8,128)(2,1)S(1)} %get-tuple-element.74), channel_id=1, source_target_pairs={{0,1},{2,3},{1,0},{3,2},{4,5},{6,7},{5,4},{7,6},{8,9},{10,11},{9,8... | collective-permute-start | bytes 737288 | tf_op jit(solution)/shard_map/ppermute | solution.py:99
  62.7 3.0 %collective-permute-done.10 = bf16[64,1920]{1,0:T(8,128)(2,1)S(1)} collective-permute-done((bf16[64,1920]{1,0:T(8,128)(2,1)S(1)}, bf16[64,1920]{1,0:T(8,128)(2,1)S(1)}, u32[]{:S(2)}, u32[]{:S(2)}) %collective-permute-start.10) | collective-permute-done | bytes 245792 | tf_op jit(solution)/shard_map/ppermute | solution.py:99
  66.6 3.4 %collective-permute-start.9 = (bf16[64,1920]{1,0:T(8,128)(2,1)S(1)}, bf16[64,1920]{1,0:T(8,128)(2,1)S(1)}, u32[]{:S(2)}, u32[]{:S(2)}) collective-permute-start(bf16[64,1920]{1,0:T(8,128)(2,1)S(1)} %get-tuple-element.72), channel_id=1, source_target_pairs={{0,1},{2,3},{1,0},{3,2},{4,5},{6,7},{5,4},{7,6},{8,9},{10,11},{9,8... | collective-permute-start | bytes 737288 | tf_op jit(solution)/shard_map/ppermute | solution.py:99
  71.5 2.1 collective-permute-start.30
  74.3 2.5 collective-permute-done.9
  77.3 2.1 collective-permute-start.20
  83.7 4.7 %collective-permute-start.28 = (bf16[64,1792]{1,0:T(8,128)(2,1)S(1)}, bf16[64,1792]{1,0:T(8,128)(2,1)S(1)}, u32[]{:S(2)}, u32[]{:S(2)}) collective-permute-start(bf16[64,1792]{1,0:T(8,128)(2,1)S(1)} %get-tuple-element.87), channel_id=1, source_target_pairs={{0,1},{2,3},{1,0},{3,2},{4,5},{6,7},{5,4},{7,6},{8,9},{10,11},{9,8... | collective-permute-start | bytes 688136 | tf_op jit(solution)/shard_map/ppermute | solution.py:99
  89.2 3.4 %collective-permute-start.18 = (bf16[64,1792]{1,0:T(8,128)(2,1)S(1)}, bf16[64,1792]{1,0:T(8,128)(2,1)S(1)}, u32[]{:S(2)}, u32[]{:S(2)}) collective-permute-start(bf16[64,1792]{1,0:T(8,128)(2,1)S(1)} %get-tuple-element.83), channel_id=1, source_target_pairs={{0,1},{2,3},{1,0},{3,2},{4,5},{6,7},{5,4},{7,6},{8,9},{10,11},{9,8... | collective-permute-start | bytes 688136 | tf_op jit(solution)/shard_map/ppermute | solution.py:99
  95.1 5.4 %collective-permute-start.32 = (bf16[64,1792]{1,0:T(8,128)(2,1)S(1)}, bf16[64,1792]{1,0:T(8,128)(2,1)S(1)}, u32[]{:S(2)}, u32[]{:S(2)}) collective-permute-start(bf16[64,1792]{1,0:T(8,128)(2,1)S(1)} %get-tuple-element.84), channel_id=1, source_target_pairs={{0,1},{2,3},{1,0},{3,2},{4,5},{6,7},{5,4},{7,6},{8,9},{10,11},{9,8... | collective-permute-start | bytes 688136 | tf_op jit(solution)/shard_map/ppermute | solution.py:99
  101.5 4.1 %collective-permute-start.22 = (bf16[64,1792]{1,0:T(8,128)(2,1)S(1)}, bf16[64,1792]{1,0:T(8,128)(2,1)S(1)}, u32[]{:S(2)}, u32[]{:S(2)}) collective-permute-start(bf16[64,1792]{1,0:T(8,128)(2,1)S(1)} %get-tuple-element.80), channel_id=1, source_target_pairs={{0,1},{2,3},{1,0},{3,2},{4,5},{6,7},{5,4},{7,6},{8,9},{10,11},{9,8... | collective-permute-start | bytes 688136 | tf_op jit(solution)/shard_map/ppermute | solution.py:99
  107.1 2.5 collective-permute-done.22
  112.1 3.5 %collective-permute-start.56 = (bf16[64,1792]{1,0:T(8,128)(2,1)S(1)}, bf16[64,1792]{1,0:T(8,128)(2,1)S(1)}, u32[]{:S(2)}, u32[]{:S(2)}) collective-permute-start(bf16[64,1792]{1,0:T(8,128)(2,1)S(1)} %get-tuple-element.78), channel_id=1, source_target_pairs={{0,1},{2,3},{1,0},{3,2},{4,5},{6,7},{5,4},{7,6},{8,9},{10,11},{9,8... | collective-permute-start | bytes 688136 | tf_op jit(solution)/shard_map/ppermute | solution.py:99
  119.6 3.7 %collective-permute-done.36 = bf16[128,512]{1,0:T(8,128)(2,1)S(1)} collective-permute-done((bf16[128,512]{1,0:T(8,128)(2,1)S(1)}, bf16[128,512]{1,0:T(8,128)(2,1)S(1)}, u32[]{:S(2)}, u32[]{:S(2)}) %collective-permute-start.36) | collective-permute-done | bytes 131104 | tf_op jit(solution)/shard_map/ppermute | solution.py:91
  125.0 2.1 collective-permute-start.41
  129.6 2.8 %collective-permute-done.37 = bf16[128,512]{1,0:T(8,128)(2,1)S(1)} collective-permute-done((bf16[128,512]{1,0:T(8,128)(2,1)S(1)}, bf16[128,512]{1,0:T(8,128)(2,1)S(1)}, u32[]{:S(2)}, u32[]{:S(2)}) %collective-permute-start.37) | collective-permute-done | bytes 131104 | tf_op jit(solution)/shard_map/ppermute | solution.py:91
  132.8 3.0 %collective-permute-done.38 = bf16[128,512]{1,0:T(8,128)(2,1)S(1)} collective-permute-done((bf16[128,512]{1,0:T(8,128)(2,1)S(1)}, bf16[128,512]{1,0:T(8,128)(2,1)S(1)}, u32[]{:S(2)}, u32[]{:S(2)}) %collective-permute-start.38) | collective-permute-done | bytes 131104 | tf_op jit(solution)/shard_map/ppermute | solution.py:91
  135.8 3.5 %collective-permute-start.62 = (bf16[64,1920]{1,0:T(8,128)(2,1)S(1)}, bf16[64,1920]{1,0:T(8,128)(2,1)S(1)}, u32[]{:S(2)}, u32[]{:S(2)}) collective-permute-start(bf16[64,1920]{1,0:T(8,128)(2,1)S(1)} %pad.13), channel_id=1, source_target_pairs={{0,1},{2,3},{1,0},{3,2},{4,5},{6,7},{5,4},{7,6},{8,9},{10,11},{9,8... | collective-permute-start | bytes 737288 | tf_op jit(solution)/shard_map/ppermute | solution.py:99
  145.6 2.5 collective-permute-start.59
  149.9 5.0 %collective-permute-start.44 = (bf16[64,1920]{1,0:T(8,128)(2,1)S(1)}, bf16[64,1920]{1,0:T(8,128)(2,1)S(1)}, u32[]{:S(2)}, u32[]{:S(2)}) collective-permute-start(bf16[64,1920]{1,0:T(8,128)(2,1)S(1)} %get-tuple-element.65), channel_id=1, source_target_pairs={{0,1},{2,3},{1,0},{3,2},{4,5},{6,7},{5,4},{7,6},{8,9},{10,11},{9,8... | collective-permute-start | bytes 737288 | tf_op jit(solution)/shard_map/ppermute | solution.py:99
  155.7 6.6 %collective-permute-start.64 = (bf16[64,1920]{1,0:T(8,128)(2,1)S(1)}, bf16[64,1920]{1,0:T(8,128)(2,1)S(1)}, u32[]{:S(2)}, u32[]{:S(2)}) collective-permute-start(bf16[64,1920]{1,0:T(8,128)(2,1)S(1)} %get-tuple-element.69), channel_id=1, source_target_pairs={{0,1},{2,3},{1,0},{3,2},{4,5},{6,7},{5,4},{7,6},{8,9},{10,11},{9,8... | collective-permute-start | bytes 737288 | tf_op jit(solution)/shard_map/ppermute | solution.py:99
  163.1 4.4 %collective-permute-start.49 = (bf16[64,1920]{1,0:T(8,128)(2,1)S(1)}, bf16[64,1920]{1,0:T(8,128)(2,1)S(1)}, u32[]{:S(2)}, u32[]{:S(2)}) collective-permute-start(bf16[64,1920]{1,0:T(8,128)(2,1)S(1)} %get-tuple-element.62), channel_id=1, source_target_pairs={{0,1},{2,3},{1,0},{3,2},{4,5},{6,7},{5,4},{7,6},{8,9},{10,11},{9,8... | collective-permute-start | bytes 737288 | tf_op jit(solution)/shard_map/ppermute | solution.py:99
  169.9 4.1 %collective-permute-start.61 = (bf16[64,1920]{1,0:T(8,128)(2,1)}, bf16[64,1920]{1,0:T(8,128)(2,1)}, u32[]{:S(2)}, u32[]{:S(2)}) collective-permute-start(bf16[64,1920]{1,0:T(8,128)(2,1)} %get-tuple-element.66), channel_id=1, source_target_pairs={{0,1},{2,3},{1,0},{3,2},{4,5},{6,7},{5,4},{7,6},{8,9},{10,11},{9,8... | collective-permute-start | bytes 737288 | tf_op jit(solution)/shard_map/ppermute | solution.py:99
  174.9 3.0 %collective-permute-start.46 = (bf16[64,1920]{1,0:T(8,128)(2,1)S(1)}, bf16[64,1920]{1,0:T(8,128)(2,1)S(1)}, u32[]{:S(2)}, u32[]{:S(2)}) collective-permute-start(bf16[64,1920]{1,0:T(8,128)(2,1)S(1)} %get-tuple-element.60), channel_id=1, source_target_pairs={{0,1},{2,3},{1,0},{3,2},{4,5},{6,7},{5,4},{7,6},{8,9},{10,11},{9,8... | collective-permute-start | bytes 737288 | tf_op jit(solution)/shard_map/ppermute | solution.py:99
  178.8 4.5 %collective-permute-done.46 = bf16[64,1920]{1,0:T(8,128)(2,1)S(1)} collective-permute-done((bf16[64,1920]{1,0:T(8,128)(2,1)S(1)}, bf16[64,1920]{1,0:T(8,128)(2,1)S(1)}, u32[]{:S(2)}, u32[]{:S(2)}) %collective-permute-start.46) | collective-permute-done | bytes 245792 | tf_op jit(solution)/shard_map/ppermute | solution.py:99
  188.7 2.1 collective-permute-start.66
  192.2 5.6 %collective-permute-start.54 = (bf16[64,1920]{1,0:T(8,128)(2,1)}, bf16[64,1920]{1,0:T(8,128)(2,1)S(1)}, u32[]{:S(2)}, u32[]{:S(2)}) collective-permute-start(bf16[64,1920]{1,0:T(8,128)(2,1)} %collective-permute-done.53), channel_id=1, source_target_pairs={{0,1},{2,3},{1,0},{3,2},{4,5},{6,7},{5,4},{7,6},{8,9},{10,11},{9,8... | collective-permute-start | bytes 737288 | tf_op jit(solution)/shard_map/ppermute | solution.py:99
  199.0 3.0 %collective-permute-start.69 = (bf16[64,1920]{1,0:T(8,128)(2,1)S(1)}, bf16[64,1920]{1,0:T(8,128)(2,1)S(1)}, u32[]{:S(2)}, u32[]{:S(2)}) collective-permute-start(bf16[64,1920]{1,0:T(8,128)(2,1)S(1)} %collective-permute-done.68), channel_id=1, source_target_pairs={{0,1},{2,3},{1,0},{3,2},{4,5},{6,7},{5,4},{7,6},{8,9},{10,11},{9,8... | collective-permute-start | bytes 737288 | tf_op jit(solution)/shard_map/ppermute | solution.py:99
  201.9 2.9 %collective-permute-done.54 = bf16[64,1920]{1,0:T(8,128)(2,1)S(1)} collective-permute-done((bf16[64,1920]{1,0:T(8,128)(2,1)}, bf16[64,1920]{1,0:T(8,128)(2,1)S(1)}, u32[]{:S(2)}, u32[]{:S(2)}) %collective-permute-start.54) | collective-permute-done | bytes 245792 | tf_op jit(solution)/shard_map/ppermute | solution.py:99
  204.8 2.1 collective-permute-start.55
  207.0 3.0 %collective-permute-done.69 = bf16[64,1920]{1,0:T(8,128)(2,1)S(1)} collective-permute-done((bf16[64,1920]{1,0:T(8,128)(2,1)S(1)}, bf16[64,1920]{1,0:T(8,128)(2,1)S(1)}, u32[]{:S(2)}, u32[]{:S(2)}) %collective-permute-start.69) | collective-permute-done | bytes 245792 | tf_op jit(solution)/shard_map/ppermute | solution.py:99
  212.0 3.0 %collective-permute-done.55 = bf16[64,1920]{1,0:T(8,128)(2,1)S(1)} collective-permute-done((bf16[64,1920]{1,0:T(8,128)(2,1)S(1)}, bf16[64,1920]{1,0:T(8,128)(2,1)S(1)}, u32[]{:S(2)}, u32[]{:S(2)}) %collective-permute-start.55) | collective-permute-done | bytes 245792 | tf_op jit(solution)/shard_map/ppermute | solution.py:99
  235.8 2.5 collective-permute-done.73
  238.4 3.7 %collective-permute-start.75 = (bf16[128,512]{1,0:T(8,128)(2,1)S(1)}, bf16[128,512]{1,0:T(8,128)(2,1)S(1)}, u32[]{:S(2)}, u32[]{:S(2)}) collective-permute-start(bf16[128,512]{1,0:T(8,128)(2,1)S(1)} %fusion.79), channel_id=1, source_target_pairs={{0,0},{1,8},{2,16},{3,24},{4,4},{5,12},{6,20},{7,28},{8,1},{9,9},{... | collective-permute-start | bytes 393224 | tf_op jit(solution)/shard_map/ppermute | solution.py:85
  242.1 2.1 collective-permute-done.78
  245.1 6.0 %collective-permute-done.75 = bf16[128,512]{1,0:T(8,128)(2,1)S(1)} collective-permute-done((bf16[128,512]{1,0:T(8,128)(2,1)S(1)}, bf16[128,512]{1,0:T(8,128)(2,1)S(1)}, u32[]{:S(2)}, u32[]{:S(2)}) %collective-permute-start.75) | collective-permute-done | bytes 131104 | tf_op jit(solution)/shard_map/ppermute | solution.py:85
  251.6 3.0 %collective-permute-start.82 = (bf16[128,512]{1,0:T(8,128)(2,1)S(1)}, bf16[128,512]{1,0:T(8,128)(2,1)S(1)}, u32[]{:S(2)}, u32[]{:S(2)}) collective-permute-start(bf16[128,512]{1,0:T(8,128)(2,1)S(1)} %fusion.82), channel_id=1, source_target_pairs={{0,24},{4,28},{8,16},{12,20},{16,8},{20,12},{24,0},{28,4},{1,25},{... | collective-permute-start | bytes 393224 | tf_op jit(solution)/shard_map/ppermute | solution.py:91
  260.6 5.5 %convolution_convert_fusion = bf16[1792,1024]{1,0:T(8,128)(2,1)} fusion(bf16[256,1792]{1,0:T(8,128)(2,1)S(1)} %get-tuple-element.59, bf16[256,1792]{1,0:T(8,128)(2,1)S(1)} %get-tuple-element.57, bf16[256,1792]{1,0:T(8,128)(2,1)S(1)} %bitcast.355, bf16[256,1792]{1,0:T(8,128)(2,1)S(1)} %bitcast.357, bf16[512,1024]{1,0:T(8,128)(2,1)S(1)} %copy-done.5, ...), kind=kOutput, calls=%fused_computation.2 | convolution fusion | flops 3778805760 | bytes 9437184 | tf_op jit(solution)/shard_map/dot_general | solution.py:50
  (307 shorter events, 90.1 us)
Async XLA Ops:
  0.6 21.2 %collective-permute-start = (bf16[128,512]{1,0:T(8,128)(2,1)}, bf16[128,512]{1,0:T(8,128)(2,1)S(1)}, u32[]{:S(2)}, u32[]{:S(2)}) collective-permute-start(bf16[128,512]{1,0:T(8,128)(2,1)} %param.7), channel_id=1, source_target_pairs={{0,0},{1,8},{2,16},{3,24},{4,4},{5,12},{6,20},{7,28},{8,1},{9,9},{... | collective-permute-start | bytes 393224 | tf_op jit(solution)/shard_map/ppermute | solution.py:85
  5.0 20.4 %collective-permute-start.4 = (bf16[144,512]{1,0:T(8,128)(2,1)S(1)}, bf16[144,512]{1,0:T(8,128)(2,1)S(1)}, u32[]{:S(2)}, u32[]{:S(2)}) collective-permute-start(bf16[144,512]{1,0:T(8,128)(2,1)S(1)} %fusion.92), channel_id=1, source_target_pairs={{0,0},{1,8},{2,16},{3,24},{4,4},{5,12},{6,20},{7,28},{8,1},{9,9},{... | collective-permute-start | bytes 442376 | tf_op jit(solution)/shard_map/ppermute | solution.py:85
  35.3 13.6 %collective-permute-start.13 = (bf16[128,512]{1,0:T(8,128)(2,1)S(1)}, bf16[128,512]{1,0:T(8,128)(2,1)S(1)}, u32[]{:S(2)}, u32[]{:S(2)}) collective-permute-start(bf16[128,512]{1,0:T(8,128)(2,1)S(1)} %slice.274), channel_id=1, source_target_pairs={{0,8},{4,12},{8,0},{12,4},{16,24},{20,28},{24,16},{28,20},{1,9},{5... | collective-permute-start | bytes 393224 | tf_op jit(solution)/shard_map/ppermute | solution.py:91
  36.9 16.7 %collective-permute-start.15 = (bf16[128,512]{1,0:T(8,128)(2,1)S(1)}, bf16[128,512]{1,0:T(8,128)(2,1)S(1)}, u32[]{:S(2)}, u32[]{:S(2)}) collective-permute-start(bf16[128,512]{1,0:T(8,128)(2,1)S(1)} %slice.274), channel_id=1, source_target_pairs={{0,16},{4,20},{8,24},{12,28},{16,0},{20,4},{24,8},{28,12},{1,17},{... | collective-permute-start | bytes 393224 | tf_op jit(solution)/shard_map/ppermute | solution.py:91
  38.4 15.2 %collective-permute-start.16 = (bf16[128,512]{1,0:T(8,128)(2,1)S(1)}, bf16[128,512]{1,0:T(8,128)(2,1)S(1)}, u32[]{:S(2)}, u32[]{:S(2)}) collective-permute-start(bf16[128,512]{1,0:T(8,128)(2,1)S(1)} %slice.274), channel_id=1, source_target_pairs={{0,24},{4,28},{8,16},{12,20},{16,8},{20,12},{24,0},{28,4},{1,25},{... | collective-permute-start | bytes 393224 | tf_op jit(solution)/shard_map/ppermute | solution.py:91
  39.3 14.3 %collective-permute-start.7 = (bf16[64,1920]{1,0:T(8,128)(2,1)S(1)}, bf16[64,1920]{1,0:T(8,128)(2,1)S(1)}, u32[]{:S(2)}, u32[]{:S(2)}) collective-permute-start(bf16[64,1920]{1,0:T(8,128)(2,1)S(1)} %dynamic-slice_bitcast_fusion.1), channel_id=1, source_target_pairs={{0,1},{2,3},{1,0},{3,2},{4,5},{6,7},{5,4},{7,6},{8,9},{10,11},{9,8... | collective-permute-start | bytes 737288 | tf_op jit(solution)/shard_map/ppermute | solution.py:99
  48.2 10.8 %collective-permute-start.23 = (bf16[64,1920]{1,0:T(8,128)(2,1)S(1)}, bf16[64,1920]{1,0:T(8,128)(2,1)S(1)}, u32[]{:S(2)}, u32[]{:S(2)}) collective-permute-start(bf16[64,1920]{1,0:T(8,128)(2,1)S(1)} %fusion.54), channel_id=1, source_target_pairs={{1,2},{2,1},{5,6},{6,5},{9,10},{10,9},{13,14},{14,13},{17,18},{18,... | collective-permute-start | bytes 737288 | tf_op jit(solution)/shard_map/ppermute | solution.py:99
  48.9 10.1 %collective-permute-start.25 = (bf16[64,1920]{1,0:T(8,128)(2,1)S(1)}, bf16[64,1920]{1,0:T(8,128)(2,1)S(1)}, u32[]{:S(2)}, u32[]{:S(2)}) collective-permute-start(bf16[64,1920]{1,0:T(8,128)(2,1)S(1)} %fusion.91), channel_id=1, source_target_pairs={{0,1},{2,3},{1,0},{3,2},{4,5},{6,7},{5,4},{7,6},{8,9},{10,11},{9,8... | collective-permute-start | bytes 737288 | tf_op jit(solution)/shard_map/ppermute | solution.py:99
  53.7 26.4 %collective-permute-start.17 = (bf16[512,512]{1,0:T(8,128)(2,1)S(1)}, bf16[512,512]{1,0:T(8,128)(2,1)S(1)}, u32[]{:S(2)}, u32[]{:S(2)}) collective-permute-start(bf16[512,512]{1,0:T(8,128)(2,1)S(1)} %bitcast.349), channel_id=1, source_target_pairs={{0,4},{4,0},{8,12},{12,8},{16,20},{20,16},{24,28},{28,24},{1,5},{5... | collective-permute-start | bytes 1572872 | tf_op jit(solution)/shard_map/ppermute | solution.py:88
  54.6 11.2 %collective-permute-start.10 = (bf16[64,1920]{1,0:T(8,128)(2,1)S(1)}, bf16[64,1920]{1,0:T(8,128)(2,1)S(1)}, u32[]{:S(2)}, u32[]{:S(2)}) collective-permute-start(bf16[64,1920]{1,0:T(8,128)(2,1)S(1)} %fusion.90), channel_id=1, source_target_pairs={{0,1},{2,3},{1,0},{3,2},{4,5},{6,7},{5,4},{7,6},{8,9},{10,11},{9,8... | collective-permute-start | bytes 737288 | tf_op jit(solution)/shard_map/ppermute | solution.py:99
  59.2 10.8 %collective-permute-start.26 = (bf16[64,1920]{1,0:T(8,128)(2,1)S(1)}, bf16[64,1920]{1,0:T(8,128)(2,1)S(1)}, u32[]{:S(2)}, u32[]{:S(2)}) collective-permute-start(bf16[64,1920]{1,0:T(8,128)(2,1)S(1)} %get-tuple-element.75), channel_id=1, source_target_pairs={{1,2},{2,1},{5,6},{6,5},{9,10},{10,9},{13,14},{14,13},{17,18},{18,... | collective-permute-start | bytes 737288 | tf_op jit(solution)/shard_map/ppermute | solution.py:99
  59.9 11.2 %collective-permute-start.24 = (bf16[64,1920]{1,0:T(8,128)(2,1)S(1)}, bf16[64,1920]{1,0:T(8,128)(2,1)S(1)}, u32[]{:S(2)}, u32[]{:S(2)}) collective-permute-start(bf16[64,1920]{1,0:T(8,128)(2,1)S(1)} %get-tuple-element.74), channel_id=1, source_target_pairs={{0,1},{2,3},{1,0},{3,2},{4,5},{6,7},{5,4},{7,6},{8,9},{10,11},{9,8... | collective-permute-start | bytes 737288 | tf_op jit(solution)/shard_map/ppermute | solution.py:99
  66.6 10.2 %collective-permute-start.9 = (bf16[64,1920]{1,0:T(8,128)(2,1)S(1)}, bf16[64,1920]{1,0:T(8,128)(2,1)S(1)}, u32[]{:S(2)}, u32[]{:S(2)}) collective-permute-start(bf16[64,1920]{1,0:T(8,128)(2,1)S(1)} %get-tuple-element.72), channel_id=1, source_target_pairs={{0,1},{2,3},{1,0},{3,2},{4,5},{6,7},{5,4},{7,6},{8,9},{10,11},{9,8... | collective-permute-start | bytes 737288 | tf_op jit(solution)/shard_map/ppermute | solution.py:99
  71.5 11.3 %collective-permute-start.30 = (bf16[64,1792]{1,0:T(8,128)(2,1)S(1)}, bf16[64,1792]{1,0:T(8,128)(2,1)S(1)}, u32[]{:S(2)}, u32[]{:S(2)}) collective-permute-start(bf16[64,1792]{1,0:T(8,128)(2,1)S(1)} %get-tuple-element.49), channel_id=1, source_target_pairs={{0,1},{2,3},{1,0},{3,2},{4,5},{6,7},{5,4},{7,6},{8,9},{10,11},{9,8... | collective-permute-start | bytes 688136 | tf_op jit(solution)/shard_map/ppermute | solution.py:99
  77.3 11.0 %collective-permute-start.20 = (bf16[64,1792]{1,0:T(8,128)(2,1)S(1)}, bf16[64,1792]{1,0:T(8,128)(2,1)S(1)}, u32[]{:S(2)}, u32[]{:S(2)}) collective-permute-start(bf16[64,1792]{1,0:T(8,128)(2,1)S(1)} %get-tuple-element.47), channel_id=1, source_target_pairs={{0,1},{2,3},{1,0},{3,2},{4,5},{6,7},{5,4},{7,6},{8,9},{10,11},{9,8... | collective-permute-start | bytes 688136 | tf_op jit(solution)/shard_map/ppermute | solution.py:99
  83.0 9.6 %collective-permute-start.31 = (bf16[64,1792]{1,0:T(8,128)(2,1)S(1)}, bf16[64,1792]{1,0:T(8,128)(2,1)S(1)}, u32[]{:S(2)}, u32[]{:S(2)}) collective-permute-start(bf16[64,1792]{1,0:T(8,128)(2,1)S(1)} %get-tuple-element.86), channel_id=1, source_target_pairs={{1,2},{2,1},{5,6},{6,5},{9,10},{10,9},{13,14},{14,13},{17,18},{18,... | collective-permute-start | bytes 688136 | tf_op jit(solution)/shard_map/ppermute | solution.py:99
  83.7 10.6 %collective-permute-start.28 = (bf16[64,1792]{1,0:T(8,128)(2,1)S(1)}, bf16[64,1792]{1,0:T(8,128)(2,1)S(1)}, u32[]{:S(2)}, u32[]{:S(2)}) collective-permute-start(bf16[64,1792]{1,0:T(8,128)(2,1)S(1)} %get-tuple-element.87), channel_id=1, source_target_pairs={{0,1},{2,3},{1,0},{3,2},{4,5},{6,7},{5,4},{7,6},{8,9},{10,11},{9,8... | collective-permute-start | bytes 688136 | tf_op jit(solution)/shard_map/ppermute | solution.py:99
  88.5 12.0 %collective-permute-start.21 = (bf16[64,1792]{1,0:T(8,128)(2,1)S(1)}, bf16[64,1792]{1,0:T(8,128)(2,1)S(1)}, u32[]{:S(2)}, u32[]{:S(2)}) collective-permute-start(bf16[64,1792]{1,0:T(8,128)(2,1)S(1)} %get-tuple-element.82), channel_id=1, source_target_pairs={{1,2},{2,1},{5,6},{6,5},{9,10},{10,9},{13,14},{14,13},{17,18},{18,... | collective-permute-start | bytes 688136 | tf_op jit(solution)/shard_map/ppermute | solution.py:99
  89.2 11.3 %collective-permute-start.18 = (bf16[64,1792]{1,0:T(8,128)(2,1)S(1)}, bf16[64,1792]{1,0:T(8,128)(2,1)S(1)}, u32[]{:S(2)}, u32[]{:S(2)}) collective-permute-start(bf16[64,1792]{1,0:T(8,128)(2,1)S(1)} %get-tuple-element.83), channel_id=1, source_target_pairs={{0,1},{2,3},{1,0},{3,2},{4,5},{6,7},{5,4},{7,6},{8,9},{10,11},{9,8... | collective-permute-start | bytes 688136 | tf_op jit(solution)/shard_map/ppermute | solution.py:99
  94.4 11.2 %collective-permute-start.29 = (bf16[64,1792]{1,0:T(8,128)(2,1)S(1)}, bf16[64,1792]{1,0:T(8,128)(2,1)S(1)}, u32[]{:S(2)}, u32[]{:S(2)}) collective-permute-start(bf16[64,1792]{1,0:T(8,128)(2,1)S(1)} %get-tuple-element.85), channel_id=1, source_target_pairs={{1,2},{2,1},{5,6},{6,5},{9,10},{10,9},{13,14},{14,13},{17,18},{18,... | collective-permute-start | bytes 688136 | tf_op jit(solution)/shard_map/ppermute | solution.py:99
  95.1 10.5 %collective-permute-start.32 = (bf16[64,1792]{1,0:T(8,128)(2,1)S(1)}, bf16[64,1792]{1,0:T(8,128)(2,1)S(1)}, u32[]{:S(2)}, u32[]{:S(2)}) collective-permute-start(bf16[64,1792]{1,0:T(8,128)(2,1)S(1)} %get-tuple-element.84), channel_id=1, source_target_pairs={{0,1},{2,3},{1,0},{3,2},{4,5},{6,7},{5,4},{7,6},{8,9},{10,11},{9,8... | collective-permute-start | bytes 688136 | tf_op jit(solution)/shard_map/ppermute | solution.py:99
  111.5 17.2 %collective-permute-start.57 = (bf16[64,1792]{1,0:T(8,128)(2,1)S(1)}, bf16[64,1792]{1,0:T(8,128)(2,1)S(1)}, u32[]{:S(2)}, u32[]{:S(2)}) collective-permute-start(bf16[64,1792]{1,0:T(8,128)(2,1)S(1)} %get-tuple-element.79), channel_id=1, source_target_pairs={{1,2},{2,1},{5,6},{6,5},{9,10},{10,9},{13,14},{14,13},{17,18},{18,... | collective-permute-start | bytes 688136 | tf_op jit(solution)/shard_map/ppermute | solution.py:99
  112.1 16.5 %collective-permute-start.56 = (bf16[64,1792]{1,0:T(8,128)(2,1)S(1)}, bf16[64,1792]{1,0:T(8,128)(2,1)S(1)}, u32[]{:S(2)}, u32[]{:S(2)}) collective-permute-start(bf16[64,1792]{1,0:T(8,128)(2,1)S(1)} %get-tuple-element.78), channel_id=1, source_target_pairs={{0,1},{2,3},{1,0},{3,2},{4,5},{6,7},{5,4},{7,6},{8,9},{10,11},{9,8... | collective-permute-start | bytes 688136 | tf_op jit(solution)/shard_map/ppermute | solution.py:99
  123.3 16.1 %collective-permute-start.42 = (bf16[64,1792]{1,0:T(8,128)(2,1)S(1)}, bf16[64,1792]{1,0:T(8,128)(2,1)S(1)}, u32[]{:S(2)}, u32[]{:S(2)}) collective-permute-start(bf16[64,1792]{1,0:T(8,128)(2,1)S(1)} %get-tuple-element.77), channel_id=1, source_target_pairs={{1,2},{2,1},{5,6},{6,5},{9,10},{10,9},{13,14},{14,13},{17,18},{18,... | collective-permute-start | bytes 688136 | tf_op jit(solution)/shard_map/ppermute | solution.py:99
  125.0 14.4 %collective-permute-start.41 = (bf16[64,1792]{1,0:T(8,128)(2,1)S(1)}, bf16[64,1792]{1,0:T(8,128)(2,1)S(1)}, u32[]{:S(2)}, u32[]{:S(2)}) collective-permute-start(bf16[64,1792]{1,0:T(8,128)(2,1)S(1)} %get-tuple-element.76), channel_id=1, source_target_pairs={{0,1},{2,3},{1,0},{3,2},{4,5},{6,7},{5,4},{7,6},{8,9},{10,11},{9,8... | collective-permute-start | bytes 688136 | tf_op jit(solution)/shard_map/ppermute | solution.py:99
  128.8 15.4 %collective-permute-start.58 = (bf16[64,1920]{1,0:T(8,128)(2,1)S(1)}, bf16[64,1920]{1,0:T(8,128)(2,1)S(1)}, u32[]{:S(2)}, u32[]{:S(2)}) collective-permute-start(bf16[64,1920]{1,0:T(8,128)(2,1)S(1)} %pad.13), channel_id=1, source_target_pairs={{1,2},{2,1},{5,6},{6,5},{9,10},{10,9},{13,14},{14,13},{17,18},{18,... | collective-permute-start | bytes 737288 | tf_op jit(solution)/shard_map/ppermute | solution.py:99
  135.8 9.7 %collective-permute-start.62 = (bf16[64,1920]{1,0:T(8,128)(2,1)S(1)}, bf16[64,1920]{1,0:T(8,128)(2,1)S(1)}, u32[]{:S(2)}, u32[]{:S(2)}) collective-permute-start(bf16[64,1920]{1,0:T(8,128)(2,1)S(1)} %pad.13), channel_id=1, source_target_pairs={{0,1},{2,3},{1,0},{3,2},{4,5},{6,7},{5,4},{7,6},{8,9},{10,11},{9,8... | collective-permute-start | bytes 737288 | tf_op jit(solution)/shard_map/ppermute | solution.py:99
  139.5 9.5 %collective-permute-start.47 = (bf16[64,1920]{1,0:T(8,128)(2,1)S(1)}, bf16[64,1920]{1,0:T(8,128)(2,1)S(1)}, u32[]{:S(2)}, u32[]{:S(2)}) collective-permute-start(bf16[64,1920]{1,0:T(8,128)(2,1)S(1)} %pad.12), channel_id=1, source_target_pairs={{0,1},{2,3},{1,0},{3,2},{4,5},{6,7},{5,4},{7,6},{8,9},{10,11},{9,8... | collective-permute-start | bytes 737288 | tf_op jit(solution)/shard_map/ppermute | solution.py:99
  139.6 9.4 %collective-permute-start.43 = (bf16[64,1920]{1,0:T(8,128)(2,1)S(1)}, bf16[64,1920]{1,0:T(8,128)(2,1)S(1)}, u32[]{:S(2)}, u32[]{:S(2)}) collective-permute-start(bf16[64,1920]{1,0:T(8,128)(2,1)S(1)} %pad.12), channel_id=1, source_target_pairs={{1,2},{2,1},{5,6},{6,5},{9,10},{10,9},{13,14},{14,13},{17,18},{18,... | collective-permute-start | bytes 737288 | tf_op jit(solution)/shard_map/ppermute | solution.py:99
  145.6 9.2 %collective-permute-start.59 = (bf16[64,1920]{1,0:T(8,128)(2,1)S(1)}, bf16[64,1920]{1,0:T(8,128)(2,1)S(1)}, u32[]{:S(2)}, u32[]{:S(2)}) collective-permute-start(bf16[64,1920]{1,0:T(8,128)(2,1)S(1)} %get-tuple-element.70), channel_id=1, source_target_pairs={{0,1},{2,3},{1,0},{3,2},{4,5},{6,7},{5,4},{7,6},{8,9},{10,11},{9,8... | collective-permute-start | bytes 737288 | tf_op jit(solution)/shard_map/ppermute | solution.py:99
  149.2 13.1 %collective-permute-start.48 = (bf16[64,1920]{1,0:T(8,128)(2,1)S(1)}, bf16[64,1920]{1,0:T(8,128)(2,1)S(1)}, u32[]{:S(2)}, u32[]{:S(2)}) collective-permute-start(bf16[64,1920]{1,0:T(8,128)(2,1)S(1)} %get-tuple-element.64), channel_id=1, source_target_pairs={{1,2},{2,1},{5,6},{6,5},{9,10},{10,9},{13,14},{14,13},{17,18},{18,... | collective-permute-start | bytes 737288 | tf_op jit(solution)/shard_map/ppermute | solution.py:99
  149.9 12.4 %collective-permute-start.44 = (bf16[64,1920]{1,0:T(8,128)(2,1)S(1)}, bf16[64,1920]{1,0:T(8,128)(2,1)S(1)}, u32[]{:S(2)}, u32[]{:S(2)}) collective-permute-start(bf16[64,1920]{1,0:T(8,128)(2,1)S(1)} %get-tuple-element.65), channel_id=1, source_target_pairs={{0,1},{2,3},{1,0},{3,2},{4,5},{6,7},{5,4},{7,6},{8,9},{10,11},{9,8... | collective-permute-start | bytes 737288 | tf_op jit(solution)/shard_map/ppermute | solution.py:99
  155.0 12.5 %collective-permute-start.60 = (bf16[64,1920]{1,0:T(8,128)(2,1)S(1)}, bf16[64,1920]{1,0:T(8,128)(2,1)S(1)}, u32[]{:S(2)}, u32[]{:S(2)}) collective-permute-start(bf16[64,1920]{1,0:T(8,128)(2,1)S(1)} %get-tuple-element.68), channel_id=1, source_target_pairs={{1,2},{2,1},{5,6},{6,5},{9,10},{10,9},{13,14},{14,13},{17,18},{18,... | collective-permute-start | bytes 737288 | tf_op jit(solution)/shard_map/ppermute | solution.py:99
  155.7 11.8 %collective-permute-start.64 = (bf16[64,1920]{1,0:T(8,128)(2,1)S(1)}, bf16[64,1920]{1,0:T(8,128)(2,1)S(1)}, u32[]{:S(2)}, u32[]{:S(2)}) collective-permute-start(bf16[64,1920]{1,0:T(8,128)(2,1)S(1)} %get-tuple-element.69), channel_id=1, source_target_pairs={{0,1},{2,3},{1,0},{3,2},{4,5},{6,7},{5,4},{7,6},{8,9},{10,11},{9,8... | collective-permute-start | bytes 737288 | tf_op jit(solution)/shard_map/ppermute | solution.py:99
  162.4 11.6 %collective-permute-start.45 = (bf16[64,1920]{1,0:T(8,128)(2,1)S(1)}, bf16[64,1920]{1,0:T(8,128)(2,1)S(1)}, u32[]{:S(2)}, u32[]{:S(2)}) collective-permute-start(bf16[64,1920]{1,0:T(8,128)(2,1)S(1)} %get-tuple-element.63), channel_id=1, source_target_pairs={{1,2},{2,1},{5,6},{6,5},{9,10},{10,9},{13,14},{14,13},{17,18},{18,... | collective-permute-start | bytes 737288 | tf_op jit(solution)/shard_map/ppermute | solution.py:99
  163.1 10.9 %collective-permute-start.49 = (bf16[64,1920]{1,0:T(8,128)(2,1)S(1)}, bf16[64,1920]{1,0:T(8,128)(2,1)S(1)}, u32[]{:S(2)}, u32[]{:S(2)}) collective-permute-start(bf16[64,1920]{1,0:T(8,128)(2,1)S(1)} %get-tuple-element.62), channel_id=1, source_target_pairs={{0,1},{2,3},{1,0},{3,2},{4,5},{6,7},{5,4},{7,6},{8,9},{10,11},{9,8... | collective-permute-start | bytes 737288 | tf_op jit(solution)/shard_map/ppermute | solution.py:99
  168.5 18.6 %collective-permute-start.65 = (bf16[64,1920]{1,0:T(8,128)(2,1)}, bf16[64,1920]{1,0:T(8,128)(2,1)}, u32[]{:S(2)}, u32[]{:S(2)}) collective-permute-start(bf16[64,1920]{1,0:T(8,128)(2,1)} %get-tuple-element.67), channel_id=1, source_target_pairs={{1,2},{2,1},{5,6},{6,5},{9,10},{10,9},{13,14},{14,13},{17,18},{18,... | collective-permute-start | bytes 737288 | tf_op jit(solution)/shard_map/ppermute | solution.py:99
  169.9 17.2 %collective-permute-start.61 = (bf16[64,1920]{1,0:T(8,128)(2,1)}, bf16[64,1920]{1,0:T(8,128)(2,1)}, u32[]{:S(2)}, u32[]{:S(2)}) collective-permute-start(bf16[64,1920]{1,0:T(8,128)(2,1)} %get-tuple-element.66), channel_id=1, source_target_pairs={{0,1},{2,3},{1,0},{3,2},{4,5},{6,7},{5,4},{7,6},{8,9},{10,11},{9,8... | collective-permute-start | bytes 737288 | tf_op jit(solution)/shard_map/ppermute | solution.py:99
  188.7 9.2 %collective-permute-start.66 = (bf16[64,1920]{1,0:T(8,128)(2,1)S(1)}, bf16[64,1920]{1,0:T(8,128)(2,1)S(1)}, u32[]{:S(2)}, u32[]{:S(2)}) collective-permute-start(bf16[64,1920]{1,0:T(8,128)(2,1)S(1)} %concatenate.99), channel_id=1, source_target_pairs={{0,1},{2,3},{1,0},{3,2},{4,5},{6,7},{5,4},{7,6},{8,9},{10,11},{9,8... | collective-permute-start | bytes 737288 | tf_op jit(solution)/shard_map/ppermute | solution.py:99
  191.5 10.4 %collective-permute-start.52 = (bf16[64,1920]{1,0:T(8,128)(2,1)}, bf16[64,1920]{1,0:T(8,128)(2,1)S(1)}, u32[]{:S(2)}, u32[]{:S(2)}) collective-permute-start(bf16[64,1920]{1,0:T(8,128)(2,1)} %collective-permute-done.51), channel_id=1, source_target_pairs={{1,2},{2,1},{5,6},{6,5},{9,10},{10,9},{13,14},{14,13},{17,18},{18,... | collective-permute-start | bytes 737288 | tf_op jit(solution)/shard_map/ppermute | solution.py:99
  192.2 12.6 %collective-permute-start.54 = (bf16[64,1920]{1,0:T(8,128)(2,1)}, bf16[64,1920]{1,0:T(8,128)(2,1)S(1)}, u32[]{:S(2)}, u32[]{:S(2)}) collective-permute-start(bf16[64,1920]{1,0:T(8,128)(2,1)} %collective-permute-done.53), channel_id=1, source_target_pairs={{0,1},{2,3},{1,0},{3,2},{4,5},{6,7},{5,4},{7,6},{8,9},{10,11},{9,8... | collective-permute-start | bytes 737288 | tf_op jit(solution)/shard_map/ppermute | solution.py:99
  199.0 11.1 %collective-permute-start.69 = (bf16[64,1920]{1,0:T(8,128)(2,1)S(1)}, bf16[64,1920]{1,0:T(8,128)(2,1)S(1)}, u32[]{:S(2)}, u32[]{:S(2)}) collective-permute-start(bf16[64,1920]{1,0:T(8,128)(2,1)S(1)} %collective-permute-done.68), channel_id=1, source_target_pairs={{0,1},{2,3},{1,0},{3,2},{4,5},{6,7},{5,4},{7,6},{8,9},{10,11},{9,8... | collective-permute-start | bytes 737288 | tf_op jit(solution)/shard_map/ppermute | solution.py:99
  204.8 10.3 %collective-permute-start.55 = (bf16[64,1920]{1,0:T(8,128)(2,1)S(1)}, bf16[64,1920]{1,0:T(8,128)(2,1)S(1)}, u32[]{:S(2)}, u32[]{:S(2)}) collective-permute-start(bf16[64,1920]{1,0:T(8,128)(2,1)S(1)} %collective-permute-done.52), channel_id=1, source_target_pairs={{0,1},{2,3},{1,0},{3,2},{4,5},{6,7},{5,4},{7,6},{8,9},{10,11},{9,8... | collective-permute-start | bytes 737288 | tf_op jit(solution)/shard_map/ppermute | solution.py:99
  210.0 10.6 %collective-permute-start.70 = (bf16[64,1920]{1,0:T(8,128)(2,1)S(1)}, bf16[64,1920]{1,0:T(8,128)(2,1)S(1)}, u32[]{:S(2)}, u32[]{:S(2)}) collective-permute-start(bf16[64,1920]{1,0:T(8,128)(2,1)S(1)} %collective-permute-done.67), channel_id=1, source_target_pairs={{0,1},{2,3},{1,0},{3,2},{4,5},{6,7},{5,4},{7,6},{8,9},{10,11},{9,8... | collective-permute-start | bytes 737288 | tf_op jit(solution)/shard_map/ppermute | solution.py:99
  229.0 9.3 %collective-permute-start.73 = (bf16[128,512]{1,0:T(8,128)(2,1)S(1)}, bf16[128,512]{1,0:T(8,128)(2,1)S(1)}, u32[]{:S(2)}, u32[]{:S(2)}) collective-permute-start(bf16[128,512]{1,0:T(8,128)(2,1)S(1)} %bitcast.377), channel_id=1, source_target_pairs={{0,16},{4,20},{8,24},{12,28},{16,0},{20,4},{24,8},{28,12},{1,17},{... | collective-permute-start | bytes 393224 | tf_op jit(solution)/shard_map/ppermute | solution.py:91
  232.0 10.1 %collective-permute-start.79 = (bf16[128,640]{1,0:T(8,128)(2,1)S(1)}, bf16[128,640]{1,0:T(8,128)(2,1)S(1)}, u32[]{:S(2)}, u32[]{:S(2)}) collective-permute-start(bf16[128,640]{1,0:T(8,128)(2,1)S(1)} %bitcast.363), channel_id=1, source_target_pairs={{0,24},{4,28},{8,16},{12,20},{16,8},{20,12},{24,0},{28,4},{1,25},{... | collective-permute-start | bytes 491528 | tf_op jit(solution)/shard_map/ppermute | solution.py:91
  232.9 11.4 %collective-permute-start.78 = (bf16[128,640]{1,0:T(8,128)(2,1)S(1)}, bf16[128,640]{1,0:T(8,128)(2,1)S(1)}, u32[]{:S(2)}, u32[]{:S(2)}) collective-permute-start(bf16[128,640]{1,0:T(8,128)(2,1)S(1)} %bitcast.362), channel_id=1, source_target_pairs={{0,16},{4,20},{8,24},{12,28},{16,0},{20,4},{24,8},{28,12},{1,17},{... | collective-permute-start | bytes 491528 | tf_op jit(solution)/shard_map/ppermute | solution.py:91
  238.4 12.7 %collective-permute-start.75 = (bf16[128,512]{1,0:T(8,128)(2,1)S(1)}, bf16[128,512]{1,0:T(8,128)(2,1)S(1)}, u32[]{:S(2)}, u32[]{:S(2)}) collective-permute-start(bf16[128,512]{1,0:T(8,128)(2,1)S(1)} %fusion.79), channel_id=1, source_target_pairs={{0,0},{1,8},{2,16},{3,24},{4,4},{5,12},{6,20},{7,28},{8,1},{9,9},{... | collective-permute-start | bytes 393224 | tf_op jit(solution)/shard_map/ppermute | solution.py:85
  (49 other events, 442.8 us)

commit v4 on v1

--- a/solution.py
+++ b/solution.py
@@ -288,7 +288,7 @@
     others = swap_chips(update)
     x2_home = (x1_home.astype(F32) + sum_chips(update, others)).astype(BF16)
     result = exchange(x2_home)
-    total = scatter_chips(after(both, x2_home))
+    total = sum_chips(both, [after(other, x2_home) for other in swap_chips(both)])
     lanes = [take(half[:, hidden_units:], chip) for half in packed]
     factor = join_pair(jnp.concatenate(lanes, axis=0))
     inner = join_pair(total[:, cols:]) / (features * factor)

time: 272 us -> 270 us (level)
  waiting for transfers between devices: 66.5 us -> 63.4 us
    ppermute x21, waiting for transfers between devices: 31.4 us -> 25.7 us  [chip_swap(): lax.ppermute(block, 'node', [(n, n ^ 2 * shift) for n in range(n_node)])]
  transfers between devices with their start and end apart: 84 -> 84, of which waited for: 32 -> 30; matrix products, arithmetic and copies ran while one was open for 10% -> 11% of each run, Pallas kernels for 3% -> 3%
where the time goes in v4:
time: 270 us; the launch traced here: 266 us
  starting transfers between devices  148 us (55%)
  waiting for transfers between devices  63.4 us (23%)
  matrix products  20.1 us (7%)
  other arithmetic  19.7 us (7%)
  Pallas kernels  6.77 us (3%)
  local copies, waits for them, and re-layouts  5.19 us (2%)
    ppermute x52, starting transfers between devices, pair_swap(): return lax.ppermute(block, 'local', pairs + [(t, s) for s, t in pairs])  113 us
    ppermute x21, waiting for transfers between devices, chip_swap(): lax.ppermute(block, 'node', [(n, n ^ 2 * shift) for n in range(n_node)])  25.7 us
    ppermute x21, starting transfers between devices, chip_swap(): lax.ppermute(block, 'node', [(n, n ^ 2 * shift) for n in range(n_node)])  23.4 us
    ppermute x52, waiting for transfers between devices, pair_swap(): return lax.ppermute(block, 'local', pairs + [(t, s) for s, t in pairs])  22.3 us
    dot_general x13, matrix products, dot(): lax.dot_general(left, right, (dims, ((), ())), preferred_element_type=F32)  20.1 us
    ppermute x3, waiting for transfers between devices, exchange(): return lax.ppermute(block, ('node', 'local'), swap)  11.9 us
    ppermute x3, starting transfers between devices, exchange(): return lax.ppermute(block, ('node', 'local'), swap)  11.3 us
    pallas_call x1, Pallas kernels, dequant_cols(): pl.pallas_call(scale_columns, grid=(rows // tile,), in_specs=[pl.BlockSpe...  6.77 us
  transfers between devices with their start and end apart: 84, of which 30 were waited for; matrix products, arithmetic and copies ran while one was open for 11% of the time, Pallas kernels for 3%

profile of v4, /device:TPU:2, one launch (start us, length us, event | category | flops | bytes accessed | tf_op | source)
XLA Modules:
  0.0 265.9 jit_solution(17670970408765924936)
XLA Ops:
  0.6 3.5 %collective-permute-start = (bf16[128,512]{1,0:T(8,128)(2,1)}, bf16[128,512]{1,0:T(8,128)(2,1)S(1)}, u32[]{:S(2)}, u32[]{:S(2)}) collective-permute-start(bf16[128,512]{1,0:T(8,128)(2,1)} %param.7), channel_id=1, source_target_pairs={{0,0},{1,8},{2,16},{3,24},{4,4},{5,12},{6,20},{7,28},{8,1},{9,9},{... | collective-permute-start | bytes 393224 | tf_op jit(solution)/shard_map/ppermute | solution.py:85
  5.0 3.3 %collective-permute-start.4 = (bf16[144,512]{1,0:T(8,128)(2,1)S(1)}, bf16[144,512]{1,0:T(8,128)(2,1)S(1)}, u32[]{:S(2)}, u32[]{:S(2)}) collective-permute-start(bf16[144,512]{1,0:T(8,128)(2,1)S(1)} %fusion.92), channel_id=1, source_target_pairs={{0,0},{1,8},{2,16},{3,24},{4,4},{5,12},{6,20},{7,28},{8,1},{9,9},{... | collective-permute-start | bytes 442376 | tf_op jit(solution)/shard_map/ppermute | solution.py:85
  10.0 6.8 %shard_map.86 = bf16[1792,1024]{1,0:T(8,128)(2,1)} custom-call(bf16[1792,1024]{1,0:T(8,128)(2,1)} %quanta_ref.1, bf16[1792,8]{1,0:T(8,128)(2,1)} %copy.26.scales_ref), custom_call_target="tpu_custom_call" | custom-call | flops 1835008 | bytes 7340032 | tf_op jit(solution)/shard_map/pallas_call | solution.py:34
  16.8 5.0 %collective-permute-done = bf16[128,512]{1,0:T(8,128)(2,1)S(1)} collective-permute-done((bf16[128,512]{1,0:T(8,128)(2,1)}, bf16[128,512]{1,0:T(8,128)(2,1)S(1)}, u32[]{:S(2)}, u32[]{:S(2)}) %collective-permute-start) | collective-permute-done | bytes 131104 | tf_op jit(solution)/shard_map/ppermute | solution.py:85
  21.9 3.5 %collective-permute-start.3 = (bf16[128,512]{1,0:T(8,128)(2,1)S(1)}, bf16[128,512]{1,0:T(8,128)(2,1)S(1)}, u32[]{:S(2)}, u32[]{:S(2)}) collective-permute-start(bf16[128,512]{1,0:T(8,128)(2,1)S(1)} %collective-permute-done), channel_id=1, source_target_pairs={{0,24},{4,28},{8,16},{12,20},{16,8},{20,12},{24,0},{28,4},{1,25},{... | collective-permute-start | bytes 393224 | tf_op jit(solution)/shard_map/ppermute | solution.py:91
  25.4 2.7 %collective-permute-done.1 = bf16[128,512]{1,0:T(8,128)(2,1)S(1)} collective-permute-done((bf16[128,512]{1,0:T(8,128)(2,1)S(1)}, bf16[128,512]{1,0:T(8,128)(2,1)S(1)}, u32[]{:S(2)}, u32[]{:S(2)}) %collective-permute-start.1) | collective-permute-done | bytes 131104 | tf_op jit(solution)/shard_map/ppermute | solution.py:91
  29.3 2.7 %fusion = bf16[1024,1792]{1,0:T(8,128)(2,1)S(1)} fusion(bf16[1024,1792]{1,0:T(8,128)(2,1)} %param.10, f32[8,1792]{1,0:T(8,128)S(1)} %convert_element_type.736), kind=kLoop, calls=%fused_computation.1 | loop fusion | flops 5505024 | bytes 7397376 | tf_op jit(solution)/shard_map/convert_element_type | solution.py:19
  39.4 2.0 collective-permute-start.7
  41.6 2.4 collective-permute-done.14
  45.5 2.8 %collective-permute-done.22 = bf16[64,1920]{1,0:T(8,128)(2,1)S(1)} collective-permute-done((bf16[64,1920]{1,0:T(8,128)(2,1)S(1)}, bf16[64,1920]{1,0:T(8,128)(2,1)S(1)}, u32[]{:S(2)}, u32[]{:S(2)}) %collective-permute-start.22) | collective-permute-done | bytes 245792 | tf_op jit(solution)/shard_map/ppermute | solution.py:99
  49.1 4.7 %collective-permute-start.25 = (bf16[64,1920]{1,0:T(8,128)(2,1)S(1)}, bf16[64,1920]{1,0:T(8,128)(2,1)S(1)}, u32[]{:S(2)}, u32[]{:S(2)}) collective-permute-start(bf16[64,1920]{1,0:T(8,128)(2,1)S(1)} %fusion.91), channel_id=1, source_target_pairs={{0,1},{2,3},{1,0},{3,2},{4,5},{6,7},{5,4},{7,6},{8,9},{10,11},{9,8... | collective-permute-start | bytes 737288 | tf_op jit(solution)/shard_map/ppermute | solution.py:99
  54.5 4.5 %collective-permute-start.10 = (bf16[64,1920]{1,0:T(8,128)(2,1)S(1)}, bf16[64,1920]{1,0:T(8,128)(2,1)S(1)}, u32[]{:S(2)}, u32[]{:S(2)}) collective-permute-start(bf16[64,1920]{1,0:T(8,128)(2,1)S(1)} %fusion.90), channel_id=1, source_target_pairs={{0,1},{2,3},{1,0},{3,2},{4,5},{6,7},{5,4},{7,6},{8,9},{10,11},{9,8... | collective-permute-start | bytes 737288 | tf_op jit(solution)/shard_map/ppermute | solution.py:99
  60.1 5.0 %collective-permute-start.24 = (bf16[64,1920]{1,0:T(8,128)(2,1)S(1)}, bf16[64,1920]{1,0:T(8,128)(2,1)S(1)}, u32[]{:S(2)}, u32[]{:S(2)}) collective-permute-start(bf16[64,1920]{1,0:T(8,128)(2,1)S(1)} %get-tuple-element.68), channel_id=1, source_target_pairs={{0,1},{2,3},{1,0},{3,2},{4,5},{6,7},{5,4},{7,6},{8,9},{10,11},{9,8... | collective-permute-start | bytes 737288 | tf_op jit(solution)/shard_map/ppermute | solution.py:99
  65.9 4.2 %collective-permute-start.9 = (bf16[64,1920]{1,0:T(8,128)(2,1)S(1)}, bf16[64,1920]{1,0:T(8,128)(2,1)S(1)}, u32[]{:S(2)}, u32[]{:S(2)}) collective-permute-start(bf16[64,1920]{1,0:T(8,128)(2,1)S(1)} %get-tuple-element.66), channel_id=1, source_target_pairs={{0,1},{2,3},{1,0},{3,2},{4,5},{6,7},{5,4},{7,6},{8,9},{10,11},{9,8... | collective-permute-start | bytes 737288 | tf_op jit(solution)/shard_map/ppermute | solution.py:99
  75.1 1.8 collective-permute-done.9
  77.4 2.3 collective-permute-start.19
  82.7 6.0 %collective-permute-start.28 = (bf16[64,1792]{1,0:T(8,128)(2,1)S(1)}, bf16[64,1792]{1,0:T(8,128)(2,1)S(1)}, u32[]{:S(2)}, u32[]{:S(2)}) collective-permute-start(bf16[64,1792]{1,0:T(8,128)(2,1)S(1)} %get-tuple-element.81), channel_id=1, source_target_pairs={{0,1},{2,3},{1,0},{3,2},{4,5},{6,7},{5,4},{7,6},{8,9},{10,11},{9,8... | collective-permute-start | bytes 688136 | tf_op jit(solution)/shard_map/ppermute | solution.py:99
  89.6 4.1 %collective-permute-start.17 = (bf16[64,1792]{1,0:T(8,128)(2,1)S(1)}, bf16[64,1792]{1,0:T(8,128)(2,1)S(1)}, u32[]{:S(2)}, u32[]{:S(2)}) collective-permute-start(bf16[64,1792]{1,0:T(8,128)(2,1)S(1)} %get-tuple-element.77), channel_id=1, source_target_pairs={{0,1},{2,3},{1,0},{3,2},{4,5},{6,7},{5,4},{7,6},{8,9},{10,11},{9,8... | collective-permute-start | bytes 688136 | tf_op jit(solution)/shard_map/ppermute | solution.py:99
  94.5 4.2 %collective-permute-start.32 = (bf16[64,1792]{1,0:T(8,128)(2,1)S(1)}, bf16[64,1792]{1,0:T(8,128)(2,1)S(1)}, u32[]{:S(2)}, u32[]{:S(2)}) collective-permute-start(bf16[64,1792]{1,0:T(8,128)(2,1)S(1)} %get-tuple-element.78), channel_id=1, source_target_pairs={{0,1},{2,3},{1,0},{3,2},{4,5},{6,7},{5,4},{7,6},{8,9},{10,11},{9,8... | collective-permute-start | bytes 688136 | tf_op jit(solution)/shard_map/ppermute | solution.py:99
  100.1 4.3 %collective-permute-start.21 = (bf16[64,1792]{1,0:T(8,128)(2,1)S(1)}, bf16[64,1792]{1,0:T(8,128)(2,1)S(1)}, u32[]{:S(2)}, u32[]{:S(2)}) collective-permute-start(bf16[64,1792]{1,0:T(8,128)(2,1)S(1)} %get-tuple-element.74), channel_id=1, source_target_pairs={{0,1},{2,3},{1,0},{3,2},{4,5},{6,7},{5,4},{7,6},{8,9},{10,11},{9,8... | collective-permute-start | bytes 688136 | tf_op jit(solution)/shard_map/ppermute | solution.py:99
  106.0 2.4 collective-permute-done.21
  111.0 4.0 %collective-permute-start.56 = (bf16[64,1792]{1,0:T(8,128)(2,1)S(1)}, bf16[64,1792]{1,0:T(8,128)(2,1)S(1)}, u32[]{:S(2)}, u32[]{:S(2)}) collective-permute-start(bf16[64,1792]{1,0:T(8,128)(2,1)S(1)} %get-tuple-element.72), channel_id=1, source_target_pairs={{0,1},{2,3},{1,0},{3,2},{4,5},{6,7},{5,4},{7,6},{8,9},{10,11},{9,8... | collective-permute-start | bytes 688136 | tf_op jit(solution)/shard_map/ppermute | solution.py:99
  116.0 2.3 collective-permute-start.35
  119.0 3.6 %collective-permute-done.36 = bf16[128,512]{1,0:T(8,128)(2,1)S(1)} collective-permute-done((bf16[128,512]{1,0:T(8,128)(2,1)S(1)}, bf16[128,512]{1,0:T(8,128)(2,1)S(1)}, u32[]{:S(2)}, u32[]{:S(2)}) %collective-permute-start.36) | collective-permute-done | bytes 131104 | tf_op jit(solution)/shard_map/ppermute | solution.py:91
  128.4 2.7 %collective-permute-done.37 = bf16[128,512]{1,0:T(8,128)(2,1)S(1)} collective-permute-done((bf16[128,512]{1,0:T(8,128)(2,1)S(1)}, bf16[128,512]{1,0:T(8,128)(2,1)S(1)}, u32[]{:S(2)}, u32[]{:S(2)}) %collective-permute-start.37) | collective-permute-done | bytes 131104 | tf_op jit(solution)/shard_map/ppermute | solution.py:91
  131.2 3.6 %collective-permute-done.38 = bf16[128,512]{1,0:T(8,128)(2,1)S(1)} collective-permute-done((bf16[128,512]{1,0:T(8,128)(2,1)S(1)}, bf16[128,512]{1,0:T(8,128)(2,1)S(1)}, u32[]{:S(2)}, u32[]{:S(2)}) %collective-permute-start.38) | collective-permute-done | bytes 131104 | tf_op jit(solution)/shard_map/ppermute | solution.py:91
  134.7 3.5 %collective-permute-start.62 = (bf16[64,1920]{1,0:T(8,128)(2,1)S(1)}, bf16[64,1920]{1,0:T(8,128)(2,1)S(1)}, u32[]{:S(2)}, u32[]{:S(2)}) collective-permute-start(bf16[64,1920]{1,0:T(8,128)(2,1)S(1)} %pad.13), channel_id=1, source_target_pairs={{0,1},{2,3},{1,0},{3,2},{4,5},{6,7},{5,4},{7,6},{8,9},{10,11},{9,8... | collective-permute-start | bytes 737288 | tf_op jit(solution)/shard_map/ppermute | solution.py:99
  144.6 2.5 collective-permute-start.59
  148.8 4.8 %collective-permute-start.44 = (bf16[64,1920]{1,0:T(8,128)(2,1)S(1)}, bf16[64,1920]{1,0:T(8,128)(2,1)S(1)}, u32[]{:S(2)}, u32[]{:S(2)}) collective-permute-start(bf16[64,1920]{1,0:T(8,128)(2,1)S(1)} %get-tuple-element.59), channel_id=1, source_target_pairs={{0,1},{2,3},{1,0},{3,2},{4,5},{6,7},{5,4},{7,6},{8,9},{10,11},{9,8... | collective-permute-start | bytes 737288 | tf_op jit(solution)/shard_map/ppermute | solution.py:99
  154.5 6.5 %collective-permute-start.64 = (bf16[64,1920]{1,0:T(8,128)(2,1)S(1)}, bf16[64,1920]{1,0:T(8,128)(2,1)S(1)}, u32[]{:S(2)}, u32[]{:S(2)}) collective-permute-start(bf16[64,1920]{1,0:T(8,128)(2,1)S(1)} %get-tuple-element.63), channel_id=1, source_target_pairs={{0,1},{2,3},{1,0},{3,2},{4,5},{6,7},{5,4},{7,6},{8,9},{10,11},{9,8... | collective-permute-start | bytes 737288 | tf_op jit(solution)/shard_map/ppermute | solution.py:99
  161.9 4.4 %collective-permute-start.49 = (bf16[64,1920]{1,0:T(8,128)(2,1)S(1)}, bf16[64,1920]{1,0:T(8,128)(2,1)S(1)}, u32[]{:S(2)}, u32[]{:S(2)}) collective-permute-start(bf16[64,1920]{1,0:T(8,128)(2,1)S(1)} %get-tuple-element.56), channel_id=1, source_target_pairs={{0,1},{2,3},{1,0},{3,2},{4,5},{6,7},{5,4},{7,6},{8,9},{10,11},{9,8... | collective-permute-start | bytes 737288 | tf_op jit(solution)/shard_map/ppermute | solution.py:99
  168.6 4.1 %collective-permute-start.61 = (bf16[64,1920]{1,0:T(8,128)(2,1)}, bf16[64,1920]{1,0:T(8,128)(2,1)}, u32[]{:S(2)}, u32[]{:S(2)}) collective-permute-start(bf16[64,1920]{1,0:T(8,128)(2,1)} %get-tuple-element.60), channel_id=1, source_target_pairs={{0,1},{2,3},{1,0},{3,2},{4,5},{6,7},{5,4},{7,6},{8,9},{10,11},{9,8... | collective-permute-start | bytes 737288 | tf_op jit(solution)/shard_map/ppermute | solution.py:99
  173.6 3.0 %collective-permute-start.46 = (bf16[64,1920]{1,0:T(8,128)(2,1)S(1)}, bf16[64,1920]{1,0:T(8,128)(2,1)S(1)}, u32[]{:S(2)}, u32[]{:S(2)}) collective-permute-start(bf16[64,1920]{1,0:T(8,128)(2,1)S(1)} %get-tuple-element.54), channel_id=1, source_target_pairs={{0,1},{2,3},{1,0},{3,2},{4,5},{6,7},{5,4},{7,6},{8,9},{10,11},{9,8... | collective-permute-start | bytes 737288 | tf_op jit(solution)/shard_map/ppermute | solution.py:99
  177.6 4.9 %collective-permute-done.46 = bf16[64,1920]{1,0:T(8,128)(2,1)S(1)} collective-permute-done((bf16[64,1920]{1,0:T(8,128)(2,1)S(1)}, bf16[64,1920]{1,0:T(8,128)(2,1)S(1)}, u32[]{:S(2)}, u32[]{:S(2)}) %collective-permute-start.46) | collective-permute-done | bytes 245792 | tf_op jit(solution)/shard_map/ppermute | solution.py:99
  183.0 1.9 collective-permute-start.51
  187.9 1.8 collective-permute-start.66
  191.6 4.4 %collective-permute-start.54 = (bf16[64,1920]{1,0:T(8,128)(2,1)}, bf16[64,1920]{1,0:T(8,128)(2,1)S(1)}, u32[]{:S(2)}, u32[]{:S(2)}) collective-permute-start(bf16[64,1920]{1,0:T(8,128)(2,1)} %collective-permute-done.53), channel_id=1, source_target_pairs={{0,1},{2,3},{1,0},{3,2},{4,5},{6,7},{5,4},{7,6},{8,9},{10,11},{9,8... | collective-permute-start | bytes 737288 | tf_op jit(solution)/shard_map/ppermute | solution.py:99
  197.1 3.7 %collective-permute-start.69 = (bf16[64,1920]{1,0:T(8,128)(2,1)S(1)}, bf16[64,1920]{1,0:T(8,128)(2,1)S(1)}, u32[]{:S(2)}, u32[]{:S(2)}) collective-permute-start(bf16[64,1920]{1,0:T(8,128)(2,1)S(1)} %collective-permute-done.68), channel_id=1, source_target_pairs={{0,1},{2,3},{1,0},{3,2},{4,5},{6,7},{5,4},{7,6},{8,9},{10,11},{9,8... | collective-permute-start | bytes 737288 | tf_op jit(solution)/shard_map/ppermute | solution.py:99
  200.8 1.9 collective-permute-done.54
  202.7 3.3 %collective-permute-start.55 = (bf16[64,1920]{1,0:T(8,128)(2,1)S(1)}, bf16[64,1920]{1,0:T(8,128)(2,1)S(1)}, u32[]{:S(2)}, u32[]{:S(2)}) collective-permute-start(bf16[64,1920]{1,0:T(8,128)(2,1)S(1)} %collective-permute-done.52), channel_id=1, source_target_pairs={{0,1},{2,3},{1,0},{3,2},{4,5},{6,7},{5,4},{7,6},{8,9},{10,11},{9,8... | collective-permute-start | bytes 737288 | tf_op jit(solution)/shard_map/ppermute | solution.py:99
  208.0 2.3 collective-permute-start.70
  210.2 3.0 %collective-permute-done.55 = bf16[64,1920]{1,0:T(8,128)(2,1)S(1)} collective-permute-done((bf16[64,1920]{1,0:T(8,128)(2,1)S(1)}, bf16[64,1920]{1,0:T(8,128)(2,1)S(1)}, u32[]{:S(2)}, u32[]{:S(2)}) %collective-permute-start.55) | collective-permute-done | bytes 245792 | tf_op jit(solution)/shard_map/ppermute | solution.py:99
  236.6 4.6 %collective-permute-start.75 = (bf16[128,512]{1,0:T(8,128)(2,1)S(1)}, bf16[128,512]{1,0:T(8,128)(2,1)S(1)}, u32[]{:S(2)}, u32[]{:S(2)}) collective-permute-start(bf16[128,512]{1,0:T(8,128)(2,1)S(1)} %fusion.79), channel_id=1, source_target_pairs={{0,0},{1,8},{2,16},{3,24},{4,4},{5,12},{6,20},{7,28},{8,1},{9,9},{... | collective-permute-start | bytes 393224 | tf_op jit(solution)/shard_map/ppermute | solution.py:85
  243.4 6.9 %collective-permute-done.75 = bf16[128,512]{1,0:T(8,128)(2,1)S(1)} collective-permute-done((bf16[128,512]{1,0:T(8,128)(2,1)S(1)}, bf16[128,512]{1,0:T(8,128)(2,1)S(1)}, u32[]{:S(2)}, u32[]{:S(2)}) %collective-permute-start.75) | collective-permute-done | bytes 131104 | tf_op jit(solution)/shard_map/ppermute | solution.py:85
  250.6 3.1 %collective-permute-start.82 = (bf16[128,512]{1,0:T(8,128)(2,1)S(1)}, bf16[128,512]{1,0:T(8,128)(2,1)S(1)}, u32[]{:S(2)}, u32[]{:S(2)}) collective-permute-start(bf16[128,512]{1,0:T(8,128)(2,1)S(1)} %fusion.82), channel_id=1, source_target_pairs={{0,24},{4,28},{8,16},{12,20},{16,8},{20,12},{24,0},{28,4},{1,25},{... | collective-permute-start | bytes 393224 | tf_op jit(solution)/shard_map/ppermute | solution.py:91
  253.8 2.2 collective-permute-done.80
  257.5 1.9 collective-permute-done.83
  259.8 5.5 %convolution_convert_fusion = bf16[1792,1024]{1,0:T(8,128)(2,1)} fusion(bf16[256,1792]{1,0:T(8,128)(2,1)S(1)} %get-tuple-element.53, bf16[256,1792]{1,0:T(8,128)(2,1)S(1)} %get-tuple-element.51, bf16[256,1792]{1,0:T(8,128)(2,1)S(1)} %bitcast.355, bf16[256,1792]{1,0:T(8,128)(2,1)S(1)} %bitcast.357, bf16[512,1024]{1,0:T(8,128)(2,1)S(1)} %copy-done.5, ...), kind=kOutput, calls=%fused_computation.2 | convolution fusion | flops 3778805760 | bytes 9437184 | tf_op jit(solution)/shard_map/dot_general | solution.py:50
  (307 shorter events, 89.1 us)
Async XLA Ops:
  0.6 21.2 %collective-permute-start = (bf16[128,512]{1,0:T(8,128)(2,1)}, bf16[128,512]{1,0:T(8,128)(2,1)S(1)}, u32[]{:S(2)}, u32[]{:S(2)}) collective-permute-start(bf16[128,512]{1,0:T(8,128)(2,1)} %param.7), channel_id=1, source_target_pairs={{0,0},{1,8},{2,16},{3,24},{4,4},{5,12},{6,20},{7,28},{8,1},{9,9},{... | collective-permute-start | bytes 393224 | tf_op jit(solution)/shard_map/ppermute | solution.py:85
  5.0 20.4 %collective-permute-start.4 = (bf16[144,512]{1,0:T(8,128)(2,1)S(1)}, bf16[144,512]{1,0:T(8,128)(2,1)S(1)}, u32[]{:S(2)}, u32[]{:S(2)}) collective-permute-start(bf16[144,512]{1,0:T(8,128)(2,1)S(1)} %fusion.92), channel_id=1, source_target_pairs={{0,0},{1,8},{2,16},{3,24},{4,4},{5,12},{6,20},{7,28},{8,1},{9,9},{... | collective-permute-start | bytes 442376 | tf_op jit(solution)/shard_map/ppermute | solution.py:85
  39.4 9.0 %collective-permute-start.22 = (bf16[64,1920]{1,0:T(8,128)(2,1)S(1)}, bf16[64,1920]{1,0:T(8,128)(2,1)S(1)}, u32[]{:S(2)}, u32[]{:S(2)}) collective-permute-start(bf16[64,1920]{1,0:T(8,128)(2,1)S(1)} %dynamic-slice_bitcast_fusion), channel_id=1, source_target_pairs={{0,1},{2,3},{1,0},{3,2},{4,5},{6,7},{5,4},{7,6},{8,9},{10,11},{9,8... | collective-permute-start | bytes 737288 | tf_op jit(solution)/shard_map/ppermute | solution.py:99
  39.4 14.3 %collective-permute-start.7 = (bf16[64,1920]{1,0:T(8,128)(2,1)S(1)}, bf16[64,1920]{1,0:T(8,128)(2,1)S(1)}, u32[]{:S(2)}, u32[]{:S(2)}) collective-permute-start(bf16[64,1920]{1,0:T(8,128)(2,1)S(1)} %dynamic-slice_bitcast_fusion.1), channel_id=1, source_target_pairs={{0,1},{2,3},{1,0},{3,2},{4,5},{6,7},{5,4},{7,6},{8,9},{10,11},{9,8... | collective-permute-start | bytes 737288 | tf_op jit(solution)/shard_map/ppermute | solution.py:99
  45.5 24.6 %collective-permute-start.16 = (bf16[512,512]{1,0:T(8,128)(2,1)S(1)}, bf16[512,512]{1,0:T(8,128)(2,1)S(1)}, u32[]{:S(2)}, u32[]{:S(2)}) collective-permute-start(bf16[512,512]{1,0:T(8,128)(2,1)S(1)} %bitcast.349), channel_id=1, source_target_pairs={{0,4},{4,0},{8,12},{12,8},{16,20},{20,16},{24,28},{28,24},{1,5},{5... | collective-permute-start | bytes 1572872 | tf_op jit(solution)/shard_map/ppermute | solution.py:88
  48.4 10.6 %collective-permute-start.23 = (bf16[64,1920]{1,0:T(8,128)(2,1)S(1)}, bf16[64,1920]{1,0:T(8,128)(2,1)S(1)}, u32[]{:S(2)}, u32[]{:S(2)}) collective-permute-start(bf16[64,1920]{1,0:T(8,128)(2,1)S(1)} %fusion.54), channel_id=1, source_target_pairs={{1,2},{2,1},{5,6},{6,5},{9,10},{10,9},{13,14},{14,13},{17,18},{18,... | collective-permute-start | bytes 737288 | tf_op jit(solution)/shard_map/ppermute | solution.py:99
  49.1 10.0 %collective-permute-start.25 = (bf16[64,1920]{1,0:T(8,128)(2,1)S(1)}, bf16[64,1920]{1,0:T(8,128)(2,1)S(1)}, u32[]{:S(2)}, u32[]{:S(2)}) collective-permute-start(bf16[64,1920]{1,0:T(8,128)(2,1)S(1)} %fusion.91), channel_id=1, source_target_pairs={{0,1},{2,3},{1,0},{3,2},{4,5},{6,7},{5,4},{7,6},{8,9},{10,11},{9,8... | collective-permute-start | bytes 737288 | tf_op jit(solution)/shard_map/ppermute | solution.py:99
  53.9 11.2 %collective-permute-start.8 = (bf16[64,1920]{1,0:T(8,128)(2,1)S(1)}, bf16[64,1920]{1,0:T(8,128)(2,1)S(1)}, u32[]{:S(2)}, u32[]{:S(2)}) collective-permute-start(bf16[64,1920]{1,0:T(8,128)(2,1)S(1)} %fusion.57), channel_id=1, source_target_pairs={{1,2},{2,1},{5,6},{6,5},{9,10},{10,9},{13,14},{14,13},{17,18},{18,... | collective-permute-start | bytes 737288 | tf_op jit(solution)/shard_map/ppermute | solution.py:99
  54.5 10.5 %collective-permute-start.10 = (bf16[64,1920]{1,0:T(8,128)(2,1)S(1)}, bf16[64,1920]{1,0:T(8,128)(2,1)S(1)}, u32[]{:S(2)}, u32[]{:S(2)}) collective-permute-start(bf16[64,1920]{1,0:T(8,128)(2,1)S(1)} %fusion.90), channel_id=1, source_target_pairs={{0,1},{2,3},{1,0},{3,2},{4,5},{6,7},{5,4},{7,6},{8,9},{10,11},{9,8... | collective-permute-start | bytes 737288 | tf_op jit(solution)/shard_map/ppermute | solution.py:99
  59.3 13.5 %collective-permute-start.26 = (bf16[64,1920]{1,0:T(8,128)(2,1)S(1)}, bf16[64,1920]{1,0:T(8,128)(2,1)S(1)}, u32[]{:S(2)}, u32[]{:S(2)}) collective-permute-start(bf16[64,1920]{1,0:T(8,128)(2,1)S(1)} %get-tuple-element.69), channel_id=1, source_target_pairs={{1,2},{2,1},{5,6},{6,5},{9,10},{10,9},{13,14},{14,13},{17,18},{18,... | collective-permute-start | bytes 737288 | tf_op jit(solution)/shard_map/ppermute | solution.py:99
  60.1 12.7 %collective-permute-start.24 = (bf16[64,1920]{1,0:T(8,128)(2,1)S(1)}, bf16[64,1920]{1,0:T(8,128)(2,1)S(1)}, u32[]{:S(2)}, u32[]{:S(2)}) collective-permute-start(bf16[64,1920]{1,0:T(8,128)(2,1)S(1)} %get-tuple-element.68), channel_id=1, source_target_pairs={{0,1},{2,3},{1,0},{3,2},{4,5},{6,7},{5,4},{7,6},{8,9},{10,11},{9,8... | collective-permute-start | bytes 737288 | tf_op jit(solution)/shard_map/ppermute | solution.py:99
  65.2 9.9 %collective-permute-start.11 = (bf16[64,1920]{1,0:T(8,128)(2,1)S(1)}, bf16[64,1920]{1,0:T(8,128)(2,1)S(1)}, u32[]{:S(2)}, u32[]{:S(2)}) collective-permute-start(bf16[64,1920]{1,0:T(8,128)(2,1)S(1)} %get-tuple-element.67), channel_id=1, source_target_pairs={{1,2},{2,1},{5,6},{6,5},{9,10},{10,9},{13,14},{14,13},{17,18},{18,... | collective-permute-start | bytes 737288 | tf_op jit(solution)/shard_map/ppermute | solution.py:99
  65.9 11.0 %collective-permute-start.9 = (bf16[64,1920]{1,0:T(8,128)(2,1)S(1)}, bf16[64,1920]{1,0:T(8,128)(2,1)S(1)}, u32[]{:S(2)}, u32[]{:S(2)}) collective-permute-start(bf16[64,1920]{1,0:T(8,128)(2,1)S(1)} %get-tuple-element.66), channel_id=1, source_target_pairs={{0,1},{2,3},{1,0},{3,2},{4,5},{6,7},{5,4},{7,6},{8,9},{10,11},{9,8... | collective-permute-start | bytes 737288 | tf_op jit(solution)/shard_map/ppermute | solution.py:99
  77.4 11.3 %collective-permute-start.19 = (bf16[64,1792]{1,0:T(8,128)(2,1)S(1)}, bf16[64,1792]{1,0:T(8,128)(2,1)S(1)}, u32[]{:S(2)}, u32[]{:S(2)}) collective-permute-start(bf16[64,1792]{1,0:T(8,128)(2,1)S(1)} %get-tuple-element.41), channel_id=1, source_target_pairs={{0,1},{2,3},{1,0},{3,2},{4,5},{6,7},{5,4},{7,6},{8,9},{10,11},{9,8... | collective-permute-start | bytes 688136 | tf_op jit(solution)/shard_map/ppermute | solution.py:99
  79.7 9.0 %collective-permute-start.12 = (bf16[64,1792]{1,0:T(8,128)(2,1)S(1)}, bf16[64,1792]{1,0:T(8,128)(2,1)S(1)}, u32[]{:S(2)}, u32[]{:S(2)}) collective-permute-start(bf16[64,1792]{1,0:T(8,128)(2,1)S(1)} %get-tuple-element.41), channel_id=1, source_target_pairs={{1,2},{2,1},{5,6},{6,5},{9,10},{10,9},{13,14},{14,13},{17,18},{18,... | collective-permute-start | bytes 688136 | tf_op jit(solution)/shard_map/ppermute | solution.py:99
  82.0 11.6 %collective-permute-start.31 = (bf16[64,1792]{1,0:T(8,128)(2,1)S(1)}, bf16[64,1792]{1,0:T(8,128)(2,1)S(1)}, u32[]{:S(2)}, u32[]{:S(2)}) collective-permute-start(bf16[64,1792]{1,0:T(8,128)(2,1)S(1)} %get-tuple-element.80), channel_id=1, source_target_pairs={{1,2},{2,1},{5,6},{6,5},{9,10},{10,9},{13,14},{14,13},{17,18},{18,... | collective-permute-start | bytes 688136 | tf_op jit(solution)/shard_map/ppermute | solution.py:99
  82.7 11.0 %collective-permute-start.28 = (bf16[64,1792]{1,0:T(8,128)(2,1)S(1)}, bf16[64,1792]{1,0:T(8,128)(2,1)S(1)}, u32[]{:S(2)}, u32[]{:S(2)}) collective-permute-start(bf16[64,1792]{1,0:T(8,128)(2,1)S(1)} %get-tuple-element.81), channel_id=1, source_target_pairs={{0,1},{2,3},{1,0},{3,2},{4,5},{6,7},{5,4},{7,6},{8,9},{10,11},{9,8... | collective-permute-start | bytes 688136 | tf_op jit(solution)/shard_map/ppermute | solution.py:99
  88.9 9.8 %collective-permute-start.20 = (bf16[64,1792]{1,0:T(8,128)(2,1)S(1)}, bf16[64,1792]{1,0:T(8,128)(2,1)S(1)}, u32[]{:S(2)}, u32[]{:S(2)}) collective-permute-start(bf16[64,1792]{1,0:T(8,128)(2,1)S(1)} %get-tuple-element.76), channel_id=1, source_target_pairs={{1,2},{2,1},{5,6},{6,5},{9,10},{10,9},{13,14},{14,13},{17,18},{18,... | collective-permute-start | bytes 688136 | tf_op jit(solution)/shard_map/ppermute | solution.py:99
  89.6 9.5 %collective-permute-start.17 = (bf16[64,1792]{1,0:T(8,128)(2,1)S(1)}, bf16[64,1792]{1,0:T(8,128)(2,1)S(1)}, u32[]{:S(2)}, u32[]{:S(2)}) collective-permute-start(bf16[64,1792]{1,0:T(8,128)(2,1)S(1)} %get-tuple-element.77), channel_id=1, source_target_pairs={{0,1},{2,3},{1,0},{3,2},{4,5},{6,7},{5,4},{7,6},{8,9},{10,11},{9,8... | collective-permute-start | bytes 688136 | tf_op jit(solution)/shard_map/ppermute | solution.py:99
  93.8 10.6 %collective-permute-start.29 = (bf16[64,1792]{1,0:T(8,128)(2,1)S(1)}, bf16[64,1792]{1,0:T(8,128)(2,1)S(1)}, u32[]{:S(2)}, u32[]{:S(2)}) collective-permute-start(bf16[64,1792]{1,0:T(8,128)(2,1)S(1)} %get-tuple-element.79), channel_id=1, source_target_pairs={{1,2},{2,1},{5,6},{6,5},{9,10},{10,9},{13,14},{14,13},{17,18},{18,... | collective-permute-start | bytes 688136 | tf_op jit(solution)/shard_map/ppermute | solution.py:99
  94.5 9.9 %collective-permute-start.32 = (bf16[64,1792]{1,0:T(8,128)(2,1)S(1)}, bf16[64,1792]{1,0:T(8,128)(2,1)S(1)}, u32[]{:S(2)}, u32[]{:S(2)}) collective-permute-start(bf16[64,1792]{1,0:T(8,128)(2,1)S(1)} %get-tuple-element.78), channel_id=1, source_target_pairs={{0,1},{2,3},{1,0},{3,2},{4,5},{6,7},{5,4},{7,6},{8,9},{10,11},{9,8... | collective-permute-start | bytes 688136 | tf_op jit(solution)/shard_map/ppermute | solution.py:99
  110.3 17.1 %collective-permute-start.57 = (bf16[64,1792]{1,0:T(8,128)(2,1)S(1)}, bf16[64,1792]{1,0:T(8,128)(2,1)S(1)}, u32[]{:S(2)}, u32[]{:S(2)}) collective-permute-start(bf16[64,1792]{1,0:T(8,128)(2,1)S(1)} %get-tuple-element.73), channel_id=1, source_target_pairs={{1,2},{2,1},{5,6},{6,5},{9,10},{10,9},{13,14},{14,13},{17,18},{18,... | collective-permute-start | bytes 688136 | tf_op jit(solution)/shard_map/ppermute | solution.py:99
  111.0 16.4 %collective-permute-start.56 = (bf16[64,1792]{1,0:T(8,128)(2,1)S(1)}, bf16[64,1792]{1,0:T(8,128)(2,1)S(1)}, u32[]{:S(2)}, u32[]{:S(2)}) collective-permute-start(bf16[64,1792]{1,0:T(8,128)(2,1)S(1)} %get-tuple-element.72), channel_id=1, source_target_pairs={{0,1},{2,3},{1,0},{3,2},{4,5},{6,7},{5,4},{7,6},{8,9},{10,11},{9,8... | collective-permute-start | bytes 688136 | tf_op jit(solution)/shard_map/ppermute | solution.py:99
  122.7 15.7 %collective-permute-start.42 = (bf16[64,1792]{1,0:T(8,128)(2,1)S(1)}, bf16[64,1792]{1,0:T(8,128)(2,1)S(1)}, u32[]{:S(2)}, u32[]{:S(2)}) collective-permute-start(bf16[64,1792]{1,0:T(8,128)(2,1)S(1)} %get-tuple-element.71), channel_id=1, source_target_pairs={{1,2},{2,1},{5,6},{6,5},{9,10},{10,9},{13,14},{14,13},{17,18},{18,... | collective-permute-start | bytes 688136 | tf_op jit(solution)/shard_map/ppermute | solution.py:99
  124.4 14.0 %collective-permute-start.41 = (bf16[64,1792]{1,0:T(8,128)(2,1)S(1)}, bf16[64,1792]{1,0:T(8,128)(2,1)S(1)}, u32[]{:S(2)}, u32[]{:S(2)}) collective-permute-start(bf16[64,1792]{1,0:T(8,128)(2,1)S(1)} %get-tuple-element.70), channel_id=1, source_target_pairs={{0,1},{2,3},{1,0},{3,2},{4,5},{6,7},{5,4},{7,6},{8,9},{10,11},{9,8... | collective-permute-start | bytes 688136 | tf_op jit(solution)/shard_map/ppermute | solution.py:99
  127.6 15.6 %collective-permute-start.58 = (bf16[64,1920]{1,0:T(8,128)(2,1)S(1)}, bf16[64,1920]{1,0:T(8,128)(2,1)S(1)}, u32[]{:S(2)}, u32[]{:S(2)}) collective-permute-start(bf16[64,1920]{1,0:T(8,128)(2,1)S(1)} %pad.13), channel_id=1, source_target_pairs={{1,2},{2,1},{5,6},{6,5},{9,10},{10,9},{13,14},{14,13},{17,18},{18,... | collective-permute-start | bytes 737288 | tf_op jit(solution)/shard_map/ppermute | solution.py:99
  134.7 9.7 %collective-permute-start.62 = (bf16[64,1920]{1,0:T(8,128)(2,1)S(1)}, bf16[64,1920]{1,0:T(8,128)(2,1)S(1)}, u32[]{:S(2)}, u32[]{:S(2)}) collective-permute-start(bf16[64,1920]{1,0:T(8,128)(2,1)S(1)} %pad.13), channel_id=1, source_target_pairs={{0,1},{2,3},{1,0},{3,2},{4,5},{6,7},{5,4},{7,6},{8,9},{10,11},{9,8... | collective-permute-start | bytes 737288 | tf_op jit(solution)/shard_map/ppermute | solution.py:99
  138.5 9.5 %collective-permute-start.47 = (bf16[64,1920]{1,0:T(8,128)(2,1)S(1)}, bf16[64,1920]{1,0:T(8,128)(2,1)S(1)}, u32[]{:S(2)}, u32[]{:S(2)}) collective-permute-start(bf16[64,1920]{1,0:T(8,128)(2,1)S(1)} %pad.12), channel_id=1, source_target_pairs={{0,1},{2,3},{1,0},{3,2},{4,5},{6,7},{5,4},{7,6},{8,9},{10,11},{9,8... | collective-permute-start | bytes 737288 | tf_op jit(solution)/shard_map/ppermute | solution.py:99
  138.6 9.4 %collective-permute-start.43 = (bf16[64,1920]{1,0:T(8,128)(2,1)S(1)}, bf16[64,1920]{1,0:T(8,128)(2,1)S(1)}, u32[]{:S(2)}, u32[]{:S(2)}) collective-permute-start(bf16[64,1920]{1,0:T(8,128)(2,1)S(1)} %pad.12), channel_id=1, source_target_pairs={{1,2},{2,1},{5,6},{6,5},{9,10},{10,9},{13,14},{14,13},{17,18},{18,... | collective-permute-start | bytes 737288 | tf_op jit(solution)/shard_map/ppermute | solution.py:99
  144.6 9.1 %collective-permute-start.59 = (bf16[64,1920]{1,0:T(8,128)(2,1)S(1)}, bf16[64,1920]{1,0:T(8,128)(2,1)S(1)}, u32[]{:S(2)}, u32[]{:S(2)}) collective-permute-start(bf16[64,1920]{1,0:T(8,128)(2,1)S(1)} %get-tuple-element.64), channel_id=1, source_target_pairs={{0,1},{2,3},{1,0},{3,2},{4,5},{6,7},{5,4},{7,6},{8,9},{10,11},{9,8... | collective-permute-start | bytes 737288 | tf_op jit(solution)/shard_map/ppermute | solution.py:99
  148.2 12.9 %collective-permute-start.48 = (bf16[64,1920]{1,0:T(8,128)(2,1)S(1)}, bf16[64,1920]{1,0:T(8,128)(2,1)S(1)}, u32[]{:S(2)}, u32[]{:S(2)}) collective-permute-start(bf16[64,1920]{1,0:T(8,128)(2,1)S(1)} %get-tuple-element.58), channel_id=1, source_target_pairs={{1,2},{2,1},{5,6},{6,5},{9,10},{10,9},{13,14},{14,13},{17,18},{18,... | collective-permute-start | bytes 737288 | tf_op jit(solution)/shard_map/ppermute | solution.py:99
  148.8 12.2 %collective-permute-start.44 = (bf16[64,1920]{1,0:T(8,128)(2,1)S(1)}, bf16[64,1920]{1,0:T(8,128)(2,1)S(1)}, u32[]{:S(2)}, u32[]{:S(2)}) collective-permute-start(bf16[64,1920]{1,0:T(8,128)(2,1)S(1)} %get-tuple-element.59), channel_id=1, source_target_pairs={{0,1},{2,3},{1,0},{3,2},{4,5},{6,7},{5,4},{7,6},{8,9},{10,11},{9,8... | collective-permute-start | bytes 737288 | tf_op jit(solution)/shard_map/ppermute | solution.py:99
  153.8 12.5 %collective-permute-start.60 = (bf16[64,1920]{1,0:T(8,128)(2,1)S(1)}, bf16[64,1920]{1,0:T(8,128)(2,1)S(1)}, u32[]{:S(2)}, u32[]{:S(2)}) collective-permute-start(bf16[64,1920]{1,0:T(8,128)(2,1)S(1)} %get-tuple-element.62), channel_id=1, source_target_pairs={{1,2},{2,1},{5,6},{6,5},{9,10},{10,9},{13,14},{14,13},{17,18},{18,... | collective-permute-start | bytes 737288 | tf_op jit(solution)/shard_map/ppermute | solution.py:99
  154.5 11.8 %collective-permute-start.64 = (bf16[64,1920]{1,0:T(8,128)(2,1)S(1)}, bf16[64,1920]{1,0:T(8,128)(2,1)S(1)}, u32[]{:S(2)}, u32[]{:S(2)}) collective-permute-start(bf16[64,1920]{1,0:T(8,128)(2,1)S(1)} %get-tuple-element.63), channel_id=1, source_target_pairs={{0,1},{2,3},{1,0},{3,2},{4,5},{6,7},{5,4},{7,6},{8,9},{10,11},{9,8... | collective-permute-start | bytes 737288 | tf_op jit(solution)/shard_map/ppermute | solution.py:99
  161.2 11.6 %collective-permute-start.45 = (bf16[64,1920]{1,0:T(8,128)(2,1)S(1)}, bf16[64,1920]{1,0:T(8,128)(2,1)S(1)}, u32[]{:S(2)}, u32[]{:S(2)}) collective-permute-start(bf16[64,1920]{1,0:T(8,128)(2,1)S(1)} %get-tuple-element.57), channel_id=1, source_target_pairs={{1,2},{2,1},{5,6},{6,5},{9,10},{10,9},{13,14},{14,13},{17,18},{18,... | collective-permute-start | bytes 737288 | tf_op jit(solution)/shard_map/ppermute | solution.py:99
  161.9 10.9 %collective-permute-start.49 = (bf16[64,1920]{1,0:T(8,128)(2,1)S(1)}, bf16[64,1920]{1,0:T(8,128)(2,1)S(1)}, u32[]{:S(2)}, u32[]{:S(2)}) collective-permute-start(bf16[64,1920]{1,0:T(8,128)(2,1)S(1)} %get-tuple-element.56), channel_id=1, source_target_pairs={{0,1},{2,3},{1,0},{3,2},{4,5},{6,7},{5,4},{7,6},{8,9},{10,11},{9,8... | collective-permute-start | bytes 737288 | tf_op jit(solution)/shard_map/ppermute | solution.py:99
  167.3 19.0 %collective-permute-start.65 = (bf16[64,1920]{1,0:T(8,128)(2,1)}, bf16[64,1920]{1,0:T(8,128)(2,1)}, u32[]{:S(2)}, u32[]{:S(2)}) collective-permute-start(bf16[64,1920]{1,0:T(8,128)(2,1)} %get-tuple-element.61), channel_id=1, source_target_pairs={{1,2},{2,1},{5,6},{6,5},{9,10},{10,9},{13,14},{14,13},{17,18},{18,... | collective-permute-start | bytes 737288 | tf_op jit(solution)/shard_map/ppermute | solution.py:99
  168.6 17.6 %collective-permute-start.61 = (bf16[64,1920]{1,0:T(8,128)(2,1)}, bf16[64,1920]{1,0:T(8,128)(2,1)}, u32[]{:S(2)}, u32[]{:S(2)}) collective-permute-start(bf16[64,1920]{1,0:T(8,128)(2,1)} %get-tuple-element.60), channel_id=1, source_target_pairs={{0,1},{2,3},{1,0},{3,2},{4,5},{6,7},{5,4},{7,6},{8,9},{10,11},{9,8... | collective-permute-start | bytes 737288 | tf_op jit(solution)/shard_map/ppermute | solution.py:99
  190.9 9.9 %collective-permute-start.52 = (bf16[64,1920]{1,0:T(8,128)(2,1)}, bf16[64,1920]{1,0:T(8,128)(2,1)S(1)}, u32[]{:S(2)}, u32[]{:S(2)}) collective-permute-start(bf16[64,1920]{1,0:T(8,128)(2,1)} %collective-permute-done.51), channel_id=1, source_target_pairs={{1,2},{2,1},{5,6},{6,5},{9,10},{10,9},{13,14},{14,13},{17,18},{18,... | collective-permute-start | bytes 737288 | tf_op jit(solution)/shard_map/ppermute | solution.py:99
  191.6 11.1 %collective-permute-start.54 = (bf16[64,1920]{1,0:T(8,128)(2,1)}, bf16[64,1920]{1,0:T(8,128)(2,1)S(1)}, u32[]{:S(2)}, u32[]{:S(2)}) collective-permute-start(bf16[64,1920]{1,0:T(8,128)(2,1)} %collective-permute-done.53), channel_id=1, source_target_pairs={{0,1},{2,3},{1,0},{3,2},{4,5},{6,7},{5,4},{7,6},{8,9},{10,11},{9,8... | collective-permute-start | bytes 737288 | tf_op jit(solution)/shard_map/ppermute | solution.py:99
  196.1 10.1 %collective-permute-start.67 = (bf16[64,1920]{1,0:T(8,128)(2,1)S(1)}, bf16[64,1920]{1,0:T(8,128)(2,1)S(1)}, u32[]{:S(2)}, u32[]{:S(2)}) collective-permute-start(bf16[64,1920]{1,0:T(8,128)(2,1)S(1)} %collective-permute-done.66), channel_id=1, source_target_pairs={{1,2},{2,1},{5,6},{6,5},{9,10},{10,9},{13,14},{14,13},{17,18},{18,... | collective-permute-start | bytes 737288 | tf_op jit(solution)/shard_map/ppermute | solution.py:99
  197.1 10.8 %collective-permute-start.69 = (bf16[64,1920]{1,0:T(8,128)(2,1)S(1)}, bf16[64,1920]{1,0:T(8,128)(2,1)S(1)}, u32[]{:S(2)}, u32[]{:S(2)}) collective-permute-start(bf16[64,1920]{1,0:T(8,128)(2,1)S(1)} %collective-permute-done.68), channel_id=1, source_target_pairs={{0,1},{2,3},{1,0},{3,2},{4,5},{6,7},{5,4},{7,6},{8,9},{10,11},{9,8... | collective-permute-start | bytes 737288 | tf_op jit(solution)/shard_map/ppermute | solution.py:99
  202.7 10.5 %collective-permute-start.55 = (bf16[64,1920]{1,0:T(8,128)(2,1)S(1)}, bf16[64,1920]{1,0:T(8,128)(2,1)S(1)}, u32[]{:S(2)}, u32[]{:S(2)}) collective-permute-start(bf16[64,1920]{1,0:T(8,128)(2,1)S(1)} %collective-permute-done.52), channel_id=1, source_target_pairs={{0,1},{2,3},{1,0},{3,2},{4,5},{6,7},{5,4},{7,6},{8,9},{10,11},{9,8... | collective-permute-start | bytes 737288 | tf_op jit(solution)/shard_map/ppermute | solution.py:99
  208.0 10.8 %collective-permute-start.70 = (bf16[64,1920]{1,0:T(8,128)(2,1)S(1)}, bf16[64,1920]{1,0:T(8,128)(2,1)S(1)}, u32[]{:S(2)}, u32[]{:S(2)}) collective-permute-start(bf16[64,1920]{1,0:T(8,128)(2,1)S(1)} %collective-permute-done.67), channel_id=1, source_target_pairs={{0,1},{2,3},{1,0},{3,2},{4,5},{6,7},{5,4},{7,6},{8,9},{10,11},{9,8... | collective-permute-start | bytes 737288 | tf_op jit(solution)/shard_map/ppermute | solution.py:99
  230.2 11.0 %collective-permute-start.79 = (bf16[128,640]{1,0:T(8,128)(2,1)S(1)}, bf16[128,640]{1,0:T(8,128)(2,1)S(1)}, u32[]{:S(2)}, u32[]{:S(2)}) collective-permute-start(bf16[128,640]{1,0:T(8,128)(2,1)S(1)} %bitcast.363), channel_id=1, source_target_pairs={{0,24},{4,28},{8,16},{12,20},{16,8},{20,12},{24,0},{28,4},{1,25},{... | collective-permute-start | bytes 491528 | tf_op jit(solution)/shard_map/ppermute | solution.py:91
  231.9 11.0 %collective-permute-start.78 = (bf16[128,640]{1,0:T(8,128)(2,1)S(1)}, bf16[128,640]{1,0:T(8,128)(2,1)S(1)}, u32[]{:S(2)}, u32[]{:S(2)}) collective-permute-start(bf16[128,640]{1,0:T(8,128)(2,1)S(1)} %bitcast.362), channel_id=1, source_target_pairs={{0,16},{4,20},{8,24},{12,28},{16,0},{20,4},{24,8},{28,12},{1,17},{... | collective-permute-start | bytes 491528 | tf_op jit(solution)/shard_map/ppermute | solution.py:91
  233.6 9.3 %collective-permute-start.77 = (bf16[128,640]{1,0:T(8,128)(2,1)S(1)}, bf16[128,640]{1,0:T(8,128)(2,1)S(1)}, u32[]{:S(2)}, u32[]{:S(2)}) collective-permute-start(bf16[128,640]{1,0:T(8,128)(2,1)S(1)} %bitcast.361), channel_id=1, source_target_pairs={{0,8},{4,12},{8,0},{12,4},{16,24},{20,28},{24,16},{28,20},{1,9},{5... | collective-permute-start | bytes 491528 | tf_op jit(solution)/shard_map/ppermute | solution.py:91
  236.6 13.6 %collective-permute-start.75 = (bf16[128,512]{1,0:T(8,128)(2,1)S(1)}, bf16[128,512]{1,0:T(8,128)(2,1)S(1)}, u32[]{:S(2)}, u32[]{:S(2)}) collective-permute-start(bf16[128,512]{1,0:T(8,128)(2,1)S(1)} %fusion.79), channel_id=1, source_target_pairs={{0,0},{1,8},{2,16},{3,24},{4,4},{5,12},{6,20},{7,28},{8,1},{9,9},{... | collective-permute-start | bytes 393224 | tf_op jit(solution)/shard_map/ppermute | solution.py:85
  (49 other events, 443.1 us)

commit v5 on v4

--- a/solution.py
+++ b/solution.py
@@ -119,11 +119,14 @@
             jnp.concatenate([other, own], axis=1),
         )
 
-    def gather_chips(block):
+    def gather_chips(block, *others):
         mine = jnp.zeros((block.shape[0] * chips, block.shape[1]), block.dtype)
         mine = put(mine, block, chip)
         for shift in range(1, chips):
-            mine = put(mine, chip_swap(block, shift), chip ^ shift)
+            arrived = chip_swap(block, shift)
+            if others:
+                arrived = after(arrived, *others)
+            mine = put(mine, arrived, chip ^ shift)
         return mine
 
     def gather_core(mine):
@@ -294,7 +297,7 @@
     inner = join_pair(total[:, cols:]) / (features * factor)
     back = factor * (total[:, :cols] * gains_home) - x1_home.astype(F32) * (factor**3 * inner)
     grad_home = (g_home.astype(F32) + back).astype(BF16)
-    below = gather_node(after(grad_home, result))
+    below = gather_core(gather_chips(grad_home, result))
     grad_down = dot(
         jnp.concatenate(hiddens + hidden_second, axis=0),
         jnp.concatenate([below, g], axis=0),

time: 270 us -> 267 us (0.989)
  the two profiles are of different devices: /device:TPU:2 before, /device:TPU:21 now
where the time goes in v5:
time: 267 us; the launch traced here: 266 us
  starting transfers between devices  127 us (48%)
  waiting for transfers between devices  85.5 us (32%)
  matrix products  20.1 us (8%)
  other arithmetic  19.7 us (7%)
  Pallas kernels  6.77 us (3%)
  local copies, waits for them, and re-layouts  5.2 us (2%)
    ppermute x52, starting transfers between devices, pair_swap(): return lax.ppermute(block, 'local', pairs + [(t, s) for s, t in pairs])  70.9 us
    ppermute x52, waiting for transfers between devices, pair_swap(): return lax.ppermute(block, 'local', pairs + [(t, s) for s, t in pairs])  52.9 us
    ppermute x21, waiting for transfers between devices, chip_swap(): lax.ppermute(block, 'node', [(n, n ^ 2 * shift) for n in range(n_node)])  30.5 us
    ppermute x21, starting transfers between devices, chip_swap(): lax.ppermute(block, 'node', [(n, n ^ 2 * shift) for n in range(n_node)])  29.4 us
    ppermute x8, starting transfers between devices, core_swap(): return lax.ppermute(block, 'node', [(n, n ^ 1) for n in range(n_node)])  23 us
    dot_general x13, matrix products, dot(): lax.dot_general(left, right, (dims, ((), ())), preferred_element_type=F32)  20.1 us
    pallas_call x1, Pallas kernels, dequant_cols(): pl.pallas_call(scale_columns, grid=(rows // tile,), in_specs=[pl.BlockSpe...  6.77 us
  transfers between devices with their start and end apart: 84, of which 38 were waited for; matrix products, arithmetic and copies ran while one was open for 11% of the time, Pallas kernels for 3%

profile of v5, /device:TPU:21, one launch (start us, length us, event | category | flops | bytes accessed | tf_op | source)
XLA Modules:
  0.0 266.0 jit_solution(11952771490785898438)
XLA Ops:
  5.5 6.8 %shard_map.86 = bf16[1792,1024]{1,0:T(8,128)(2,1)} custom-call(bf16[1792,1024]{1,0:T(8,128)(2,1)} %quanta_ref.1, bf16[1792,8]{1,0:T(8,128)(2,1)} %copy.26.scales_ref), custom_call_target="tpu_custom_call" | custom-call | flops 1835008 | bytes 7340032 | tf_op jit(solution)/shard_map/pallas_call | solution.py:34
  12.3 7.3 %collective-permute-start.1 = (bf16[128,512]{1,0:T(8,128)(2,1)S(1)}, bf16[128,512]{1,0:T(8,128)(2,1)S(1)}, u32[]{:S(2)}, u32[]{:S(2)}) collective-permute-start(bf16[128,512]{1,0:T(8,128)(2,1)S(1)} %collective-permute-done), channel_id=1, source_target_pairs={{0,8},{4,12},{8,0},{12,4},{16,24},{20,28},{24,16},{28,20},{1,9},{5... | collective-permute-start | bytes 393224 | tf_op jit(solution)/shard_map/ppermute | solution.py:91
  22.0 3.1 %collective-permute-done.2 = bf16[128,512]{1,0:T(8,128)(2,1)S(1)} collective-permute-done((bf16[128,512]{1,0:T(8,128)(2,1)S(1)}, bf16[128,512]{1,0:T(8,128)(2,1)S(1)}, u32[]{:S(2)}, u32[]{:S(2)}) %collective-permute-start.2) | collective-permute-done | bytes 131104 | tf_op jit(solution)/shard_map/ppermute | solution.py:91
  25.2 3.6 %collective-permute-start.5 = (bf16[512,512]{1,0:T(8,128)(2,1)S(1)}, bf16[512,512]{1,0:T(8,128)(2,1)S(1)}, u32[]{:S(2)}, u32[]{:S(2)}) collective-permute-start(bf16[512,512]{1,0:T(8,128)(2,1)S(1)} %bitcast.347), channel_id=1, source_target_pairs={{0,4},{4,0},{8,12},{12,8},{16,20},{20,16},{24,28},{28,24},{1,5},{5... | collective-permute-start | bytes 1572872 | tf_op jit(solution)/shard_map/ppermute | solution.py:88
  28.8 2.7 %fusion = bf16[1024,1792]{1,0:T(8,128)(2,1)S(1)} fusion(bf16[1024,1792]{1,0:T(8,128)(2,1)} %param.10, f32[8,1792]{1,0:T(8,128)S(1)} %convert_element_type.736), kind=kLoop, calls=%fused_computation.1 | loop fusion | flops 5505024 | bytes 7397376 | tf_op jit(solution)/shard_map/convert_element_type | solution.py:19
  37.7 2.7 %collective-permute-start.22 = (bf16[64,1920]{1,0:T(8,128)(2,1)S(1)}, bf16[64,1920]{1,0:T(8,128)(2,1)S(1)}, u32[]{:S(2)}, u32[]{:S(2)}) collective-permute-start(bf16[64,1920]{1,0:T(8,128)(2,1)S(1)} %dynamic-slice_bitcast_fusion), channel_id=1, source_target_pairs={{0,1},{2,3},{1,0},{3,2},{4,5},{6,7},{5,4},{7,6},{8,9},{10,11},{9,8... | collective-permute-start | bytes 737288 | tf_op jit(solution)/shard_map/ppermute | solution.py:99
  40.6 2.6 collective-permute-done.15
  48.3 2.7 %collective-permute-done.7 = bf16[64,1920]{1,0:T(8,128)(2,1)S(1)} collective-permute-done((bf16[64,1920]{1,0:T(8,128)(2,1)S(1)}, bf16[64,1920]{1,0:T(8,128)(2,1)S(1)}, u32[]{:S(2)}, u32[]{:S(2)}) %collective-permute-start.7) | collective-permute-done | bytes 245792 | tf_op jit(solution)/shard_map/ppermute | solution.py:99
  53.1 2.7 %collective-permute-done.25 = bf16[64,1920]{1,0:T(8,128)(2,1)S(1)} collective-permute-done((bf16[64,1920]{1,0:T(8,128)(2,1)S(1)}, bf16[64,1920]{1,0:T(8,128)(2,1)S(1)}, u32[]{:S(2)}, u32[]{:S(2)}) %collective-permute-start.25) | collective-permute-done | bytes 245792 | tf_op jit(solution)/shard_map/ppermute | solution.py:99
  56.0 2.2 collective-permute-start.26
  58.9 2.2 collective-permute-done.10
  68.5 2.8 %collective-permute-start.27 = (bf16[64,1792]{1,0:T(8,128)(2,1)S(1)}, bf16[64,1792]{1,0:T(8,128)(2,1)S(1)}, u32[]{:S(2)}, u32[]{:S(2)}) collective-permute-start(bf16[64,1792]{1,0:T(8,128)(2,1)S(1)} %get-tuple-element.47), channel_id=1, source_target_pairs={{1,2},{2,1},{5,6},{6,5},{9,10},{10,9},{13,14},{14,13},{17,18},{18,... | collective-permute-start | bytes 688136 | tf_op jit(solution)/shard_map/ppermute | solution.py:99
  76.1 3.2 %collective-permute-start.31 = (bf16[64,1792]{1,0:T(8,128)(2,1)S(1)}, bf16[64,1792]{1,0:T(8,128)(2,1)S(1)}, u32[]{:S(2)}, u32[]{:S(2)}) collective-permute-start(bf16[64,1792]{1,0:T(8,128)(2,1)S(1)} %get-tuple-element.84), channel_id=1, source_target_pairs={{1,2},{2,1},{5,6},{6,5},{9,10},{10,9},{13,14},{14,13},{17,18},{18,... | collective-permute-start | bytes 688136 | tf_op jit(solution)/shard_map/ppermute | solution.py:99
  82.6 2.2 collective-permute-start.20
  84.8 2.4 collective-permute-done.31
  87.3 2.3 collective-permute-start.29
  89.7 2.0 collective-permute-done.20
  91.9 3.1 %collective-permute-start.18 = (bf16[64,1792]{1,0:T(8,128)(2,1)S(1)}, bf16[64,1792]{1,0:T(8,128)(2,1)S(1)}, u32[]{:S(2)}, u32[]{:S(2)}) collective-permute-start(bf16[64,1792]{1,0:T(8,128)(2,1)S(1)} %get-tuple-element.79), channel_id=1, source_target_pairs={{1,2},{2,1},{5,6},{6,5},{9,10},{10,9},{13,14},{14,13},{17,18},{18,... | collective-permute-start | bytes 688136 | tf_op jit(solution)/shard_map/ppermute | solution.py:99
  97.9 3.2 %collective-permute-done.18 = bf16[64,1792]{1,0:T(8,128)(2,1)S(1)} collective-permute-done((bf16[64,1792]{1,0:T(8,128)(2,1)S(1)}, bf16[64,1792]{1,0:T(8,128)(2,1)S(1)}, u32[]{:S(2)}, u32[]{:S(2)}) %collective-permute-start.18) | collective-permute-done | bytes 229408 | tf_op jit(solution)/shard_map/ppermute | solution.py:99
  102.8 6.8 %collective-permute-start.33 = (bf16[512,512]{1,0:T(8,128)(2,1)S(1)}, bf16[512,512]{1,0:T(8,128)(2,1)S(1)}, u32[]{:S(2)}, u32[]{:S(2)}) collective-permute-start(bf16[512,512]{1,0:T(8,128)(2,1)S(1)} %broadcast_select_fusion.3), channel_id=1, source_target_pairs={{0,4},{4,0},{8,12},{12,8},{16,20},{20,16},{24,28},{28,24},{1,5},{5... | collective-permute-start | bytes 1572872 | tf_op jit(solution)/shard_map/ppermute | solution.py:88
  109.7 2.3 collective-permute-start.57
  112.4 2.7 %collective-permute-start.36 = (bf16[128,512]{1,0:T(8,128)(2,1)S(1)}, bf16[128,512]{1,0:T(8,128)(2,1)S(1)}, u32[]{:S(2)}, u32[]{:S(2)}) collective-permute-start(bf16[128,512]{1,0:T(8,128)(2,1)S(1)} %bitcast.381), channel_id=1, source_target_pairs={{0,24},{4,28},{8,16},{12,20},{16,8},{20,12},{24,0},{28,4},{1,25},{... | collective-permute-start | bytes 393224 | tf_op jit(solution)/shard_map/ppermute | solution.py:91
  116.3 2.4 collective-permute-done.36
  118.7 2.4 collective-permute-start.42
  125.2 2.1 collective-permute-start.58
  131.5 2.1 collective-permute-done.39
  133.6 3.0 %collective-permute-start.40 = (bf16[512,512]{1,0:T(8,128)(2,1)S(1)}, bf16[512,512]{1,0:T(8,128)(2,1)S(1)}, u32[]{:S(2)}, u32[]{:S(2)}) collective-permute-start(bf16[512,512]{1,0:T(8,128)(2,1)S(1)} %bitcast.351), channel_id=1, source_target_pairs={{0,4},{4,0},{8,12},{12,8},{16,20},{20,16},{24,28},{28,24},{1,5},{5... | collective-permute-start | bytes 1572872 | tf_op jit(solution)/shard_map/ppermute | solution.py:88
  138.5 3.2 %collective-permute-start.43 = (bf16[64,1920]{1,0:T(8,128)(2,1)S(1)}, bf16[64,1920]{1,0:T(8,128)(2,1)S(1)}, u32[]{:S(2)}, u32[]{:S(2)}) collective-permute-start(bf16[64,1920]{1,0:T(8,128)(2,1)S(1)} %pad.12), channel_id=1, source_target_pairs={{1,2},{2,1},{5,6},{6,5},{9,10},{10,9},{13,14},{14,13},{17,18},{18,... | collective-permute-start | bytes 737288 | tf_op jit(solution)/shard_map/ppermute | solution.py:99
  145.2 2.1 collective-permute-start.63
  147.8 3.2 %collective-permute-start.48 = (bf16[64,1920]{1,0:T(8,128)(2,1)S(1)}, bf16[64,1920]{1,0:T(8,128)(2,1)S(1)}, u32[]{:S(2)}, u32[]{:S(2)}) collective-permute-start(bf16[64,1920]{1,0:T(8,128)(2,1)S(1)} %get-tuple-element.62), channel_id=1, source_target_pairs={{1,2},{2,1},{5,6},{6,5},{9,10},{10,9},{13,14},{14,13},{17,18},{18,... | collective-permute-start | bytes 737288 | tf_op jit(solution)/shard_map/ppermute | solution.py:99
  156.1 3.1 %collective-permute-done.48 = bf16[64,1920]{1,0:T(8,128)(2,1)S(1)} collective-permute-done((bf16[64,1920]{1,0:T(8,128)(2,1)S(1)}, bf16[64,1920]{1,0:T(8,128)(2,1)S(1)}, u32[]{:S(2)}, u32[]{:S(2)}) %collective-permute-start.48) | collective-permute-done | bytes 245792 | tf_op jit(solution)/shard_map/ppermute | solution.py:99
  161.4 2.7 %collective-permute-done.60 = bf16[64,1920]{1,0:T(8,128)(2,1)S(1)} collective-permute-done((bf16[64,1920]{1,0:T(8,128)(2,1)S(1)}, bf16[64,1920]{1,0:T(8,128)(2,1)S(1)}, u32[]{:S(2)}, u32[]{:S(2)}) %collective-permute-start.60) | collective-permute-done | bytes 245792 | tf_op jit(solution)/shard_map/ppermute | solution.py:99
  167.1 2.3 collective-permute-done.45
  172.4 7.0 %collective-permute-done.50 = bf16[64,1920]{1,0:T(8,128)(2,1)S(1)} collective-permute-done((bf16[64,1920]{1,0:T(8,128)(2,1)S(1)}, bf16[64,1920]{1,0:T(8,128)(2,1)S(1)}, u32[]{:S(2)}, u32[]{:S(2)}) %collective-permute-start.50) | collective-permute-done | bytes 245792 | tf_op jit(solution)/shard_map/ppermute | solution.py:99
  180.1 3.4 %collective-permute-start.53 = (bf16[64,1920]{1,0:T(8,128)(2,1)S(1)}, bf16[64,1920]{1,0:T(8,128)(2,1)}, u32[]{:S(2)}, u32[]{:S(2)}) collective-permute-start(bf16[64,1920]{1,0:T(8,128)(2,1)S(1)} %concatenate.97), channel_id=1, source_target_pairs={{1,2},{2,1},{5,6},{6,5},{9,10},{10,9},{13,14},{14,13},{17,18},{18,... | collective-permute-start | bytes 737288 | tf_op jit(solution)/shard_map/ppermute | solution.py:99
  185.3 2.7 %collective-permute-start.68 = (bf16[64,1920]{1,0:T(8,128)(2,1)S(1)}, bf16[64,1920]{1,0:T(8,128)(2,1)S(1)}, u32[]{:S(2)}, u32[]{:S(2)}) collective-permute-start(bf16[64,1920]{1,0:T(8,128)(2,1)S(1)} %concatenate.99), channel_id=1, source_target_pairs={{1,2},{2,1},{5,6},{6,5},{9,10},{10,9},{13,14},{14,13},{17,18},{18,... | collective-permute-start | bytes 737288 | tf_op jit(solution)/shard_map/ppermute | solution.py:99
  188.0 2.5 collective-permute-start.52
  191.7 3.7 %collective-permute-start.67 = (bf16[64,1920]{1,0:T(8,128)(2,1)S(1)}, bf16[64,1920]{1,0:T(8,128)(2,1)S(1)}, u32[]{:S(2)}, u32[]{:S(2)}) collective-permute-start(bf16[64,1920]{1,0:T(8,128)(2,1)S(1)} %collective-permute-done.66), channel_id=1, source_target_pairs={{1,2},{2,1},{5,6},{6,5},{9,10},{10,9},{13,14},{14,13},{17,18},{18,... | collective-permute-start | bytes 737288 | tf_op jit(solution)/shard_map/ppermute | solution.py:99
  195.5 3.7 %collective-permute-done.52 = bf16[64,1920]{1,0:T(8,128)(2,1)S(1)} collective-permute-done((bf16[64,1920]{1,0:T(8,128)(2,1)}, bf16[64,1920]{1,0:T(8,128)(2,1)S(1)}, u32[]{:S(2)}, u32[]{:S(2)}) %collective-permute-start.52) | collective-permute-done | bytes 245792 | tf_op jit(solution)/shard_map/ppermute | solution.py:99
  199.3 5.1 %collective-permute-done.67 = bf16[64,1920]{1,0:T(8,128)(2,1)S(1)} collective-permute-done((bf16[64,1920]{1,0:T(8,128)(2,1)S(1)}, bf16[64,1920]{1,0:T(8,128)(2,1)S(1)}, u32[]{:S(2)}, u32[]{:S(2)}) %collective-permute-start.67) | collective-permute-done | bytes 245792 | tf_op jit(solution)/shard_map/ppermute | solution.py:99
  204.4 3.7 %collective-permute-done.55 = bf16[64,1920]{1,0:T(8,128)(2,1)S(1)} collective-permute-done((bf16[64,1920]{1,0:T(8,128)(2,1)S(1)}, bf16[64,1920]{1,0:T(8,128)(2,1)S(1)}, u32[]{:S(2)}, u32[]{:S(2)}) %collective-permute-start.55) | collective-permute-done | bytes 245792 | tf_op jit(solution)/shard_map/ppermute | solution.py:99
  215.5 6.3 %collective-permute-start.71 = (bf16[512,512]{1,0:T(8,128)(2,1)S(1)}, bf16[512,512]{1,0:T(8,128)(2,1)S(1)}, u32[]{:S(2)}, u32[]{:S(2)}) collective-permute-start(bf16[512,512]{1,0:T(8,128)(2,1)S(1)} %broadcast_select_fusion.2), channel_id=1, source_target_pairs={{0,4},{4,0},{8,12},{12,8},{16,20},{20,16},{24,28},{28,24},{1,5},{5... | collective-permute-start | bytes 1572872 | tf_op jit(solution)/shard_map/ppermute | solution.py:88
  233.3 3.2 %collective-permute-done.73 = bf16[128,512]{1,0:T(8,128)(2,1)S(1)} collective-permute-done((bf16[128,512]{1,0:T(8,128)(2,1)S(1)}, bf16[128,512]{1,0:T(8,128)(2,1)S(1)}, u32[]{:S(2)}, u32[]{:S(2)}) %collective-permute-start.73) | collective-permute-done | bytes 131104 | tf_op jit(solution)/shard_map/ppermute | solution.py:91
  237.5 2.1 collective-permute-done.79
  239.6 3.7 %collective-permute-done.78 = bf16[128,640]{1,0:T(8,128)(2,1)S(1)} collective-permute-done((bf16[128,640]{1,0:T(8,128)(2,1)S(1)}, bf16[128,640]{1,0:T(8,128)(2,1)S(1)}, u32[]{:S(2)}, u32[]{:S(2)}) %collective-permute-start.78) | collective-permute-done | bytes 163872 | tf_op jit(solution)/shard_map/ppermute | solution.py:91
  243.8 5.4 %collective-permute-start.80 = (bf16[128,512]{1,0:T(8,128)(2,1)S(1)}, bf16[128,512]{1,0:T(8,128)(2,1)S(1)}, u32[]{:S(2)}, u32[]{:S(2)}) collective-permute-start(bf16[128,512]{1,0:T(8,128)(2,1)S(1)} %fusion.82), channel_id=1, source_target_pairs={{0,8},{4,12},{8,0},{12,4},{16,24},{20,28},{24,16},{28,20},{1,9},{5... | collective-permute-start | bytes 393224 | tf_op jit(solution)/shard_map/ppermute | solution.py:91
  252.1 4.3 %collective-permute-done.81 = bf16[128,512]{1,0:T(8,128)(2,1)S(1)} collective-permute-done((bf16[128,512]{1,0:T(8,128)(2,1)S(1)}, bf16[128,512]{1,0:T(8,128)(2,1)S(1)}, u32[]{:S(2)}, u32[]{:S(2)}) %collective-permute-start.81) | collective-permute-done | bytes 131104 | tf_op jit(solution)/shard_map/ppermute | solution.py:91
  259.9 5.5 %convolution_convert_fusion = bf16[1792,1024]{1,0:T(8,128)(2,1)} fusion(bf16[256,1792]{1,0:T(8,128)(2,1)S(1)} %get-tuple-element.57, bf16[256,1792]{1,0:T(8,128)(2,1)S(1)} %get-tuple-element.55, bf16[256,1792]{1,0:T(8,128)(2,1)S(1)} %bitcast.355, bf16[256,1792]{1,0:T(8,128)(2,1)S(1)} %bitcast.357, bf16[512,1024]{1,0:T(8,128)(2,1)S(1)} %copy-done.5, ...), kind=kOutput, calls=%fused_computation.2 | convolution fusion | flops 3778805760 | bytes 9437184 | tf_op jit(solution)/shard_map/dot_general | solution.py:50
  (307 shorter events, 101.5 us)
Async XLA Ops:
  0.6 11.7 %collective-permute-start = (bf16[128,512]{1,0:T(8,128)(2,1)}, bf16[128,512]{1,0:T(8,128)(2,1)S(1)}, u32[]{:S(2)}, u32[]{:S(2)}) collective-permute-start(bf16[128,512]{1,0:T(8,128)(2,1)} %param.7), channel_id=1, source_target_pairs={{0,0},{1,8},{2,16},{3,24},{4,4},{5,12},{6,20},{7,28},{8,1},{9,9},{... | collective-permute-start | bytes 393224 | tf_op jit(solution)/shard_map/ppermute | solution.py:85
  3.1 17.7 %collective-permute-start.4 = (bf16[144,512]{1,0:T(8,128)(2,1)S(1)}, bf16[144,512]{1,0:T(8,128)(2,1)S(1)}, u32[]{:S(2)}, u32[]{:S(2)}) collective-permute-start(bf16[144,512]{1,0:T(8,128)(2,1)S(1)} %fusion.92), channel_id=1, source_target_pairs={{0,0},{1,8},{2,16},{3,24},{4,4},{5,12},{6,20},{7,28},{8,1},{9,9},{... | collective-permute-start | bytes 442376 | tf_op jit(solution)/shard_map/ppermute | solution.py:85
  12.3 9.6 %collective-permute-start.1 = (bf16[128,512]{1,0:T(8,128)(2,1)S(1)}, bf16[128,512]{1,0:T(8,128)(2,1)S(1)}, u32[]{:S(2)}, u32[]{:S(2)}) collective-permute-start(bf16[128,512]{1,0:T(8,128)(2,1)S(1)} %collective-permute-done), channel_id=1, source_target_pairs={{0,8},{4,12},{8,0},{12,4},{16,24},{20,28},{24,16},{28,20},{1,9},{5... | collective-permute-start | bytes 393224 | tf_op jit(solution)/shard_map/ppermute | solution.py:91
  40.4 10.6 %collective-permute-start.7 = (bf16[64,1920]{1,0:T(8,128)(2,1)S(1)}, bf16[64,1920]{1,0:T(8,128)(2,1)S(1)}, u32[]{:S(2)}, u32[]{:S(2)}) collective-permute-start(bf16[64,1920]{1,0:T(8,128)(2,1)S(1)} %dynamic-slice_bitcast_fusion.1), channel_id=1, source_target_pairs={{0,1},{2,3},{1,0},{3,2},{4,5},{6,7},{5,4},{7,6},{8,9},{10,11},{9,8... | collective-permute-start | bytes 737288 | tf_op jit(solution)/shard_map/ppermute | solution.py:99
  43.3 20.3 %collective-permute-start.16 = (bf16[512,512]{1,0:T(8,128)(2,1)S(1)}, bf16[512,512]{1,0:T(8,128)(2,1)S(1)}, u32[]{:S(2)}, u32[]{:S(2)}) collective-permute-start(bf16[512,512]{1,0:T(8,128)(2,1)S(1)} %bitcast.349), channel_id=1, source_target_pairs={{0,4},{4,0},{8,12},{12,8},{16,20},{20,16},{24,28},{28,24},{1,5},{5... | collective-permute-start | bytes 1572872 | tf_op jit(solution)/shard_map/ppermute | solution.py:88
  56.0 10.4 %collective-permute-start.26 = (bf16[64,1920]{1,0:T(8,128)(2,1)S(1)}, bf16[64,1920]{1,0:T(8,128)(2,1)S(1)}, u32[]{:S(2)}, u32[]{:S(2)}) collective-permute-start(bf16[64,1920]{1,0:T(8,128)(2,1)S(1)} %get-tuple-element.73), channel_id=1, source_target_pairs={{1,2},{2,1},{5,6},{6,5},{9,10},{10,9},{13,14},{14,13},{17,18},{18,... | collective-permute-start | bytes 737288 | tf_op jit(solution)/shard_map/ppermute | solution.py:99
  61.2 10.1 %collective-permute-start.11 = (bf16[64,1920]{1,0:T(8,128)(2,1)S(1)}, bf16[64,1920]{1,0:T(8,128)(2,1)S(1)}, u32[]{:S(2)}, u32[]{:S(2)}) collective-permute-start(bf16[64,1920]{1,0:T(8,128)(2,1)S(1)} %get-tuple-element.71), channel_id=1, source_target_pairs={{1,2},{2,1},{5,6},{6,5},{9,10},{10,9},{13,14},{14,13},{17,18},{18,... | collective-permute-start | bytes 737288 | tf_op jit(solution)/shard_map/ppermute | solution.py:99
  63.2 8.2 %collective-permute-start.9 = (bf16[64,1920]{1,0:T(8,128)(2,1)S(1)}, bf16[64,1920]{1,0:T(8,128)(2,1)S(1)}, u32[]{:S(2)}, u32[]{:S(2)}) collective-permute-start(bf16[64,1920]{1,0:T(8,128)(2,1)S(1)} %get-tuple-element.70), channel_id=1, source_target_pairs={{0,1},{2,3},{1,0},{3,2},{4,5},{6,7},{5,4},{7,6},{8,9},{10,11},{9,8... | collective-permute-start | bytes 737288 | tf_op jit(solution)/shard_map/ppermute | solution.py:99
  66.8 9.1 %collective-permute-start.30 = (bf16[64,1792]{1,0:T(8,128)(2,1)S(1)}, bf16[64,1792]{1,0:T(8,128)(2,1)S(1)}, u32[]{:S(2)}, u32[]{:S(2)}) collective-permute-start(bf16[64,1792]{1,0:T(8,128)(2,1)S(1)} %get-tuple-element.47), channel_id=1, source_target_pairs={{0,1},{2,3},{1,0},{3,2},{4,5},{6,7},{5,4},{7,6},{8,9},{10,11},{9,8... | collective-permute-start | bytes 688136 | tf_op jit(solution)/shard_map/ppermute | solution.py:99
  71.9 9.0 %collective-permute-start.19 = (bf16[64,1792]{1,0:T(8,128)(2,1)S(1)}, bf16[64,1792]{1,0:T(8,128)(2,1)S(1)}, u32[]{:S(2)}, u32[]{:S(2)}) collective-permute-start(bf16[64,1792]{1,0:T(8,128)(2,1)S(1)} %get-tuple-element.45), channel_id=1, source_target_pairs={{0,1},{2,3},{1,0},{3,2},{4,5},{6,7},{5,4},{7,6},{8,9},{10,11},{9,8... | collective-permute-start | bytes 688136 | tf_op jit(solution)/shard_map/ppermute | solution.py:99
  73.8 8.6 %collective-permute-start.12 = (bf16[64,1792]{1,0:T(8,128)(2,1)S(1)}, bf16[64,1792]{1,0:T(8,128)(2,1)S(1)}, u32[]{:S(2)}, u32[]{:S(2)}) collective-permute-start(bf16[64,1792]{1,0:T(8,128)(2,1)S(1)} %get-tuple-element.45), channel_id=1, source_target_pairs={{1,2},{2,1},{5,6},{6,5},{9,10},{10,9},{13,14},{14,13},{17,18},{18,... | collective-permute-start | bytes 688136 | tf_op jit(solution)/shard_map/ppermute | solution.py:99
  76.1 11.1 %collective-permute-start.31 = (bf16[64,1792]{1,0:T(8,128)(2,1)S(1)}, bf16[64,1792]{1,0:T(8,128)(2,1)S(1)}, u32[]{:S(2)}, u32[]{:S(2)}) collective-permute-start(bf16[64,1792]{1,0:T(8,128)(2,1)S(1)} %get-tuple-element.84), channel_id=1, source_target_pairs={{1,2},{2,1},{5,6},{6,5},{9,10},{10,9},{13,14},{14,13},{17,18},{18,... | collective-permute-start | bytes 688136 | tf_op jit(solution)/shard_map/ppermute | solution.py:99
  82.6 9.2 %collective-permute-start.20 = (bf16[64,1792]{1,0:T(8,128)(2,1)S(1)}, bf16[64,1792]{1,0:T(8,128)(2,1)S(1)}, u32[]{:S(2)}, u32[]{:S(2)}) collective-permute-start(bf16[64,1792]{1,0:T(8,128)(2,1)S(1)} %get-tuple-element.80), channel_id=1, source_target_pairs={{1,2},{2,1},{5,6},{6,5},{9,10},{10,9},{13,14},{14,13},{17,18},{18,... | collective-permute-start | bytes 688136 | tf_op jit(solution)/shard_map/ppermute | solution.py:99
  87.3 9.0 %collective-permute-start.29 = (bf16[64,1792]{1,0:T(8,128)(2,1)S(1)}, bf16[64,1792]{1,0:T(8,128)(2,1)S(1)}, u32[]{:S(2)}, u32[]{:S(2)}) collective-permute-start(bf16[64,1792]{1,0:T(8,128)(2,1)S(1)} %get-tuple-element.83), channel_id=1, source_target_pairs={{1,2},{2,1},{5,6},{6,5},{9,10},{10,9},{13,14},{14,13},{17,18},{18,... | collective-permute-start | bytes 688136 | tf_op jit(solution)/shard_map/ppermute | solution.py:99
  91.9 9.2 %collective-permute-start.18 = (bf16[64,1792]{1,0:T(8,128)(2,1)S(1)}, bf16[64,1792]{1,0:T(8,128)(2,1)S(1)}, u32[]{:S(2)}, u32[]{:S(2)}) collective-permute-start(bf16[64,1792]{1,0:T(8,128)(2,1)S(1)} %get-tuple-element.79), channel_id=1, source_target_pairs={{1,2},{2,1},{5,6},{6,5},{9,10},{10,9},{13,14},{14,13},{17,18},{18,... | collective-permute-start | bytes 688136 | tf_op jit(solution)/shard_map/ppermute | solution.py:99
  102.8 9.4 %collective-permute-start.33 = (bf16[512,512]{1,0:T(8,128)(2,1)S(1)}, bf16[512,512]{1,0:T(8,128)(2,1)S(1)}, u32[]{:S(2)}, u32[]{:S(2)}) collective-permute-start(bf16[512,512]{1,0:T(8,128)(2,1)S(1)} %broadcast_select_fusion.3), channel_id=1, source_target_pairs={{0,4},{4,0},{8,12},{12,8},{16,20},{20,16},{24,28},{28,24},{1,5},{5... | collective-permute-start | bytes 1572872 | tf_op jit(solution)/shard_map/ppermute | solution.py:88
  109.7 15.3 %collective-permute-start.57 = (bf16[64,1792]{1,0:T(8,128)(2,1)S(1)}, bf16[64,1792]{1,0:T(8,128)(2,1)S(1)}, u32[]{:S(2)}, u32[]{:S(2)}) collective-permute-start(bf16[64,1792]{1,0:T(8,128)(2,1)S(1)} %get-tuple-element.77), channel_id=1, source_target_pairs={{1,2},{2,1},{5,6},{6,5},{9,10},{10,9},{13,14},{14,13},{17,18},{18,... | collective-permute-start | bytes 688136 | tf_op jit(solution)/shard_map/ppermute | solution.py:99
  112.1 13.0 %collective-permute-start.56 = (bf16[64,1792]{1,0:T(8,128)(2,1)S(1)}, bf16[64,1792]{1,0:T(8,128)(2,1)S(1)}, u32[]{:S(2)}, u32[]{:S(2)}) collective-permute-start(bf16[64,1792]{1,0:T(8,128)(2,1)S(1)} %get-tuple-element.76), channel_id=1, source_target_pairs={{0,1},{2,3},{1,0},{3,2},{4,5},{6,7},{5,4},{7,6},{8,9},{10,11},{9,8... | collective-permute-start | bytes 688136 | tf_op jit(solution)/shard_map/ppermute | solution.py:99
  118.7 17.9 %collective-permute-start.42 = (bf16[64,1792]{1,0:T(8,128)(2,1)S(1)}, bf16[64,1792]{1,0:T(8,128)(2,1)S(1)}, u32[]{:S(2)}, u32[]{:S(2)}) collective-permute-start(bf16[64,1792]{1,0:T(8,128)(2,1)S(1)} %get-tuple-element.75), channel_id=1, source_target_pairs={{1,2},{2,1},{5,6},{6,5},{9,10},{10,9},{13,14},{14,13},{17,18},{18,... | collective-permute-start | bytes 688136 | tf_op jit(solution)/shard_map/ppermute | solution.py:99
  121.9 14.7 %collective-permute-start.41 = (bf16[64,1792]{1,0:T(8,128)(2,1)S(1)}, bf16[64,1792]{1,0:T(8,128)(2,1)S(1)}, u32[]{:S(2)}, u32[]{:S(2)}) collective-permute-start(bf16[64,1792]{1,0:T(8,128)(2,1)S(1)} %get-tuple-element.74), channel_id=1, source_target_pairs={{0,1},{2,3},{1,0},{3,2},{4,5},{6,7},{5,4},{7,6},{8,9},{10,11},{9,8... | collective-permute-start | bytes 688136 | tf_op jit(solution)/shard_map/ppermute | solution.py:99
  125.2 19.7 %collective-permute-start.58 = (bf16[64,1920]{1,0:T(8,128)(2,1)S(1)}, bf16[64,1920]{1,0:T(8,128)(2,1)S(1)}, u32[]{:S(2)}, u32[]{:S(2)}) collective-permute-start(bf16[64,1920]{1,0:T(8,128)(2,1)S(1)} %pad.13), channel_id=1, source_target_pairs={{1,2},{2,1},{5,6},{6,5},{9,10},{10,9},{13,14},{14,13},{17,18},{18,... | collective-permute-start | bytes 737288 | tf_op jit(solution)/shard_map/ppermute | solution.py:99
  131.5 13.4 %collective-permute-start.62 = (bf16[64,1920]{1,0:T(8,128)(2,1)S(1)}, bf16[64,1920]{1,0:T(8,128)(2,1)S(1)}, u32[]{:S(2)}, u32[]{:S(2)}) collective-permute-start(bf16[64,1920]{1,0:T(8,128)(2,1)S(1)} %pad.13), channel_id=1, source_target_pairs={{0,1},{2,3},{1,0},{3,2},{4,5},{6,7},{5,4},{7,6},{8,9},{10,11},{9,8... | collective-permute-start | bytes 737288 | tf_op jit(solution)/shard_map/ppermute | solution.py:99
  133.6 8.4 %collective-permute-start.40 = (bf16[512,512]{1,0:T(8,128)(2,1)S(1)}, bf16[512,512]{1,0:T(8,128)(2,1)S(1)}, u32[]{:S(2)}, u32[]{:S(2)}) collective-permute-start(bf16[512,512]{1,0:T(8,128)(2,1)S(1)} %bitcast.351), channel_id=1, source_target_pairs={{0,4},{4,0},{8,12},{12,8},{16,20},{20,16},{24,28},{28,24},{1,5},{5... | collective-permute-start | bytes 1572872 | tf_op jit(solution)/shard_map/ppermute | solution.py:88
  136.7 10.7 %collective-permute-start.47 = (bf16[64,1920]{1,0:T(8,128)(2,1)S(1)}, bf16[64,1920]{1,0:T(8,128)(2,1)S(1)}, u32[]{:S(2)}, u32[]{:S(2)}) collective-permute-start(bf16[64,1920]{1,0:T(8,128)(2,1)S(1)} %pad.12), channel_id=1, source_target_pairs={{0,1},{2,3},{1,0},{3,2},{4,5},{6,7},{5,4},{7,6},{8,9},{10,11},{9,8... | collective-permute-start | bytes 737288 | tf_op jit(solution)/shard_map/ppermute | solution.py:99
  138.5 9.1 %collective-permute-start.43 = (bf16[64,1920]{1,0:T(8,128)(2,1)S(1)}, bf16[64,1920]{1,0:T(8,128)(2,1)S(1)}, u32[]{:S(2)}, u32[]{:S(2)}) collective-permute-start(bf16[64,1920]{1,0:T(8,128)(2,1)S(1)} %pad.12), channel_id=1, source_target_pairs={{1,2},{2,1},{5,6},{6,5},{9,10},{10,9},{13,14},{14,13},{17,18},{18,... | collective-permute-start | bytes 737288 | tf_op jit(solution)/shard_map/ppermute | solution.py:99
  145.2 8.8 %collective-permute-start.63 = (bf16[64,1920]{1,0:T(8,128)(2,1)S(1)}, bf16[64,1920]{1,0:T(8,128)(2,1)S(1)}, u32[]{:S(2)}, u32[]{:S(2)}) collective-permute-start(bf16[64,1920]{1,0:T(8,128)(2,1)S(1)} %get-tuple-element.69), channel_id=1, source_target_pairs={{1,2},{2,1},{5,6},{6,5},{9,10},{10,9},{13,14},{14,13},{17,18},{18,... | collective-permute-start | bytes 737288 | tf_op jit(solution)/shard_map/ppermute | solution.py:99
  147.8 11.4 %collective-permute-start.48 = (bf16[64,1920]{1,0:T(8,128)(2,1)S(1)}, bf16[64,1920]{1,0:T(8,128)(2,1)S(1)}, u32[]{:S(2)}, u32[]{:S(2)}) collective-permute-start(bf16[64,1920]{1,0:T(8,128)(2,1)S(1)} %get-tuple-element.62), channel_id=1, source_target_pairs={{1,2},{2,1},{5,6},{6,5},{9,10},{10,9},{13,14},{14,13},{17,18},{18,... | collective-permute-start | bytes 737288 | tf_op jit(solution)/shard_map/ppermute | solution.py:99
  151.0 8.2 %collective-permute-start.44 = (bf16[64,1920]{1,0:T(8,128)(2,1)S(1)}, bf16[64,1920]{1,0:T(8,128)(2,1)S(1)}, u32[]{:S(2)}, u32[]{:S(2)}) collective-permute-start(bf16[64,1920]{1,0:T(8,128)(2,1)S(1)} %get-tuple-element.63), channel_id=1, source_target_pairs={{0,1},{2,3},{1,0},{3,2},{4,5},{6,7},{5,4},{7,6},{8,9},{10,11},{9,8... | collective-permute-start | bytes 737288 | tf_op jit(solution)/shard_map/ppermute | solution.py:99
  154.1 10.0 %collective-permute-start.60 = (bf16[64,1920]{1,0:T(8,128)(2,1)S(1)}, bf16[64,1920]{1,0:T(8,128)(2,1)S(1)}, u32[]{:S(2)}, u32[]{:S(2)}) collective-permute-start(bf16[64,1920]{1,0:T(8,128)(2,1)S(1)} %get-tuple-element.66), channel_id=1, source_target_pairs={{1,2},{2,1},{5,6},{6,5},{9,10},{10,9},{13,14},{14,13},{17,18},{18,... | collective-permute-start | bytes 737288 | tf_op jit(solution)/shard_map/ppermute | solution.py:99
  159.4 10.0 %collective-permute-start.45 = (bf16[64,1920]{1,0:T(8,128)(2,1)S(1)}, bf16[64,1920]{1,0:T(8,128)(2,1)S(1)}, u32[]{:S(2)}, u32[]{:S(2)}) collective-permute-start(bf16[64,1920]{1,0:T(8,128)(2,1)S(1)} %get-tuple-element.61), channel_id=1, source_target_pairs={{1,2},{2,1},{5,6},{6,5},{9,10},{10,9},{13,14},{14,13},{17,18},{18,... | collective-permute-start | bytes 737288 | tf_op jit(solution)/shard_map/ppermute | solution.py:99
  165.1 18.4 %collective-permute-start.65 = (bf16[64,1920]{1,0:T(8,128)(2,1)}, bf16[64,1920]{1,0:T(8,128)(2,1)}, u32[]{:S(2)}, u32[]{:S(2)}) collective-permute-start(bf16[64,1920]{1,0:T(8,128)(2,1)} %get-tuple-element.65), channel_id=1, source_target_pairs={{1,2},{2,1},{5,6},{6,5},{9,10},{10,9},{13,14},{14,13},{17,18},{18,... | collective-permute-start | bytes 737288 | tf_op jit(solution)/shard_map/ppermute | solution.py:99
  167.0 16.5 %collective-permute-start.61 = (bf16[64,1920]{1,0:T(8,128)(2,1)}, bf16[64,1920]{1,0:T(8,128)(2,1)}, u32[]{:S(2)}, u32[]{:S(2)}) collective-permute-start(bf16[64,1920]{1,0:T(8,128)(2,1)} %get-tuple-element.64), channel_id=1, source_target_pairs={{0,1},{2,3},{1,0},{3,2},{4,5},{6,7},{5,4},{7,6},{8,9},{10,11},{9,8... | collective-permute-start | bytes 737288 | tf_op jit(solution)/shard_map/ppermute | solution.py:99
  169.5 9.9 %collective-permute-start.50 = (bf16[64,1920]{1,0:T(8,128)(2,1)S(1)}, bf16[64,1920]{1,0:T(8,128)(2,1)S(1)}, u32[]{:S(2)}, u32[]{:S(2)}) collective-permute-start(bf16[64,1920]{1,0:T(8,128)(2,1)S(1)} %get-tuple-element.59), channel_id=1, source_target_pairs={{1,2},{2,1},{5,6},{6,5},{9,10},{10,9},{13,14},{14,13},{17,18},{18,... | collective-permute-start | bytes 737288 | tf_op jit(solution)/shard_map/ppermute | solution.py:99
  180.1 10.4 %collective-permute-start.53 = (bf16[64,1920]{1,0:T(8,128)(2,1)S(1)}, bf16[64,1920]{1,0:T(8,128)(2,1)}, u32[]{:S(2)}, u32[]{:S(2)}) collective-permute-start(bf16[64,1920]{1,0:T(8,128)(2,1)S(1)} %concatenate.97), channel_id=1, source_target_pairs={{1,2},{2,1},{5,6},{6,5},{9,10},{10,9},{13,14},{14,13},{17,18},{18,... | collective-permute-start | bytes 737288 | tf_op jit(solution)/shard_map/ppermute | solution.py:99
  185.3 10.1 %collective-permute-start.68 = (bf16[64,1920]{1,0:T(8,128)(2,1)S(1)}, bf16[64,1920]{1,0:T(8,128)(2,1)S(1)}, u32[]{:S(2)}, u32[]{:S(2)}) collective-permute-start(bf16[64,1920]{1,0:T(8,128)(2,1)S(1)} %concatenate.99), channel_id=1, source_target_pairs={{1,2},{2,1},{5,6},{6,5},{9,10},{10,9},{13,14},{14,13},{17,18},{18,... | collective-permute-start | bytes 737288 | tf_op jit(solution)/shard_map/ppermute | solution.py:99
  188.0 11.1 %collective-permute-start.52 = (bf16[64,1920]{1,0:T(8,128)(2,1)}, bf16[64,1920]{1,0:T(8,128)(2,1)S(1)}, u32[]{:S(2)}, u32[]{:S(2)}) collective-permute-start(bf16[64,1920]{1,0:T(8,128)(2,1)} %collective-permute-done.51), channel_id=1, source_target_pairs={{1,2},{2,1},{5,6},{6,5},{9,10},{10,9},{13,14},{14,13},{17,18},{18,... | collective-permute-start | bytes 737288 | tf_op jit(solution)/shard_map/ppermute | solution.py:99
  190.6 8.6 %collective-permute-start.54 = (bf16[64,1920]{1,0:T(8,128)(2,1)}, bf16[64,1920]{1,0:T(8,128)(2,1)S(1)}, u32[]{:S(2)}, u32[]{:S(2)}) collective-permute-start(bf16[64,1920]{1,0:T(8,128)(2,1)} %collective-permute-done.53), channel_id=1, source_target_pairs={{0,1},{2,3},{1,0},{3,2},{4,5},{6,7},{5,4},{7,6},{8,9},{10,11},{9,8... | collective-permute-start | bytes 737288 | tf_op jit(solution)/shard_map/ppermute | solution.py:99
  191.7 12.7 %collective-permute-start.67 = (bf16[64,1920]{1,0:T(8,128)(2,1)S(1)}, bf16[64,1920]{1,0:T(8,128)(2,1)S(1)}, u32[]{:S(2)}, u32[]{:S(2)}) collective-permute-start(bf16[64,1920]{1,0:T(8,128)(2,1)S(1)} %collective-permute-done.66), channel_id=1, source_target_pairs={{1,2},{2,1},{5,6},{6,5},{9,10},{10,9},{13,14},{14,13},{17,18},{18,... | collective-permute-start | bytes 737288 | tf_op jit(solution)/shard_map/ppermute | solution.py:99
  195.4 9.0 %collective-permute-start.69 = (bf16[64,1920]{1,0:T(8,128)(2,1)S(1)}, bf16[64,1920]{1,0:T(8,128)(2,1)S(1)}, u32[]{:S(2)}, u32[]{:S(2)}) collective-permute-start(bf16[64,1920]{1,0:T(8,128)(2,1)S(1)} %collective-permute-done.68), channel_id=1, source_target_pairs={{0,1},{2,3},{1,0},{3,2},{4,5},{6,7},{5,4},{7,6},{8,9},{10,11},{9,8... | collective-permute-start | bytes 737288 | tf_op jit(solution)/shard_map/ppermute | solution.py:99
  199.2 9.0 %collective-permute-start.55 = (bf16[64,1920]{1,0:T(8,128)(2,1)S(1)}, bf16[64,1920]{1,0:T(8,128)(2,1)S(1)}, u32[]{:S(2)}, u32[]{:S(2)}) collective-permute-start(bf16[64,1920]{1,0:T(8,128)(2,1)S(1)} %collective-permute-done.52), channel_id=1, source_target_pairs={{0,1},{2,3},{1,0},{3,2},{4,5},{6,7},{5,4},{7,6},{8,9},{10,11},{9,8... | collective-permute-start | bytes 737288 | tf_op jit(solution)/shard_map/ppermute | solution.py:99
  204.4 9.3 %collective-permute-start.70 = (bf16[64,1920]{1,0:T(8,128)(2,1)S(1)}, bf16[64,1920]{1,0:T(8,128)(2,1)S(1)}, u32[]{:S(2)}, u32[]{:S(2)}) collective-permute-start(bf16[64,1920]{1,0:T(8,128)(2,1)S(1)} %collective-permute-done.67), channel_id=1, source_target_pairs={{0,1},{2,3},{1,0},{3,2},{4,5},{6,7},{5,4},{7,6},{8,9},{10,11},{9,8... | collective-permute-start | bytes 737288 | tf_op jit(solution)/shard_map/ppermute | solution.py:99
  228.1 8.3 %collective-permute-start.73 = (bf16[128,512]{1,0:T(8,128)(2,1)S(1)}, bf16[128,512]{1,0:T(8,128)(2,1)S(1)}, u32[]{:S(2)}, u32[]{:S(2)}) collective-permute-start(bf16[128,512]{1,0:T(8,128)(2,1)S(1)} %bitcast.377), channel_id=1, source_target_pairs={{0,16},{4,20},{8,24},{12,28},{16,0},{20,4},{24,8},{28,12},{1,17},{... | collective-permute-start | bytes 393224 | tf_op jit(solution)/shard_map/ppermute | solution.py:91
  228.2 8.3 %collective-permute-start.72 = (bf16[128,512]{1,0:T(8,128)(2,1)S(1)}, bf16[128,512]{1,0:T(8,128)(2,1)S(1)}, u32[]{:S(2)}, u32[]{:S(2)}) collective-permute-start(bf16[128,512]{1,0:T(8,128)(2,1)S(1)} %bitcast.376), channel_id=1, source_target_pairs={{0,8},{4,12},{8,0},{12,4},{16,24},{20,28},{24,16},{28,20},{1,9},{5... | collective-permute-start | bytes 393224 | tf_op jit(solution)/shard_map/ppermute | solution.py:91
  230.3 9.3 %collective-permute-start.79 = (bf16[128,640]{1,0:T(8,128)(2,1)S(1)}, bf16[128,640]{1,0:T(8,128)(2,1)S(1)}, u32[]{:S(2)}, u32[]{:S(2)}) collective-permute-start(bf16[128,640]{1,0:T(8,128)(2,1)S(1)} %bitcast.363), channel_id=1, source_target_pairs={{0,24},{4,28},{8,16},{12,20},{16,8},{20,12},{24,0},{28,4},{1,25},{... | collective-permute-start | bytes 491528 | tf_op jit(solution)/shard_map/ppermute | solution.py:91
  231.2 12.1 %collective-permute-start.78 = (bf16[128,640]{1,0:T(8,128)(2,1)S(1)}, bf16[128,640]{1,0:T(8,128)(2,1)S(1)}, u32[]{:S(2)}, u32[]{:S(2)}) collective-permute-start(bf16[128,640]{1,0:T(8,128)(2,1)S(1)} %bitcast.362), channel_id=1, source_target_pairs={{0,16},{4,20},{8,24},{12,28},{16,0},{20,4},{24,8},{28,12},{1,17},{... | collective-permute-start | bytes 491528 | tf_op jit(solution)/shard_map/ppermute | solution.py:91
  233.3 10.0 %collective-permute-start.77 = (bf16[128,640]{1,0:T(8,128)(2,1)S(1)}, bf16[128,640]{1,0:T(8,128)(2,1)S(1)}, u32[]{:S(2)}, u32[]{:S(2)}) collective-permute-start(bf16[128,640]{1,0:T(8,128)(2,1)S(1)} %bitcast.361), channel_id=1, source_target_pairs={{0,8},{4,12},{8,0},{12,4},{16,24},{20,28},{24,16},{28,20},{1,9},{5... | collective-permute-start | bytes 491528 | tf_op jit(solution)/shard_map/ppermute | solution.py:91
  236.5 13.9 %collective-permute-start.75 = (bf16[128,512]{1,0:T(8,128)(2,1)S(1)}, bf16[128,512]{1,0:T(8,128)(2,1)S(1)}, u32[]{:S(2)}, u32[]{:S(2)}) collective-permute-start(bf16[128,512]{1,0:T(8,128)(2,1)S(1)} %fusion.79), channel_id=1, source_target_pairs={{0,0},{1,8},{2,16},{3,24},{4,4},{5,12},{6,20},{7,28},{8,1},{9,9},{... | collective-permute-start | bytes 393224 | tf_op jit(solution)/shard_map/ppermute | solution.py:85
  243.8 8.3 %collective-permute-start.80 = (bf16[128,512]{1,0:T(8,128)(2,1)S(1)}, bf16[128,512]{1,0:T(8,128)(2,1)S(1)}, u32[]{:S(2)}, u32[]{:S(2)}) collective-permute-start(bf16[128,512]{1,0:T(8,128)(2,1)S(1)} %fusion.82), channel_id=1, source_target_pairs={{0,8},{4,12},{8,0},{12,4},{16,24},{20,28},{24,16},{28,20},{1,9},{5... | collective-permute-start | bytes 393224 | tf_op jit(solution)/shard_map/ppermute | solution.py:91
  (49 other events, 458.9 us)
